TPU v7x, 128 devices: a whole 4x4x4 slice. The times are simulated.
128 devices in a mesh: wide: 32 (over z, x, core), rhs: 4 (over y).
Axes of the slice: x: 4, y: 4, z: 4, core: 2. Of those that a mesh axis runs over, the one named last changes fastest.
Arguments:
- child_rhs: float32 [1024, 18432], P('rhs', 'wide'), may hold values from -6 to 6
- parent_rhs: float32 [1024, 12288], P('rhs', 'wide'), may hold values from -6 to 6
- child_inverse: bfloat16 [18432, 9216], P('wide'), as said below
- coupling: bfloat16 [18432, 3072], P('wide'), may hold values from -0.0625 to 0.0625
- parent_inverse: bfloat16 [12288, 12288], P('wide'), as said below
- child_blocks: int32 [2], replicated, may hold values from 36 to 72, as said below
- parent_block: int32 [2, 24], replicated, may hold values from 0 to 95, as said below
Outputs:
- child_solution: float32 [1024, 18432], P('rhs', 'wide')
- parent_solution: float32 [1024, 12288], P('rhs', 'wide')
Inputs may be any that keep to these rules, and one draw needn't show every extreme that they name: `child_blocks`: one child has exactly 72 blocks, the other at least half of that. `parent_block`: the 24 entries of a row are distinct. `child_inverse`: lower triangular with unit diagonal. `parent_inverse`: lower triangular with unit diagonal.
All inputs are finite; a program needn't handle non-finite values.
Results may differ from a plain program's by a relative error of at most 0.0038.
Values may be sent and summed in bfloat16 or wider, within the bound.
No kernel may reach another device: no remote copies, remote signals or barrier semaphores. Data moves between devices by JAX's collectives and lax.ppermute only.
A program may use at most 192 MiB of HBM per device.

v0:
```python
import jax
import jax.numpy as jnp
from jax import lax
from jax.sharding import PartitionSpec as P

S0 = 12288
BLK = 128


def from_partner(value, axis, bit):
    mask = 2**bit
    pairs = [(source, source ^ mask) for source in range(lax.axis_size(axis))]
    return lax.ppermute(value, axis, pairs)


def on_device(
    child_rhs, parent_rhs, child_inverse, coupling, parent_inverse, child_blocks, parent_block
):
    half_size = lax.axis_size("wide") // 2
    my_rank = lax.axis_index("wide")
    my_child = my_rank // half_size
    local_rows = child_inverse.shape[0]
    columns = child_rhs.shape[0]
    update_width = coupling.shape[1]
    panels = child_rhs.astype(jnp.bfloat16)
    panel_full = panels
    bit_count = half_size.bit_length() - 1
    for level in range(bit_count):
        partner = from_partner(panel_full, "wide", level)
        upper_side = my_rank >> level & 1 == 1
        panel_full = jnp.where(
            upper_side,
            jnp.concatenate([partner, panel_full], axis=1),
            jnp.concatenate([panel_full, partner], axis=1),
        )
    product = lax.dot_general(
        panel_full, child_inverse, (((1,), (1,)), ((), ())), preferred_element_type=jnp.float32
    )
    row_global = my_rank % half_size * local_rows + jnp.arange(local_rows, dtype=jnp.int32)
    limit_rows = BLK * jnp.take(child_blocks, my_child)
    child_solution = jnp.where((row_global < limit_rows)[None, :], product, jnp.zeros_like(product))
    solved = child_solution.astype(jnp.bfloat16)
    partial_update = jnp.dot(solved, coupling, preferred_element_type=jnp.float32)
    targets = jnp.take(parent_block, my_child, axis=0)
    blank = jnp.zeros((columns, S0 // BLK, BLK), jnp.float32)
    placed = blank.at[:, targets].add(partial_update.reshape(columns, update_width // BLK, BLK))
    received = lax.psum_scatter(
        placed.reshape(columns, S0), "wide", scatter_dimension=1, tiled=True
    )
    parent_panel = (parent_rhs - received).astype(jnp.bfloat16)
    parent_solution = lax.dot_general(
        lax.all_gather(parent_panel, "wide", axis=1, tiled=True),
        parent_inverse,
        (((1,), (1,)), ((), ())),
        preferred_element_type=jnp.float32,
    )
    return (child_solution, parent_solution)


def solution(mesh):
    placed = (
        P("rhs", "wide"),
        P("rhs", "wide"),
        P("wide", None),
        P("wide", None),
        P("wide", None),
        P(),
        P(),
    )
    return jax.shard_map(
        on_device,
        mesh=mesh,
        in_specs=placed,
        out_specs=(P("rhs", "wide"), P("rhs", "wide")),
        check_vma=False,
    )
```

profile of v0, /device:TPU:1, one launch (start us, length us, event | category | flops | bytes accessed | tf_op | source)
XLA Modules:
  0.0 333.4 jit_solution(9278880204674069176)
XLA Ops:
  7.2 2.0 convert_element_type.9
  9.2 1.4 collective-permute-start
  10.6 1.6 collective-permute-done
  12.2 2.2 maximum_select_fusion.6
  14.3 1.3 collective-permute-start.1
  15.6 13.6 %collective-permute-done.1 = bf16[256,1152]{0,1:T(8,128)(2,1)} collective-permute-done((bf16[256,1152]{0,1:T(8,128)(2,1)}, bf16[256,1152]{0,1:T(8,128)(2,1)}, u32[]{:S(2)}, u32[]{:S(2)}) %collective-permute-start.1) | collective-permute-done | bytes 589856 | tf_op jit(solution)/shard_map/ppermute | solution.py:13
  29.2 2.9 maximum_select_fusion.5
  32.1 2.8 collective-permute-start.2
  34.9 25.3 %collective-permute-done.2 = bf16[256,2304]{0,1:T(8,128)(2,1)} collective-permute-done((bf16[256,2304]{0,1:T(8,128)(2,1)}, bf16[256,2304]{0,1:T(8,128)(2,1)}, u32[]{:S(2)}, u32[]{:S(2)}) %collective-permute-start.2) | collective-permute-done | bytes 1179680 | tf_op jit(solution)/shard_map/ppermute | solution.py:13
  60.2 3.7 %maximum_select_fusion.2 = bf16[256,4608]{0,1:T(8,128)(2,1)} fusion(bf16[256,2304]{0,1:T(8,128)(2,1)} %maximum_select_fusion.5, bf16[256,2304]{0,1:T(8,128)(2,1)} %collective-permute-done.2, pred[]{:T(512)S(6)} %eq.15), kind=kLoop, calls=%fused_computation.10 | loop fusion | flops 10616832 | bytes 4718593 | tf_op jit(solution)/shard_map/jit(_where)/select_n | solution.py:31
  63.9 1.7 collective-permute-start.3
  65.6 0.6 dynamic-slice.5
  66.9 48.4 %collective-permute-done.3 = bf16[256,4608]{0,1:T(8,128)(2,1)} collective-permute-done((bf16[256,4608]{0,1:T(8,128)(2,1)}, bf16[256,4608]{0,1:T(8,128)(2,1)}, u32[]{:S(2)}, u32[]{:S(2)}) %collective-permute-start.3) | collective-permute-done | bytes 2359328 | tf_op jit(solution)/shard_map/ppermute | solution.py:13
  115.3 11.3 %fusion.7 = f32[256,576]{0,1:T(8,128)S(1)} fusion(bf16[576,9216]{1,0:T(8,128)(2,1)} %param.9, bf16[256,4608]{0,1:T(8,128)(2,1)} %maximum_select_fusion.2, bf16[256,4608]{0,1:T(8,128)(2,1)} %collective-permute-done.3, pred[]{:T(512)S(6)} %eq.14, pred[576]{0:T(1024)(128)(4,1)S(1)} %add_compare_fusion), kind=kOutput, calls=%fused_computation.12 | convolution fusion | flops 2739290112 | bytes 15925825 | tf_op jit(solution)/shard_map/dot_general | solution.py:36
  126.7 1.4 convolution_bitcast_fusion
  128.2 0.4 copy.15
  128.5 6.0 %broadcast_in_dim.29 = f32[256,96,128]{2,0,1:T(8,128)} broadcast(f32[]{:T(128)} %constant.73.clone.1), dimensions={} | broadcast | bytes 12582916 | tf_op jit(solution)/shard_map/broadcast_in_dim | solution.py:45
  134.6 8.6 %scatter_fusion = f32[256,96,128]{2,0,1:T(8,128)} fusion(f32[256,96,128]{2,0,1:T(8,128)} %broadcast_in_dim.29, s32[24]{0:T(128)S(1)} %fusion.10, f32[24,256,128]{2,1,0:T(8,128)S(1)} %bitcast.23), kind=kCustom, calls=%fused_computation | custom fusion | flops 786432 | bytes 9437280 | tf_op jit(solution)/shard_map/scatter-add | solution.py:46
  143.2 12.6 %copy.11 = f32[256,96,128]{0,2,1:T(8,128)} copy(f32[256,96,128]{2,0,1:T(8,128)} %scatter_fusion) | data formatting | bytes 25165824 | tf_op jit(solution)/shard_map/scatter-add | solution.py:46
  156.0 0.7 copy-done.3
  156.9 106.7 %reduce-scatter.2.cloned.1.call-done = f32[256,384]{0,1:T(8,128)} async-done(((f32[256,12288]{0,1:T(8,128)}), f32[256,384]{0,1:T(8,128)}) %reduce-scatter.2.cloned.1.call-update) | async-done | bytes 393232 | tf_op jit(solution)/shard_map/reduce_scatter | solution.py:47
  263.6 1.7 subtract_convert_fusion
  265.3 51.4 %all-gather.2.cloned.1.call-done = bf16[256,12288]{0,1:T(8,128)(2,1)} async-done(((bf16[256,384]{0,1:T(8,128)(2,1)}), bf16[256,12288]{0,1:T(8,128)(2,1)}) %all-gather.2.cloned.1.call-update) | async-done | bytes 6291472 | tf_op jit(solution)/shard_map/all_gather | solution.py:52
  316.7 9.9 %fusion.12 = f32[256,384]{1,0:T(8,128)} fusion(bf16[256,12288]{0,1:T(8,128)(2,1)} %all-gather.2.cloned.1.call-done, bf16[384,12288]{1,0:T(8,128)(2,1)} %param.11), kind=kOutput, calls=%fused_computation.23 | convolution fusion | flops 2415919104 | bytes 16121856 | tf_op jit(solution)/shard_map/dot_general | solution.py:51
  (18 shorter events, 0.5 us)
Async XLA Ops:
  7.2 119.5 %copy-start = (bf16[576,3072]{1,0:T(8,128)(2,1)S(1)}, bf16[576,3072]{1,0:T(8,128)(2,1)}, u32[]{:S(2)}) copy-start(bf16[576,3072]{1,0:T(8,128)(2,1)} %param.10) | copy-start | bytes 10616836
  7.2 256.4 %reduce-scatter.2.cloned.1.call-start = ((), (), s32[]{:S(2)}) async-start(), calls=%async_computation.1 | async-start | bytes 12976128 | tf_op jit(solution)/shard_map/reduce_scatter | solution.py:47
  9.2 3.0 collective-permute-start
  14.3 14.9 %collective-permute-start.1 = (bf16[256,1152]{0,1:T(8,128)(2,1)}, bf16[256,1152]{0,1:T(8,128)(2,1)}, u32[]{:S(2)}, u32[]{:S(2)}) collective-permute-start(bf16[256,1152]{0,1:T(8,128)(2,1)} %maximum_select_fusion.6), channel_id=1, source_target_pairs={{0,8},{4,12},{8,0},{12,4},{16,24},{20,28},{24,16},{28,20},{32,40},... | collective-permute-start | bytes 1769480 | tf_op jit(solution)/shard_map/ppermute | solution.py:13
  15.6 50.0 %copy-start.5 = (s32[2]{0:T(128)S(1)}, s32[2]{0:T(128)}, u32[]{:S(2)}) copy-start(s32[2]{0:T(128)} %param.12) | copy-start | bytes 28
  15.6 51.2 %copy-start.4 = (s32[2,24]{1,0:T(2,128)S(1)}, s32[2,24]{1,0:T(2,128)}, u32[]{:S(2)}) copy-start(s32[2,24]{1,0:T(2,128)} %param.13) | copy-start | bytes 580
  32.1 28.1 %collective-permute-start.2 = (bf16[256,2304]{0,1:T(8,128)(2,1)}, bf16[256,2304]{0,1:T(8,128)(2,1)}, u32[]{:S(2)}, u32[]{:S(2)}) collective-permute-start(bf16[256,2304]{0,1:T(8,128)(2,1)} %maximum_select_fusion.5), channel_id=1, source_target_pairs={{0,16},{4,20},{8,24},{12,28},{16,0},{20,4},{24,8},{28,12},{32,48},... | collective-permute-start | bytes 3538952 | tf_op jit(solution)/shard_map/ppermute | solution.py:13
  63.9 51.4 %collective-permute-start.3 = (bf16[256,4608]{0,1:T(8,128)(2,1)}, bf16[256,4608]{0,1:T(8,128)(2,1)}, u32[]{:S(2)}, u32[]{:S(2)}) collective-permute-start(bf16[256,4608]{0,1:T(8,128)(2,1)} %maximum_select_fusion.2), channel_id=1, source_target_pairs={{0,32},{4,36},{8,40},{12,44},{16,48},{20,52},{24,56},{28,60},{32,0... | collective-permute-start | bytes 7077896 | tf_op jit(solution)/shard_map/ppermute | solution.py:13
  126.7 1.5 copy-start.2
  155.8 1.0 copy-start.3
  155.8 160.9 %all-gather.2.cloned.1.call-start = ((), (), s32[]{:S(2)}) async-start(), calls=%async_computation.2 | async-start | bytes 6488064 | tf_op jit(solution)/shard_map/all_gather | solution.py:52
  316.7 9.9 %copy-start.1 = (bf16[576,3072]{1,0:T(8,128)(2,1)S(1)}, bf16[576,3072]{1,0:T(8,128)(2,1)}, u32[]{:S(2)}) copy-start(bf16[576,3072]{1,0:T(8,128)(2,1)} %param.10) | copy-start | bytes 10616836
Sparse Core Ops, SparseCore 0:
  155.9 107.6 reduce-scatter.1
  266.7 49.9 all-gather.1
where the time goes:
time: 334 us; the launch traced here: 333 us
  waiting for transfers between devices  247 us (74%)
  matrix products  22.6 us (7%)
  other arithmetic  21.1 us (6%)
  local copies, waits for them, and re-layouts  20.5 us (6%)
  between operations  14.8 us (4%)
  starting transfers between devices  7.52 us (2%)
    reduce_scatter x1, waiting for transfers between devices, on_device(): lax.psum_scatter(placed.reshape(columns, S0), 'wide', scatter_dimension=1...  107 us
    ppermute x4, waiting for transfers between devices, from_partner(): return lax.ppermute(value, axis, pairs)  88.8 us
    all_gather x1, waiting for transfers between devices, on_device(): lax.all_gather(parent_panel, 'wide', axis=1, tiled=True)  51.4 us
    scatter-add x1, local copies, waits for them, and re-layouts, on_device(): blank.at[:, targets]  12.6 us
    dot_general x1, matrix products, on_device(): lax.dot_general(panel_full, child_inverse, (((1,), (1,)), ((), ())), pref...  11.3 us
    dot_general x1, matrix products, on_device(): lax.dot_general(lax.all_gather(parent_panel, 'wide', axis=1, tiled=True),...  9.86 us
    select_n x3, other arithmetic, on_device(): jnp.where(upper_side, jnp.concatenate([partner, panel_full], axis=1), jnp...  8.78 us
    scatter-add x1, other arithmetic, on_device(): blank.at[:, targets]  8.59 us
  transfers between devices with their start and end apart: 6, of which 6 were waited for; matrix products, arithmetic and copies ran while one was open for 0% of the time, Pallas kernels for 0%

commit v1 on v0

v1 whole, which is shorter than its diff:
```python
import functools

import jax
import jax.numpy as jnp
from jax import lax
from jax.experimental import pallas as pl
from jax.experimental.pallas import tpu as pltpu
from jax.sharding import PartitionSpec as P

BLK = 128
BF = jnp.bfloat16
F32 = jnp.float32
VMEM_LIMIT = 48 * 1024 * 1024


def flat(z, x, c):
    return (z % 4) * 8 + (x % 4) * 2 + c


def receive(value, source):
    pairs = []
    for z in range(4):
        for x in range(4):
            for c in range(2):
                pairs.append((flat(*source(z, x, c)), flat(z, x, c)))
    return lax.ppermute(value, "wide", pairs)


def from_sibling(value):
    return receive(value, lambda z, x, c: (z, x, 1 - c))


STEPS = (1, -1, 2)
REL = (0, 1, -1, 2)


def along(step, first):
    def source(z, x, c):
        return (z, x + step, c) if (c == 0) == first else (z + step, x, c)

    return source


def child_part_kernel(where_ref, inv_ref, own_ref, sib_ref, acc_ref, out_ref):
    @pl.when(pl.program_id(0) == 0)
    def _():
        out_ref[...] = acc_ref[...]

    block = jnp.concatenate([own_ref[...], sib_ref[...]], axis=1)
    out_ref[...] += jnp.dot(inv_ref[...], block, preferred_element_type=F32)


def child_part_first_kernel(where_ref, inv_ref, own_ref, sib_ref, out_ref):
    block = jnp.concatenate([own_ref[...], sib_ref[...]], axis=1)
    part = jnp.dot(inv_ref[...], block, preferred_element_type=F32)

    @pl.when(pl.program_id(0) == 0)
    def _():
        out_ref[...] = part

    @pl.when(pl.program_id(0) > 0)
    def _():
        out_ref[...] += part


def child_part(where, inverse, own, sib, acc=None):
    rows, depth = inverse.shape[0], 2 * inverse.shape[0]
    steps = own.shape[0] // depth
    half = own.shape[1]
    specs = [
        pl.BlockSpec((rows, depth), lambda i, w: (0, w[i])),
        pl.BlockSpec((depth, half), lambda i, w: (i, 0)),
        pl.BlockSpec((depth, half), lambda i, w: (i, 0)),
    ]
    operands = [where, inverse, own, sib]
    kernel = child_part_first_kernel
    if acc is not None:
        specs.append(pl.BlockSpec((rows, 2 * half), lambda i, w: (0, 0)))
        operands.append(acc)
        kernel = child_part_kernel
    return pl.pallas_call(
        kernel,
        grid_spec=pltpu.PrefetchScalarGridSpec(
            num_scalar_prefetch=1,
            grid=(steps,),
            in_specs=specs,
            out_specs=pl.BlockSpec((rows, 2 * half), lambda i, w: (0, 0)),
        ),
        out_shape=jax.ShapeDtypeStruct((rows, 2 * half), F32),
        compiler_params=pltpu.CompilerParams(vmem_limit_bytes=VMEM_LIMIT),
        cost_estimate=pl.CostEstimate(
            flops=2 * rows * depth * steps * 2 * half,
            bytes_accessed=2 * rows * depth * steps,
            transcendentals=0,
        ),
    )(*operands)


def coupling_kernel(solved_ref, coupling_ref, own_ref, sib_ref):
    half = own_ref.shape[1]
    update = jnp.dot(solved_ref[...], coupling_ref[...], preferred_element_type=F32)
    own_ref[0] = update[:half]
    sib_ref[0] = update[half:].astype(BF)


def coupling_product(solved, coupling, pieces):
    columns, depth = solved.shape
    width = coupling.shape[1] // pieces
    half = columns // 2
    return pl.pallas_call(
        coupling_kernel,
        grid=(pieces,),
        in_specs=[
            pl.BlockSpec((columns, depth), lambda i: (0, 0)),
            pl.BlockSpec((depth, width), lambda i: (0, i)),
        ],
        out_specs=[
            pl.BlockSpec((1, half, width), lambda i: (i, 0, 0)),
            pl.BlockSpec((1, half, width), lambda i: (i, 0, 0)),
        ],
        out_shape=[
            jax.ShapeDtypeStruct((pieces, half, width), F32),
            jax.ShapeDtypeStruct((pieces, half, width), BF),
        ],
        compiler_params=pltpu.CompilerParams(vmem_limit_bytes=VMEM_LIMIT),
        cost_estimate=pl.CostEstimate(
            flops=2 * columns * depth * width * pieces,
            bytes_accessed=2 * depth * width * pieces,
            transcendentals=0,
        ),
    )(solved, coupling)


def pick_kernel(count, blocks_ref, p_ref, out_ref, sems):
    def copy(i):
        source = pl.ds(pl.multiple_of(blocks_ref[i] * BLK, BLK), BLK)
        return pltpu.make_async_copy(
            p_ref.at[:, source], out_ref.at[:, pl.ds(i * BLK, BLK)], sems.at[i]
        )

    for i in range(count):
        copy(i).start()
    for i in range(count):
        copy(i).wait()


def pick_columns(blocks, inverse):
    count, rows = blocks.shape[0], inverse.shape[0]
    return pl.pallas_call(
        functools.partial(pick_kernel, count),
        in_specs=[
            pl.BlockSpec(memory_space=pltpu.SMEM),
            pl.BlockSpec(memory_space=pl.ANY),
        ],
        out_specs=pl.BlockSpec(memory_space=pl.ANY),
        out_shape=jax.ShapeDtypeStruct((rows, count * BLK), inverse.dtype),
        scratch_shapes=[pltpu.SemaphoreType.DMA((count,))],
        cost_estimate=pl.CostEstimate(
            flops=0, bytes_accessed=4 * rows * count * BLK, transcendentals=0
        ),
    )(blocks, inverse)


NT = (((1,), (1,)), ((), ()))


def base_kernel(where_ref, p_ref, *refs):
    r_refs, out_ref = refs[:-1], refs[-1]
    i = pl.program_id(0)

    @pl.when(i == 0)
    def _():
        out_ref[...] = jnp.zeros_like(out_ref)

    for k, r_ref in enumerate(r_refs):

        @pl.when(i // 4 == k)
        def _(r_ref=r_ref):
            out_ref[...] += lax.dot_general(
                r_ref[i % 4], p_ref[...], NT, preferred_element_type=F32
            )


def base_product(where, inverse, parts):
    columns, rows = parts[0].shape[1:]
    steps = 4 * len(parts)
    whole = pl.BlockSpec(parts[0].shape, lambda i, w: (0, 0, 0))
    return pl.pallas_call(
        base_kernel,
        grid_spec=pltpu.PrefetchScalarGridSpec(
            num_scalar_prefetch=1,
            grid=(steps,),
            in_specs=[pl.BlockSpec((rows, rows), lambda i, w: (0, w[i]))]
            + [whole] * len(parts),
            out_specs=pl.BlockSpec((columns, rows), lambda i, w: (0, 0)),
        ),
        out_shape=jax.ShapeDtypeStruct((columns, rows), F32),
        compiler_params=pltpu.CompilerParams(vmem_limit_bytes=VMEM_LIMIT),
        cost_estimate=pl.CostEstimate(
            flops=2 * columns * rows * rows * steps,
            bytes_accessed=2 * rows * rows * steps,
            transcendentals=0,
        ),
    )(where, inverse, *parts)


def final_kernel(core_ref, base_ref, p_ref, *refs):
    own_refs, sib_refs, out_ref = refs[:4], refs[4:8], refs[8]
    half, width = own_refs[0].shape[1:]
    total = jnp.zeros(base_ref.shape, F32)
    for j in range(4):
        for i in range(4):
            block = jnp.concatenate([own_refs[j][i], sib_refs[i][j]], axis=0)
            at = (j * 4 + i) * width
            total += lax.dot_general(
                block, p_ref[:, at : at + width], NT, preferred_element_type=F32
            )
    core = core_ref[0]

    @pl.when(core == 0)
    def _():
        out_ref[...] = base_ref[...] - total

    @pl.when(core == 1)
    def _():
        out_ref[:half] = base_ref[:half] - total[half:]
        out_ref[half:] = base_ref[half:] - total[:half]


def final_product(core, base, picked, own, sib):
    vmem = pl.BlockSpec(memory_space=pltpu.VMEM)
    return pl.pallas_call(
        final_kernel,
        in_specs=[pl.BlockSpec(memory_space=pltpu.SMEM)] + [vmem] * 10,
        out_specs=vmem,
        out_shape=jax.ShapeDtypeStruct(base.shape, F32),
        compiler_params=pltpu.CompilerParams(vmem_limit_bytes=VMEM_LIMIT),
        cost_estimate=pl.CostEstimate(
            flops=2 * base.shape[0] * picked.shape[0] * picked.shape[1],
            bytes_accessed=2 * picked.shape[0] * picked.shape[1],
            transcendentals=0,
        ),
    )(core, base, picked, *own, *sib)


def gather_16(block):
    first = [block] + [receive(block, along(s, True)) for s in STEPS]
    part = jnp.stack(first)
    return [part] + [receive(part, along(s, False)) for s in STEPS]


def on_device(
    child_rhs, parent_rhs, child_inverse, coupling, parent_inverse, child_blocks, parent_block
):
    rank = lax.axis_index("wide")
    z, x, core = rank // 8, rank // 2 % 4, rank % 2
    child = z // 2
    local_rows = child_inverse.shape[0]
    columns = child_rhs.shape[0]
    half = columns // 2

    mine = child_rhs.T.astype(BF)
    keep = lax.dynamic_slice_in_dim(mine, core * half, half, axis=1)
    give = lax.dynamic_slice_in_dim(mine, (1 - core) * half, half, axis=1)
    got = from_sibling(give)
    b0 = jnp.where(
        core == 0, jnp.concatenate([keep, got], axis=0), jnp.concatenate([got, keep], axis=0)
    )
    xp = receive(b0, lambda z, x, c: (z, x + 1, c))
    xm = receive(b0, lambda z, x, c: (z, x - 1, c))
    zb = receive(b0, lambda z, x, c: (z ^ 1, x, c))
    x2 = receive(xp, lambda z, x, c: (z, x + 1, c))
    zm = receive(zb, lambda z, x, c: (z, x - 1, c))
    zp = receive(xp, lambda z, x, c: (z ^ 1, x, c))
    third = b0.shape[0] // 3
    z2 = jnp.concatenate(
        [
            receive(zp[:third], lambda z, x, c: (z, x + 1, c)),
            receive(zm[third : 2 * third], lambda z, x, c: (z, x - 1, c)),
            receive(x2[2 * third :], lambda z, x, c: (z ^ 1, x, c)),
        ],
        axis=0,
    )
    zr = z % 2
    other = 1 - zr

    def chip(zz, xx):
        return zz * 4 + xx % 4

    g1 = jnp.concatenate([b0, xp, xm, zb], axis=0)
    g2 = jnp.concatenate([x2, zm, zp], axis=0)
    w1 = jnp.stack([chip(zr, x), chip(zr, x + 1), chip(zr, x + 3), chip(other, x)])
    w2 = jnp.stack([chip(zr, x + 2), chip(other, x + 3), chip(other, x + 1)])
    w3 = jnp.stack([chip(other, x + 2)])
    acc = child_part(w1, child_inverse, g1, from_sibling(g1))
    acc = child_part(w2, child_inverse, g2, from_sibling(g2), acc)
    acc = child_part(w3, child_inverse, z2, from_sibling(z2), acc)

    row = (rank % 16) * local_rows + jnp.arange(local_rows, dtype=jnp.int32)
    limit = BLK * jnp.take(child_blocks, child)
    solved = jnp.where((row < limit)[:, None], acc, jnp.zeros_like(acc))
    swapped = jnp.concatenate([solved[:, half:], solved[:, :half]], axis=1)
    child_solution = jnp.where(core == 0, solved, swapped).T

    own, sib = coupling_product(solved.T.astype(BF), coupling, 8)
    chip_sum = (own + from_sibling(sib).astype(F32)).astype(BF)
    groups = [
        [flat(2 * h + dz, xx, c) for dz in range(2) for xx in range(4)]
        for h in range(2)
        for c in range(2)
    ]
    pieces = lax.all_to_all(
        chip_sum, "wide", split_axis=0, concat_axis=0, axis_index_groups=groups, tiled=True
    )
    update = jnp.sum(pieces.astype(F32), axis=0).astype(BF)
    u_own = gather_16(update)
    u_sib = [from_sibling(part) for part in u_own]

    r_own = gather_16(parent_rhs.astype(BF))
    r_sib = [from_sibling(part) for part in r_own]

    def places(c):
        rel = jnp.array(REL, jnp.int32)
        second, first = rel[:, None], rel[None, :]
        dx = jnp.where(c == 0, first, second)
        dz = jnp.where(c == 0, second, first)
        return ((z + dz) % 4).reshape(-1), ((x + dx) % 4).reshape(-1)

    zs, xs = places(core)
    zs_sib, xs_sib = places(1 - core)
    where = jnp.concatenate(
        [zs * 8 + xs * 2 + core, zs_sib * 8 + xs_sib * 2 + (1 - core)]
    )
    base = base_product(where, parent_inverse, r_own + r_sib)
    table = parent_block.reshape(2 * 8, 3)
    blocks = table[zs * 4 + xs].reshape(-1)
    picked = pick_columns(blocks, parent_inverse)
    parent_solution = final_product(core.reshape(1), base, picked, u_own, u_sib)
    return (child_solution, parent_solution)


def solution(mesh):
    placed = (
        P("rhs", "wide"),
        P("rhs", "wide"),
        P("wide", None),
        P("wide", None),
        P("wide", None),
        P(),
        P(),
    )
    return jax.shard_map(
        on_device,
        mesh=mesh,
        in_specs=placed,
        out_specs=(P("rhs", "wide"), P("rhs", "wide")),
        check_vma=False,
    )
```

time: 334 us -> 302 us (0.904)
  waiting for transfers between devices: 247 us -> 40.8 us
  Pallas kernels: 0 us -> 189 us
  starting transfers between devices: 7.52 us -> 48.9 us
  matrix products: 22.6 us -> 0 us
  between operations: 14.8 us -> 1.67 us
  other arithmetic: 21.1 us -> 9.72 us
  local copies, waits for them, and re-layouts: 20.5 us -> 11.4 us
    pallas_call x0 -> x7, Pallas kernels: none -> 189 us  [the longest x1 145 us: pick_columns(): pl.pallas_call(functools.partial(pick_kernel, count), in_specs=[pl.BlockS...]
    reduce_scatter x1 -> x0, waiting for transfers between devices: 107 us -> none  [on_device(): lax.psum_scatter(placed.reshape(columns, S0), 'wide', scatter_dimension=1...]
    ppermute x4 -> x34, waiting for transfers between devices: 88.8 us -> 34.9 us  [receive(): return lax.ppermute(value, 'wide', pairs)]
    all_gather x1 -> x0, waiting for transfers between devices: 51.4 us -> none  [on_device(): lax.all_gather(parent_panel, 'wide', axis=1, tiled=True)]
    ppermute x4 -> x34, starting transfers between devices: 7.26 us -> 44.5 us  [receive(): return lax.ppermute(value, 'wide', pairs)]
    dot_general x3 -> x0, matrix products: 22.6 us -> none  [the longest x1 11.3 us: on_device(): lax.dot_general(panel_full, child_inverse, (((1,), (1,)), ((), ())), pref...]
    scatter-add x1 -> x0, local copies, waits for them, and re-layouts: 12.6 us -> none  [on_device(): blank.at[:, targets]]
    select_n x4 -> x2, other arithmetic: 8.79 us -> 0.11 us  [the longest x1 0.09 us: on_device(): jnp.where(core == 0, jnp.concatenate([keep, got], axis=0), jnp.concatenat...]
  transfers between devices with their start and end apart: 6 -> 35, of which waited for: 6 -> 14; matrix products, arithmetic and copies ran while one was open for 0% -> 5% of each run, Pallas kernels for 0% -> 59%
where the time goes in v1:
time: 302 us; the launch traced here: 301 us
  Pallas kernels  189 us (63%)
  starting transfers between devices  48.9 us (16%)
  waiting for transfers between devices  40.8 us (14%)
  local copies, waits for them, and re-layouts  11.4 us (4%)
  other arithmetic  9.72 us (3%)
    pallas_call x1, Pallas kernels, pick_columns(): pl.pallas_call(functools.partial(pick_kernel, count), in_specs=[pl.BlockS...  145 us
    ppermute x34, starting transfers between devices, receive(): return lax.ppermute(value, 'wide', pairs)  44.5 us
    ppermute x34, waiting for transfers between devices, receive(): return lax.ppermute(value, 'wide', pairs)  34.9 us
    pallas_call x1, Pallas kernels, base_product(): pl.pallas_call(base_kernel, grid_spec=pltpu.PrefetchScalarGridSpec(num_sc...  22.8 us
    pallas_call x3, Pallas kernels, child_part(): pl.pallas_call(kernel, grid_spec=pltpu.PrefetchScalarGridSpec(num_scalar_...  11.6 us
  transfers between devices with their start and end apart: 35, of which 14 were waited for; matrix products, arithmetic and copies ran while one was open for 5% of the time, Pallas kernels for 59%

profile of v1, /device:TPU:1, one launch (start us, length us, event | category | flops | bytes accessed | tf_op | source)
XLA Modules:
  0.0 301.2 jit_solution(13575556744393285916)
XLA Ops:
  6.2 2.5 collective-permute-start.1
  8.7 4.6 %collective-permute-done.4 = bf16[1152,128]{1,0:T(8,128)(2,1)S(1)} collective-permute-done((bf16[1152,128]{1,0:T(8,128)(2,1)S(1)}, bf16[1152,128]{1,0:T(8,128)(2,1)S(1)}, u32[]{:S(2)}, u32[]{:S(2)}) %collective-permute-start.4) | collective-permute-done | bytes 294944 | tf_op jit(solution)/shard_map/ppermute | solution.py:26
  14.4 3.4 %collective-permute-start.7 = (bf16[1152,128]{1,0:T(8,128)(2,1)S(1)}, bf16[1152,128]{1,0:T(8,128)(2,1)S(1)}, u32[]{:S(2)}, u32[]{:S(2)}) collective-permute-start(bf16[1152,128]{1,0:T(8,128)(2,1)S(1)} %collective-permute-done.1), channel_id=1, source_target_pairs={{8,0},{12,4},{16,8},{20,12},{24,16},{28,20},{0,24},{4,28},{40,32},... | collective-permute-start | bytes 884744 | tf_op jit(solution)/shard_map/ppermute | solution.py:26
  17.9 3.0 %collective-permute-start.12 = (bf16[4608,128]{1,0:T(8,128)(2,1)S(1)}, bf16[4608,128]{1,0:T(8,128)(2,1)S(1)}, u32[]{:S(2)}, u32[]{:S(2)}) collective-permute-start(bf16[4608,128]{1,0:T(8,128)(2,1)S(1)} %pad_maximum_fusion.own_ref), channel_id=1, source_target_pairs={{4,0},{0,4},{12,8},{8,12},{20,16},{16,20},{28,24},{24,28},{36,32},... | collective-permute-start | bytes 3538952 | tf_op jit(solution)/shard_map/ppermute | solution.py:26
  23.8 5.6 %collective-permute-done.2 = bf16[1152,128]{1,0:T(8,128)(2,1)S(1)} collective-permute-done((bf16[1152,128]{1,0:T(8,128)(2,1)S(1)}, bf16[1152,128]{1,0:T(8,128)(2,1)S(1)}, u32[]{:S(2)}, u32[]{:S(2)}) %collective-permute-start.2) | collective-permute-done | bytes 294944 | tf_op jit(solution)/shard_map/ppermute | solution.py:26
  41.3 5.1 %shard_map.104.acc_ref = f32[576,256]{1,0:T(8,128)S(1)} custom-call(s32[4]{0:T(128)S(1)} %pad_add_fusion.1.where_ref, bf16[576,9216]{1,0:T(8,128)(2,1)} %inv_ref.5, bf16[4608,128]{1,0:T(8,128)(2,1)S(1)} %pad_maximum_fusion.own_ref, bf16[4608,128]{1,0:T(8,128)(2,1)S(1)} %collective-permute-done.12.sib_ref), custom_call_target="tpu_custom_call" | custom-call | flops 1358954496 | bytes 5308416 | tf_op jit(solution)/shard_map/pallas_call | solution.py:81
  46.4 4.5 %shard_map.105.acc_ref = f32[576,256]{1,0:T(8,128)S(1)} custom-call(s32[3]{0:T(128)S(1)} %pad_add_fusion.where_ref, bf16[576,9216]{1,0:T(8,128)(2,1)} %inv_ref.5, bf16[3456,128]{1,0:T(8,128)(2,1)S(1)} %constant_dynamic-update-slice_fusion.3.own_ref, bf16[3456,128]{1,0:T(8,128)(2,1)} %collective-permute-done.10.sib_ref, f32[576,256]{1,0:T(8,128)S(1)} %shard_map.104.acc_ref), custom_call_target="tpu_custom_call" | custom-call | flops 1019215872 | bytes 3981312 | tf_op jit(solution)/shard_map/pallas_call | solution.py:81
  53.8 2.1 copy.13
  58.0 3.1 %shard_map.109 = (f32[8,128,384]{2,1,0:T(8,128)S(1)}, bf16[8,128,384]{2,1,0:T(8,128)(2,1)S(1)}) custom-call(bf16[256,576]{1,0:T(8,128)(2,1)S(1)} %get-tuple-element.21.solved_ref, bf16[576,3072]{1,0:T(8,128)(2,1)S(1)} %copy-done), custom_call_target="tpu_custom_call" | custom-call | flops 905969664 | bytes 3538944 | tf_op jit(solution)/shard_map/pallas_call | solution.py:110
  61.2 3.4 %collective-permute-start.15 = (bf16[256,384]{1,0:T(8,128)(2,1)S(1)}, bf16[256,384]{1,0:T(8,128)(2,1)S(1)}, u32[]{:S(2)}, u32[]{:S(2)}) collective-permute-start(bf16[256,384]{1,0:T(8,128)(2,1)S(1)} %convert_element_type.21), channel_id=1, source_target_pairs={{16,0},{68,4},{24,8},{76,12},{0,16},{84,20},{8,24},{92,28},{48,32}... | collective-permute-start | bytes 589832 | tf_op jit(solution)/shard_map/ppermute | solution.py:26
  64.6 2.7 collective-permute-start.13
  68.0 2.5 collective-permute-done.14
  73.1 4.4 %all-to-all-start = ((bf16[8,128,384]{2,1,0:T(8,128)(2,1)}), bf16[8,128,384]{2,1,0:T(8,128)(2,1)}, u32[]{:S(2)}, u32[]{:S(2)}) async-start(bf16[8,128,384]{2,1,0:T(8,128)(2,1)} %add_convert_fusion), calls=%async_computation | async-start | bytes 1572864 | tf_op jit(solution)/shard_map/all_to_all | solution.py:312
  78.8 2.4 collective-permute-start.18
  84.7 5.9 %all-to-all-done = bf16[8,128,384]{2,1,0:T(8,128)(2,1)} async-done(((bf16[8,128,384]{2,1,0:T(8,128)(2,1)}), bf16[8,128,384]{2,1,0:T(8,128)(2,1)}, u32[]{:S(2)}, u32[]{:S(2)}) %all-to-all-start) | async-done | bytes 786464 | tf_op jit(solution)/shard_map/all_to_all | solution.py:312
  91.8 3.8 %collective-permute-start.26 = (bf16[128,384]{1,0:T(8,128)(2,1)S(1)}, bf16[128,384]{1,0:T(8,128)(2,1)S(1)}, u32[]{:S(2)}, u32[]{:S(2)}) collective-permute-start(bf16[128,384]{1,0:T(8,128)(2,1)S(1)} %reduce_sum.12), channel_id=1, source_target_pairs={{16,0},{68,4},{24,8},{76,12},{0,16},{84,20},{8,24},{92,28},{48,32}... | collective-permute-start | bytes 294920 | tf_op jit(solution)/shard_map/ppermute | solution.py:26
  96.3 2.6 collective-permute-done.17.refs_2_
  98.8 9.0 %collective-permute-done.18.refs_3_ = bf16[4,256,384]{2,1,0:T(8,128)(2,1)S(1)} collective-permute-done((bf16[4,256,384]{2,1,0:T(8,128)(2,1)S(1)}, bf16[4,256,384]{2,1,0:T(8,128)(2,1)S(1)}, u32[]{:S(2)}, u32[]{:S(2)}) %collective-permute-start.18) | collective-permute-done | bytes 786464 | tf_op jit(solution)/shard_map/ppermute | solution.py:26
  107.9 2.3 collective-permute-start.25
  110.6 2.3 collective-permute-done.25
  120.0 145.3 %shard_map.108.p_ref = bf16[384,6144]{1,0:T(8,128)(2,1)} custom-call(s32[48]{0:T(128)} %reshape.182.blocks_ref, bf16[384,12288]{1,0:T(8,128)(2,1)} %p_ref.3), custom_call_target="tpu_custom_call" | custom-call | bytes 9437184 | tf_op jit(solution)/shard_map/pallas_call | solution.py:149
  266.5 2.1 collective-permute-start.30
  272.4 22.8 %shard_map.107.base_ref = f32[256,384]{1,0:T(8,128)S(1)} custom-call(s32[32]{0:T(128)S(1)} %pad_add_fusion.2.where_ref, bf16[384,12288]{1,0:T(8,128)(2,1)} %p_ref.3, bf16[4,256,384]{2,1,0:T(8,128)(2,1)S(1)} %pad_maximum_fusion.1.refs_0_, bf16[4,256,384]{2,1,0:T(8,128)(2,1)S(1)} %collective-permute-done.16.refs_1_, ...), custom_call_target="tpu_custom_call" | custom-call | flops 2415919104 | bytes 9437184 | tf_op jit(solution)/shard_map/pallas_call | solution.py:188
  295.3 6.0 %shard_map.110 = f32[256,384]{1,0:T(8,128)} custom-call(s32[1]{0:T(128)} %bitcast.13.core_ref, f32[256,384]{1,0:T(8,128)S(1)} %shard_map.107.base_ref, bf16[384,6144]{1,0:T(8,128)(2,1)} %shard_map.108.p_ref, bf16[4,128,384]{2,1,0:T(8,128)(2,1)S(1)} %pad_maximum_fusion.2.refs_0_, bf16[4,128,384]{2,1,0:T(8,128)(2,1)} %collective-permute-done.27.refs_1_, ...), custom_call_target="tpu_custom_call" | custom-call | flops 1207959552 | bytes 4718592 | tf_op jit(solution)/shard_map/pallas_call | solution.py:232
  (120 shorter events, 48.3 us)
Async XLA Ops:
  4.4 8.9 %collective-permute-start.4 = (bf16[1152,128]{1,0:T(8,128)(2,1)S(1)}, bf16[1152,128]{1,0:T(8,128)(2,1)S(1)}, u32[]{:S(2)}, u32[]{:S(2)}) collective-permute-start(bf16[1152,128]{1,0:T(8,128)(2,1)S(1)} %maximum_select_fusion.1), channel_id=1, source_target_pairs={{32,0},{36,4},{40,8},{44,12},{48,16},{52,20},{56,24},{60,28},{0,32... | collective-permute-start | bytes 884744 | tf_op jit(solution)/shard_map/ppermute | solution.py:26
  8.7 9.1 %collective-permute-start.11 = (bf16[1152,128]{1,0:T(8,128)(2,1)S(1)}, bf16[1152,128]{1,0:T(8,128)(2,1)S(1)}, u32[]{:S(2)}, u32[]{:S(2)}) collective-permute-start(bf16[1152,128]{1,0:T(8,128)(2,1)S(1)} %maximum_select_fusion.1), channel_id=1, source_target_pairs={{24,0},{28,4},{0,8},{4,12},{8,16},{12,20},{16,24},{20,28},{56,32},... | collective-permute-start | bytes 884744 | tf_op jit(solution)/shard_map/ppermute | solution.py:26
  13.3 10.5 %collective-permute-start.5 = (bf16[1152,128]{1,0:T(8,128)(2,1)S(1)}, bf16[1152,128]{1,0:T(8,128)(2,1)S(1)}, u32[]{:S(2)}, u32[]{:S(2)}) collective-permute-start(bf16[1152,128]{1,0:T(8,128)(2,1)S(1)} %collective-permute-done.4), channel_id=1, source_target_pairs={{24,0},{28,4},{0,8},{4,12},{8,16},{12,20},{16,24},{20,28},{56,32},... | collective-permute-start | bytes 884744 | tf_op jit(solution)/shard_map/ppermute | solution.py:26
  17.9 23.4 %collective-permute-start.12 = (bf16[4608,128]{1,0:T(8,128)(2,1)S(1)}, bf16[4608,128]{1,0:T(8,128)(2,1)S(1)}, u32[]{:S(2)}, u32[]{:S(2)}) collective-permute-start(bf16[4608,128]{1,0:T(8,128)(2,1)S(1)} %pad_maximum_fusion.own_ref), channel_id=1, source_target_pairs={{4,0},{0,4},{12,8},{8,12},{20,16},{16,20},{28,24},{24,28},{36,32},... | collective-permute-start | bytes 3538952 | tf_op jit(solution)/shard_map/ppermute | solution.py:26
  20.9 8.6 %collective-permute-start.2 = (bf16[1152,128]{1,0:T(8,128)(2,1)S(1)}, bf16[1152,128]{1,0:T(8,128)(2,1)S(1)}, u32[]{:S(2)}, u32[]{:S(2)}) collective-permute-start(bf16[1152,128]{1,0:T(8,128)(2,1)S(1)} %collective-permute-done.1), channel_id=1, source_target_pairs={{32,0},{36,4},{40,8},{44,12},{48,16},{52,20},{56,24},{60,28},{0,32... | collective-permute-start | bytes 884744 | tf_op jit(solution)/shard_map/ppermute | solution.py:26
  30.2 16.2 %collective-permute-start.10 = (bf16[3456,128]{1,0:T(8,128)(2,1)S(1)}, bf16[3456,128]{1,0:T(8,128)(2,1)}, u32[]{:S(2)}, u32[]{:S(2)}) collective-permute-start(bf16[3456,128]{1,0:T(8,128)(2,1)S(1)} %constant_dynamic-update-slice_fusion.3.own_ref), channel_id=1, source_target_pairs={{4,0},{0,4},{12,8},{8,12},{20,16},{16,20},{28,24},{24,28},{36,32},... | collective-permute-start | bytes 2654216 | tf_op jit(solution)/shard_map/ppermute | solution.py:26
  39.7 11.2 %collective-permute-start.9 = (bf16[1152,128]{1,0:T(8,128)(2,1)S(1)}, bf16[1152,128]{1,0:T(8,128)(2,1)S(1)}, u32[]{:S(2)}, u32[]{:S(2)}) collective-permute-start(bf16[1152,128]{1,0:T(8,128)(2,1)S(1)} %constant_dynamic-update-slice_fusion.own_ref), channel_id=1, source_target_pairs={{4,0},{0,4},{12,8},{8,12},{20,16},{16,20},{28,24},{24,28},{36,32},... | collective-permute-start | bytes 884744 | tf_op jit(solution)/shard_map/ppermute | solution.py:26
  61.1 11.0 %collective-permute-start.23 = (bf16[8,128,384]{2,1,0:T(8,128)(2,1)S(1)}, bf16[8,128,384]{2,1,0:T(8,128)(2,1)S(1)}, u32[]{:S(2)}, u32[]{:S(2)}) collective-permute-start(bf16[8,128,384]{2,1,0:T(8,128)(2,1)S(1)} %get-tuple-element.5), channel_id=1, source_target_pairs={{4,0},{0,4},{12,8},{8,12},{20,16},{16,20},{28,24},{24,28},{36,32},... | collective-permute-start | bytes 2359304 | tf_op jit(solution)/shard_map/ppermute | solution.py:26
  70.6 12.1 %collective-permute-start.16 = (bf16[4,256,384]{2,1,0:T(8,128)(2,1)S(1)}, bf16[4,256,384]{2,1,0:T(8,128)(2,1)S(1)}, u32[]{:S(2)}, u32[]{:S(2)}) collective-permute-start(bf16[4,256,384]{2,1,0:T(8,128)(2,1)S(1)} %pad_maximum_fusion.1.refs_0_), channel_id=1, source_target_pairs={{32,0},{12,4},{40,8},{20,12},{48,16},{28,20},{56,24},{4,28},{64,32... | collective-permute-start | bytes 2359304 | tf_op jit(solution)/shard_map/ppermute | solution.py:26
  73.1 17.4 %all-to-all-start = ((bf16[8,128,384]{2,1,0:T(8,128)(2,1)}), bf16[8,128,384]{2,1,0:T(8,128)(2,1)}, u32[]{:S(2)}, u32[]{:S(2)}) async-start(bf16[8,128,384]{2,1,0:T(8,128)(2,1)} %add_convert_fusion), calls=%async_computation | async-start | bytes 1572864 | tf_op jit(solution)/shard_map/all_to_all | solution.py:312
  77.5 21.3 %collective-permute-start.17 = (bf16[4,256,384]{2,1,0:T(8,128)(2,1)S(1)}, bf16[4,256,384]{2,1,0:T(8,128)(2,1)S(1)}, u32[]{:S(2)}, u32[]{:S(2)}) collective-permute-start(bf16[4,256,384]{2,1,0:T(8,128)(2,1)S(1)} %pad_maximum_fusion.1.refs_0_), channel_id=1, source_target_pairs={{96,0},{28,4},{104,8},{4,12},{112,16},{12,20},{120,24},{20,28},{0,... | collective-permute-start | bytes 2359304 | tf_op jit(solution)/shard_map/ppermute | solution.py:26
  78.8 29.0 %collective-permute-start.18 = (bf16[4,256,384]{2,1,0:T(8,128)(2,1)S(1)}, bf16[4,256,384]{2,1,0:T(8,128)(2,1)S(1)}, u32[]{:S(2)}, u32[]{:S(2)}) collective-permute-start(bf16[4,256,384]{2,1,0:T(8,128)(2,1)S(1)} %pad_maximum_fusion.1.refs_0_), channel_id=1, source_target_pairs={{64,0},{20,4},{72,8},{28,12},{80,16},{4,20},{88,24},{12,28},{96,32... | collective-permute-start | bytes 2359304 | tf_op jit(solution)/shard_map/ppermute | solution.py:26
  81.6 35.1 %collective-permute-start.19 = (bf16[4,256,384]{2,1,0:T(8,128)(2,1)S(1)}, bf16[4,256,384]{2,1,0:T(8,128)(2,1)}, u32[]{:S(2)}, u32[]{:S(2)}) collective-permute-start(bf16[4,256,384]{2,1,0:T(8,128)(2,1)S(1)} %pad_maximum_fusion.1.refs_0_), channel_id=1, source_target_pairs={{4,0},{0,4},{12,8},{8,12},{20,16},{16,20},{28,24},{24,28},{36,32},... | collective-permute-start | bytes 2359304 | tf_op jit(solution)/shard_map/ppermute | solution.py:26
  82.7 34.1 %collective-permute-start.20 = (bf16[4,256,384]{2,1,0:T(8,128)(2,1)S(1)}, bf16[4,256,384]{2,1,0:T(8,128)(2,1)}, u32[]{:S(2)}, u32[]{:S(2)}) collective-permute-start(bf16[4,256,384]{2,1,0:T(8,128)(2,1)S(1)} %collective-permute-done.16.refs_1_), channel_id=1, source_target_pairs={{4,0},{0,4},{12,8},{8,12},{20,16},{16,20},{28,24},{24,28},{36,32},... | collective-permute-start | bytes 2359304 | tf_op jit(solution)/shard_map/ppermute | solution.py:26
  91.8 18.4 %collective-permute-start.26 = (bf16[128,384]{1,0:T(8,128)(2,1)S(1)}, bf16[128,384]{1,0:T(8,128)(2,1)S(1)}, u32[]{:S(2)}, u32[]{:S(2)}) collective-permute-start(bf16[128,384]{1,0:T(8,128)(2,1)S(1)} %reduce_sum.12), channel_id=1, source_target_pairs={{16,0},{68,4},{24,8},{76,12},{0,16},{84,20},{8,24},{92,28},{48,32}... | collective-permute-start | bytes 294920 | tf_op jit(solution)/shard_map/ppermute | solution.py:26
  98.8 167.7 %collective-permute-start.21 = (bf16[4,256,384]{2,1,0:T(8,128)(2,1)S(1)}, bf16[4,256,384]{2,1,0:T(8,128)(2,1)}, u32[]{:S(2)}, u32[]{:S(2)}) collective-permute-start(bf16[4,256,384]{2,1,0:T(8,128)(2,1)S(1)} %collective-permute-done.17.refs_2_), channel_id=1, source_target_pairs={{4,0},{0,4},{12,8},{8,12},{20,16},{16,20},{28,24},{24,28},{36,32},... | collective-permute-start | bytes 2359304 | tf_op jit(solution)/shard_map/ppermute | solution.py:26
  112.8 159.6 %collective-permute-start.22 = (bf16[4,256,384]{2,1,0:T(8,128)(2,1)S(1)}, bf16[4,256,384]{2,1,0:T(8,128)(2,1)}, u32[]{:S(2)}, u32[]{:S(2)}) collective-permute-start(bf16[4,256,384]{2,1,0:T(8,128)(2,1)S(1)} %collective-permute-done.18.refs_3_), channel_id=1, source_target_pairs={{4,0},{0,4},{12,8},{8,12},{20,16},{16,20},{28,24},{24,28},{36,32},... | collective-permute-start | bytes 2359304 | tf_op jit(solution)/shard_map/ppermute | solution.py:26
  115.0 153.7 %collective-permute-start.27 = (bf16[4,128,384]{2,1,0:T(8,128)(2,1)S(1)}, bf16[4,128,384]{2,1,0:T(8,128)(2,1)}, u32[]{:S(2)}, u32[]{:S(2)}) collective-permute-start(bf16[4,128,384]{2,1,0:T(8,128)(2,1)S(1)} %pad_maximum_fusion.2.refs_0_), channel_id=1, source_target_pairs={{32,0},{12,4},{40,8},{20,12},{48,16},{28,20},{56,24},{4,28},{64,32... | collective-permute-start | bytes 1179656 | tf_op jit(solution)/shard_map/ppermute | solution.py:26
  116.8 152.0 %collective-permute-start.28 = (bf16[4,128,384]{2,1,0:T(8,128)(2,1)S(1)}, bf16[4,128,384]{2,1,0:T(8,128)(2,1)}, u32[]{:S(2)}, u32[]{:S(2)}) collective-permute-start(bf16[4,128,384]{2,1,0:T(8,128)(2,1)S(1)} %pad_maximum_fusion.2.refs_0_), channel_id=1, source_target_pairs={{96,0},{28,4},{104,8},{4,12},{112,16},{12,20},{120,24},{20,28},{0,... | collective-permute-start | bytes 1179656 | tf_op jit(solution)/shard_map/ppermute | solution.py:26
  116.8 152.4 %collective-permute-start.29 = (bf16[4,128,384]{2,1,0:T(8,128)(2,1)S(1)}, bf16[4,128,384]{2,1,0:T(8,128)(2,1)}, u32[]{:S(2)}, u32[]{:S(2)}) collective-permute-start(bf16[4,128,384]{2,1,0:T(8,128)(2,1)S(1)} %pad_maximum_fusion.2.refs_0_), channel_id=1, source_target_pairs={{64,0},{20,4},{72,8},{28,12},{80,16},{4,20},{88,24},{12,28},{96,32... | collective-permute-start | bytes 1179656 | tf_op jit(solution)/shard_map/ppermute | solution.py:26
  266.5 28.7 %collective-permute-start.30 = (bf16[4,128,384]{2,1,0:T(8,128)(2,1)S(1)}, bf16[4,128,384]{2,1,0:T(8,128)(2,1)}, u32[]{:S(2)}, u32[]{:S(2)}) collective-permute-start(bf16[4,128,384]{2,1,0:T(8,128)(2,1)S(1)} %pad_maximum_fusion.2.refs_0_), channel_id=1, source_target_pairs={{4,0},{0,4},{12,8},{8,12},{20,16},{16,20},{28,24},{24,28},{36,32},... | collective-permute-start | bytes 1179656 | tf_op jit(solution)/shard_map/ppermute | solution.py:26
  268.7 26.5 %collective-permute-start.31 = (bf16[4,128,384]{2,1,0:T(8,128)(2,1)}, bf16[4,128,384]{2,1,0:T(8,128)(2,1)}, u32[]{:S(2)}, u32[]{:S(2)}) collective-permute-start(bf16[4,128,384]{2,1,0:T(8,128)(2,1)} %collective-permute-done.27.refs_1_), channel_id=1, source_target_pairs={{4,0},{0,4},{12,8},{8,12},{20,16},{16,20},{28,24},{24,28},{36,32},... | collective-permute-start | bytes 1179656 | tf_op jit(solution)/shard_map/ppermute | solution.py:26
  268.8 26.5 %collective-permute-start.32 = (bf16[4,128,384]{2,1,0:T(8,128)(2,1)}, bf16[4,128,384]{2,1,0:T(8,128)(2,1)}, u32[]{:S(2)}, u32[]{:S(2)}) collective-permute-start(bf16[4,128,384]{2,1,0:T(8,128)(2,1)} %collective-permute-done.28.refs_2_), channel_id=1, source_target_pairs={{4,0},{0,4},{12,8},{8,12},{20,16},{16,20},{28,24},{24,28},{36,32},... | collective-permute-start | bytes 1179656 | tf_op jit(solution)/shard_map/ppermute | solution.py:26
  269.2 26.1 %collective-permute-start.33 = (bf16[4,128,384]{2,1,0:T(8,128)(2,1)}, bf16[4,128,384]{2,1,0:T(8,128)(2,1)}, u32[]{:S(2)}, u32[]{:S(2)}) collective-permute-start(bf16[4,128,384]{2,1,0:T(8,128)(2,1)} %collective-permute-done.29.refs_3_), channel_id=1, source_target_pairs={{4,0},{0,4},{12,8},{8,12},{20,16},{16,20},{28,24},{24,28},{36,32},... | collective-permute-start | bytes 1179656 | tf_op jit(solution)/shard_map/ppermute | solution.py:26
  (23 other events, 478.9 us)

commit v2 on v0

v2 whole, which is shorter than its diff:
```python
import functools

import jax
import jax.numpy as jnp
from jax import lax
from jax.experimental import pallas as pl
from jax.experimental.pallas import tpu as pltpu
from jax.sharding import PartitionSpec as P

BLK = 128
BF = jnp.bfloat16
F32 = jnp.float32
BANDS = 8
VMEM_LIMIT = 12 * 1024 * 1024


def flat(z, x, c):
    return (z % 4) * 8 + (x % 4) * 2 + c


def receive(value, source):
    pairs = []
    for z in range(4):
        for x in range(4):
            for c in range(2):
                pairs.append((flat(*source(z, x, c)), flat(z, x, c)))
    return lax.ppermute(value, "wide", pairs)


def from_sibling(value):
    return receive(value, lambda z, x, c: (z, x, 1 - c))


def tie(*values):
    return lax.optimization_barrier(values)


STEPS = (1, -1, 2)
REL = (0, 1, -1, 2)


def along(step, first):
    def source(z, x, c):
        return (z, x + step, c) if (c == 0) == first else (z + step, x, c)

    return source


VMEM = pl.BlockSpec(memory_space=pltpu.VMEM)
SMEM = pl.BlockSpec(memory_space=pltpu.SMEM)


HBM = pl.BlockSpec(memory_space=pltpu.HBM)


def call(kernel, out_shape, flops, nbytes, *operands, smem=0, hbm=(), scratch=()):
    specs = [SMEM if i < smem else HBM if i in hbm else VMEM for i in range(len(operands))]
    operands = [
        pltpu.with_memory_space_constraint(operand, pltpu.HBM) if i in hbm else operand
        for i, operand in enumerate(operands)
    ]
    return pl.pallas_call(
        kernel,
        in_specs=specs,
        out_specs=jax.tree.map(lambda _: VMEM, out_shape),
        out_shape=out_shape,
        scratch_shapes=scratch,
        compiler_params=pltpu.CompilerParams(vmem_limit_bytes=VMEM_LIMIT),
        cost_estimate=pl.CostEstimate(flops=flops, bytes_accessed=nbytes, transcendentals=0),
    )(*operands)


def shape(dims, dtype):
    return jax.ShapeDtypeStruct(dims, dtype)


def load_kernel(count, sources, *refs):
    targets, sems = refs[:count], refs[count]
    copies = []
    for k in range(count):
        band = sources[k].shape[0] // BANDS
        for i in range(BANDS):
            rows = pl.ds(i * band, band)
            copies.append(
                pltpu.make_async_copy(sources[k].at[rows], targets[k].at[rows], sems.at[k, i])
            )
    for copy in copies:
        copy.start()
    for copy in copies:
        copy.wait()


def load(*arrays):
    count = len(arrays)

    def kernel(*refs):
        load_kernel(count, refs[:count], *refs[count:])

    return call(
        kernel,
        [shape(a.shape, a.dtype) for a in arrays],
        0,
        sum(2 * a.size for a in arrays),
        *arrays,
        hbm=range(count),
        scratch=[pltpu.SemaphoreType.DMA((count, BANDS))],
    )


def place():
    rank = lax.axis_index("wide")
    return rank // 8, rank // 2 % 4, rank % 2


def part_sum(chips, inv_ref, own_ref, sib_ref, total):
    depth = 2 * inv_ref.shape[0]
    z, x, _ = place()
    for i, (dz, dx) in enumerate(chips):
        rows = slice(i * depth, (i + 1) * depth)
        block = jnp.concatenate([own_ref[rows], sib_ref[rows]], axis=1)
        at = ((z + dz) % 2 * 4 + (x + dx) % 4) * depth
        columns = pl.ds(pl.multiple_of(at, BLK), depth)
        part = jnp.dot(inv_ref[:, columns], block, preferred_element_type=F32)
        total = part if total is None else total + part
    return total


def child_part(chips, inverse, own, sib, *acc):
    rows, columns = inverse.shape[0], 2 * own.shape[1]

    def kernel(inv_ref, own_ref, sib_ref, *refs):
        acc = refs[0][...] if len(refs) > 1 else None
        refs[-1][...] = part_sum(chips, inv_ref, own_ref, sib_ref, acc)

    return call(
        kernel,
        shape((rows, columns), F32),
        2 * rows * own.shape[0] * columns,
        2 * rows * own.shape[0],
        inverse,
        own,
        sib,
        *acc,
    )


def child_last_kernel(
    chips, blocks_ref, inv_ref, own_ref, sib_ref, acc_ref, coupling_ref, out_ref, keep_ref, give_ref
):
    total = part_sum(chips, inv_ref, own_ref, sib_ref, acc_ref[...])
    half = own_ref.shape[1]
    z, x, core = place()
    row = lax.broadcasted_iota(jnp.int32, total.shape, 0)
    first = (z % 2 * 8 + x * 2 + core) * total.shape[0]
    limit = BLK * blocks_ref[z // 2] - first
    total = jnp.where(row < limit, total, 0.0)

    @pl.when(core == 0)
    def _():
        out_ref[...] = total

    @pl.when(core == 1)
    def _():
        out_ref[:, :half] = total[:, half:]
        out_ref[:, half:] = total[:, :half]

    solved = total.T.astype(BF)
    pieces, _, width = keep_ref.shape
    for i in range(pieces):
        update = jnp.dot(
            solved, coupling_ref[:, i * width : (i + 1) * width], preferred_element_type=F32
        )
        keep_ref[i] = update[:half]
        give_ref[i] = update[half:].astype(BF)


def child_last(chips, blocks, inverse, own, sib, acc, coupling, pieces):
    rows, columns = acc.shape
    half, width = columns // 2, coupling.shape[1] // pieces
    return call(
        functools.partial(child_last_kernel, chips),
        [
            shape((rows, columns), F32),
            shape((pieces, half, width), F32),
            shape((pieces, half, width), BF),
        ],
        2 * columns * rows * (own.shape[0] + coupling.shape[1]),
        2 * rows * (own.shape[0] + coupling.shape[1]),
        blocks,
        inverse,
        own,
        sib,
        acc,
        coupling,
        smem=1,
    )


def pack_kernel(x2_ref, zm_ref, zp_ref, group_ref, a_ref, b_ref, c_ref):
    rows = x2_ref.shape[0]
    third = rows // 3
    group_ref[:rows] = x2_ref[...]
    group_ref[rows : 2 * rows] = zm_ref[...]
    group_ref[2 * rows :] = zp_ref[...]
    a_ref[...] = zp_ref[:third]
    b_ref[...] = zm_ref[third : 2 * third]
    c_ref[...] = x2_ref[2 * third :]


def pack(x2, zm, zp):
    rows, half = x2.shape
    return call(
        pack_kernel,
        [shape((3 * rows, half), BF)] + [shape((rows // 3, half), BF)] * 3,
        0,
        16 * rows * half,
        x2,
        zm,
        zp,
    )


def reduce_kernel(pieces_ref, out_ref):
    total = pieces_ref[0].astype(F32)
    for i in range(1, pieces_ref.shape[0]):
        total += pieces_ref[i].astype(F32)
    out_ref[...] = total.T.astype(BF)


def reduce_pieces(pieces):
    count, half, width = pieces.shape
    return call(reduce_kernel, shape((width, half), BF), 0, 4 * count * half * width, pieces)


def chip_at(i, j, core):
    z, x, _ = place()
    dx = jnp.where(core == 0, REL[i], REL[j])
    dz = jnp.where(core == 0, REL[j], REL[i])
    return (z + dz + 4) % 4, (x + dx + 4) % 4


def base_kernel(blocks_ref, p_ref, *refs):
    r_refs, (out_ref, picked_ref) = refs[:-2], refs[-2:]
    rows = p_ref.shape[0]
    core = place()[2]
    total = None
    for k, r_ref in enumerate(r_refs):
        owner = core if k < 4 else 1 - core
        for i in range(4):
            z, x = chip_at(i, k % 4, owner)
            at = pl.multiple_of((z * 8 + x * 2 + owner) * rows, BLK)
            part = jnp.dot(p_ref[:, pl.ds(at, rows)], r_ref[i], preferred_element_type=F32)
            total = part if total is None else total + part
    out_ref[...] = total
    for n in range(picked_ref.shape[1] // BLK):
        z, x = chip_at(n // 3 % 4, n // 12, core)
        block = blocks_ref[z // 2, (z % 2 * 4 + x) * 3 + n % 3]
        at = pl.multiple_of(block * BLK, BLK)
        picked_ref[:, n * BLK : (n + 1) * BLK] = p_ref[:, pl.ds(at, BLK)]


def base_product(blocks, inverse, parts):
    rows, order = inverse.shape
    columns = parts[0].shape[2]
    return call(
        base_kernel,
        [shape((rows, columns), F32), shape((rows, blocks.size * BLK), inverse.dtype)],
        2 * rows * order * columns,
        2 * rows * order,
        blocks,
        inverse,
        *parts,
        smem=1,
    )


def final_kernel(base_ref, p_ref, *refs):
    own_refs, sib_refs, out_ref = refs[:4], refs[4:8], refs[8]
    width, half = own_refs[0].shape[1:]
    total = base_ref[...]
    change = None
    for j in range(4):
        for i in range(4):
            block = jnp.concatenate([own_refs[j][i], sib_refs[i][j]], axis=1)
            at = (j * 4 + i) * width
            part = jnp.dot(p_ref[:, at : at + width], block, preferred_element_type=F32)
            change = part if change is None else change + part
    core = place()[2]

    @pl.when(core == 0)
    def _():
        out_ref[...] = (total - change).T

    @pl.when(core == 1)
    def _():
        out_ref[:half] = (total[:, :half] - change[:, half:]).T
        out_ref[half:] = (total[:, half:] - change[:, :half]).T


def final_product(base, picked, own, sib):
    rows, columns = base.shape
    return call(
        final_kernel,
        shape((columns, rows), F32),
        2 * columns * picked.shape[0] * picked.shape[1],
        2 * picked.shape[0] * picked.shape[1],
        base,
        picked,
        *own,
        *sib,
    )


def gather_first(block):
    return [block] + [receive(block, along(s, True)) for s in STEPS]


def gather_second(first):
    part = jnp.stack(first)
    return [part] + [receive(part, along(s, False)) for s in STEPS]


def on_device(
    child_rhs, parent_rhs, child_inverse, coupling, parent_inverse, child_blocks, parent_block
):
    core = lax.axis_index("wide") % 2
    half = child_rhs.shape[0] // 2

    mine = child_rhs.T.astype(BF)
    keep = lax.dynamic_slice_in_dim(mine, core * half, half, axis=1)
    give = lax.dynamic_slice_in_dim(mine, (1 - core) * half, half, axis=1)
    got = from_sibling(give)
    b0 = jnp.where(
        core == 0, jnp.concatenate([keep, got], axis=0), jnp.concatenate([got, keep], axis=0)
    )
    xp = receive(b0, lambda z, x, c: (z, x + 1, c))
    xm = receive(b0, lambda z, x, c: (z, x - 1, c))
    zb = receive(b0, lambda z, x, c: (z ^ 1, x, c))
    r_first = gather_first(parent_rhs.T.astype(BF))
    (child_inverse,) = load(child_inverse)
    xp, xm, zb, child_inverse, *r_first = tie(xp, xm, zb, child_inverse, *r_first)
    g1 = jnp.concatenate([b0, xp, xm, zb], axis=0)
    g1_sib = from_sibling(g1)
    x2 = receive(xp, lambda z, x, c: (z, x + 1, c))
    zm = receive(zb, lambda z, x, c: (z, x - 1, c))
    zp = receive(xp, lambda z, x, c: (z ^ 1, x, c))
    coupling, parent_inverse = load(coupling, parent_inverse)
    r_own = gather_second(r_first)
    acc = child_part([(0, 0), (0, 1), (0, 3), (1, 0)], child_inverse, g1, g1_sib)
    x2, zm, zp, acc, coupling, parent_inverse, *r_own[1:3] = tie(
        x2, zm, zp, acc, coupling, parent_inverse, *r_own[1:3]
    )
    g2, last_a, last_b, last_c = pack(x2, zm, zp)
    z2 = jnp.concatenate(
        [
            receive(last_a, lambda z, x, c: (z, x + 1, c)),
            receive(last_b, lambda z, x, c: (z, x - 1, c)),
            receive(last_c, lambda z, x, c: (z ^ 1, x, c)),
        ],
        axis=0,
    )
    acc = child_part([(0, 2), (1, 3), (1, 1)], child_inverse, g2, from_sibling(g2), acc)
    z2, acc = tie(z2, acc)
    solution_t, keep, give = child_last(
        [(1, 2)], child_blocks, child_inverse, z2, from_sibling(z2), acc, coupling, 8
    )

    chip_sum = (keep + from_sibling(give).astype(F32)).astype(BF)
    groups = [
        [flat(2 * h + dz, xx, c) for dz in range(2) for xx in range(4)]
        for h in range(2)
        for c in range(2)
    ]
    chip_sum, r_own[3] = tie(chip_sum, r_own[3])
    pieces = lax.all_to_all(
        chip_sum, "wide", split_axis=0, concat_axis=0, axis_index_groups=groups, tiled=True
    )
    r_sib = [from_sibling(part) for part in r_own]
    base, picked = base_product(parent_block, parent_inverse, r_own + r_sib)
    update, base, picked = tie(reduce_pieces(pieces), base, picked)
    u_own = gather_second(gather_first(update))
    u_sib = [from_sibling(part) for part in u_own]
    parent_solution = final_product(base, picked, u_own, u_sib)
    return (solution_t.T, parent_solution)


def solution(mesh):
    placed = (
        P("rhs", "wide"),
        P("rhs", "wide"),
        P("wide", None),
        P("wide", None),
        P("wide", None),
        P(),
        P(),
    )
    return jax.shard_map(
        on_device,
        mesh=mesh,
        in_specs=placed,
        out_specs=(P("rhs", "wide"), P("rhs", "wide")),
        check_vma=False,
    )
```

time: 334 us -> 122 us (0.37)
  waiting for transfers between devices: 247 us -> 39.4 us
  starting transfers between devices: 7.52 us -> 38.8 us
  Pallas kernels: 0 us -> 23 us
  matrix products: 22.6 us -> 0 us
  other arithmetic: 21.1 us -> 1.63 us
  local copies, waits for them, and re-layouts: 20.5 us -> 1.16 us
  blocking collectives: 0 us -> 16.8 us
  between operations: 14.8 us -> 0.9 us
    reduce_scatter x1 -> x0, waiting for transfers between devices: 107 us -> none  [on_device(): lax.psum_scatter(placed.reshape(columns, S0), 'wide', scatter_dimension=1...]
    all_gather x1 -> x0, waiting for transfers between devices: 51.4 us -> none  [on_device(): lax.all_gather(parent_panel, 'wide', axis=1, tiled=True)]
    ppermute x4 -> x34, waiting for transfers between devices: 88.8 us -> 39.4 us  [receive(): return lax.ppermute(value, 'wide', pairs)]
    ppermute x4 -> x34, starting transfers between devices: 7.26 us -> 38.8 us  [receive(): return lax.ppermute(value, 'wide', pairs)]
    pallas_call x0 -> x9, Pallas kernels: none -> 23 us  [call(): pl.pallas_call(kernel, in_specs=specs, out_specs=jax.tree.map(lambda _: V...]
    dot_general x3 -> x0, matrix products: 22.6 us -> none  [the longest x1 11.3 us: on_device(): lax.dot_general(panel_full, child_inverse, (((1,), (1,)), ((), ())), pref...]
    all_to_all x0 -> x1, blocking collectives: none -> 16.8 us  [on_device(): lax.all_to_all(chip_sum, 'wide', split_axis=0, concat_axis=0, axis_index_...]
    scatter-add x1 -> x0, local copies, waits for them, and re-layouts: 12.6 us -> none  [on_device(): blank.at[:, targets]]
  transfers between devices with their start and end apart: 6 -> 34, of which waited for: 6 -> 14; matrix products, arithmetic and copies ran while one was open for 0% -> 1% of each run, Pallas kernels for 0% -> 9%
where the time goes in v2:
time: 122 us
  waiting for transfers between devices  39.4 us (32%)
  starting transfers between devices  38.8 us (32%)
  Pallas kernels  23 us (19%)
  blocking collectives  16.8 us (14%)
  other arithmetic  1.63 us (1%)
    ppermute x34, waiting for transfers between devices, receive(): return lax.ppermute(value, 'wide', pairs)  39.4 us
    ppermute x34, starting transfers between devices, receive(): return lax.ppermute(value, 'wide', pairs)  38.8 us
    pallas_call x9, Pallas kernels, call(): pl.pallas_call(kernel, in_specs=specs, out_specs=jax.tree.map(lambda _: V...  23 us
    all_to_all x1, blocking collectives, on_device(): lax.all_to_all(chip_sum, 'wide', split_axis=0, concat_axis=0, axis_index_...  16.8 us
  transfers between devices with their start and end apart: 34, of which 14 were waited for; matrix products, arithmetic and copies ran while one was open for 1% of the time, Pallas kernels for 9%

profile of v2, /device:TPU:1, one launch (start us, length us, event | category | flops | bytes accessed | tf_op | source)
XLA Modules:
  0.0 121.7 jit_solution(10538630191895546413)
XLA Ops:
  4.4 3.9 %collective-permute-start.4 = (bf16[384,256]{1,0:T(8,128)(2,1)S(1)}, bf16[384,256]{1,0:T(8,128)(2,1)S(1)}, u32[]{:S(2)}, u32[]{:S(2)}) collective-permute-start(bf16[384,256]{1,0:T(8,128)(2,1)S(1)} %bitcast.17), channel_id=1, source_target_pairs={{8,0},{36,4},{16,8},{44,12},{24,16},{52,20},{0,24},{60,28},{40,32}... | collective-permute-start | bytes 589832 | tf_op jit(solution)/shard_map/ppermute | solution.py:27
  8.4 2.5 %collective-permute-start.1 = (bf16[1152,128]{1,0:T(8,128)(2,1)S(1)}, bf16[1152,128]{1,0:T(8,128)(2,1)S(1)}, u32[]{:S(2)}, u32[]{:S(2)}) collective-permute-start(bf16[1152,128]{1,0:T(8,128)(2,1)S(1)} %maximum_select_fusion), channel_id=1, source_target_pairs={{8,0},{12,4},{16,8},{20,12},{24,16},{28,20},{0,24},{4,28},{40,32},... | collective-permute-start | bytes 884744 | tf_op jit(solution)/shard_map/ppermute | solution.py:27
  13.0 4.1 %shard_map.86.inv_ref = bf16[576,9216]{1,0:T(8,128)(2,1)S(1)} custom-call(bf16[576,9216]{1,0:T(8,128)(2,1)} %refs_0_.2), custom_call_target="tpu_custom_call" | custom-call | bytes 10616832 | tf_op jit(solution)/shard_map/pallas_call | solution.py:62
  17.1 2.8 %collective-permute-done.5 = bf16[384,256]{1,0:T(8,128)(2,1)S(1)} collective-permute-done((bf16[384,256]{1,0:T(8,128)(2,1)S(1)}, bf16[384,256]{1,0:T(8,128)(2,1)S(1)}, u32[]{:S(2)}, u32[]{:S(2)}) %collective-permute-start.5) | collective-permute-done | bytes 196640 | tf_op jit(solution)/shard_map/ppermute | solution.py:27
  19.9 3.8 %collective-permute-done.6 = bf16[384,256]{1,0:T(8,128)(2,1)S(1)} collective-permute-done((bf16[384,256]{1,0:T(8,128)(2,1)S(1)}, bf16[384,256]{1,0:T(8,128)(2,1)S(1)}, u32[]{:S(2)}, u32[]{:S(2)}) %collective-permute-start.6) | collective-permute-done | bytes 196640 | tf_op jit(solution)/shard_map/ppermute | solution.py:27
  24.1 2.7 %collective-permute-start.11 = (bf16[4,384,256]{2,1,0:T(8,128)(2,1)S(1)}, bf16[4,384,256]{2,1,0:T(8,128)(2,1)S(1)}, u32[]{:S(2)}, u32[]{:S(2)}) collective-permute-start(bf16[4,384,256]{2,1,0:T(8,128)(2,1)S(1)} %pad_maximum_fusion.1.refs_0_), channel_id=1, source_target_pairs={{32,0},{12,4},{40,8},{20,12},{48,16},{28,20},{56,24},{4,28},{64,32... | collective-permute-start | bytes 2359304 | tf_op jit(solution)/shard_map/ppermute | solution.py:27
  26.8 2.7 %collective-permute-start.7 = (bf16[1152,128]{1,0:T(8,128)(2,1)S(1)}, bf16[1152,128]{1,0:T(8,128)(2,1)S(1)}, u32[]{:S(2)}, u32[]{:S(2)}) collective-permute-start(bf16[1152,128]{1,0:T(8,128)(2,1)S(1)} %collective-permute-done.1), channel_id=1, source_target_pairs={{8,0},{12,4},{16,8},{20,12},{24,16},{28,20},{0,24},{4,28},{40,32},... | collective-permute-start | bytes 884744 | tf_op jit(solution)/shard_map/ppermute | solution.py:27
  29.5 4.9 %shard_map.88 = (bf16[576,3072]{1,0:T(8,128)(2,1)S(1)}, bf16[384,12288]{1,0:T(8,128)(2,1)S(1)}) custom-call(bf16[576,3072]{1,0:T(8,128)(2,1)} %refs_0_.3, bf16[384,12288]{1,0:T(8,128)(2,1)} %refs_1_.1), custom_call_target="tpu_custom_call" | custom-call | bytes 12976128 | tf_op jit(solution)/shard_map/pallas_call | solution.py:62
  34.4 1.7 %shard_map.87.refs_0_ = f32[576,256]{1,0:T(8,128)S(1)} custom-call(bf16[576,9216]{1,0:T(8,128)(2,1)S(1)} %shard_map.86.inv_ref, bf16[4608,128]{1,0:T(8,128)(2,1)S(1)} %pad_maximum_fusion.own_ref, bf16[4608,128]{1,0:T(8,128)(2,1)S(1)} %collective-permute-done.10.sib_ref), custom_call_target="tpu_custom_call" | custom-call | flops 1358954496 | bytes 5308416 | tf_op jit(solution)/shard_map/pallas_call | solution.py:62
  36.1 5.9 %collective-permute-done.7.x2_ref = bf16[1152,128]{1,0:T(8,128)(2,1)S(1)} collective-permute-done((bf16[1152,128]{1,0:T(8,128)(2,1)S(1)}, bf16[1152,128]{1,0:T(8,128)(2,1)S(1)}, u32[]{:S(2)}, u32[]{:S(2)}) %collective-permute-start.7) | collective-permute-done | bytes 294944 | tf_op jit(solution)/shard_map/ppermute | solution.py:27
  42.1 3.1 %collective-permute-done.8.zm_ref = bf16[1152,128]{1,0:T(8,128)(2,1)S(1)} collective-permute-done((bf16[1152,128]{1,0:T(8,128)(2,1)S(1)}, bf16[1152,128]{1,0:T(8,128)(2,1)S(1)}, u32[]{:S(2)}, u32[]{:S(2)}) %collective-permute-start.8) | collective-permute-done | bytes 294944 | tf_op jit(solution)/shard_map/ppermute | solution.py:27
  47.6 1.8 %collective-permute-done.13 = bf16[384,128]{1,0:T(8,128)(2,1)S(1)} collective-permute-done((bf16[384,128]{1,0:T(8,128)(2,1)S(1)}, bf16[384,128]{1,0:T(8,128)(2,1)S(1)}, u32[]{:S(2)}, u32[]{:S(2)}) %collective-permute-start.13) | collective-permute-done | bytes 98336 | tf_op jit(solution)/shard_map/ppermute | solution.py:27
  55.2 3.6 %shard_map.91 = (f32[576,256]{1,0:T(8,128)}, f32[8,128,384]{2,1,0:T(8,128)S(1)}, bf16[8,128,384]{2,1,0:T(8,128)(2,1)S(1)}) custom-call(s32[2]{0:T(128)S(1)} %copy-done.1, bf16[576,9216]{1,0:T(8,128)(2,1)S(1)} %shard_map.86.inv_ref, bf16[1152,128]{1,0:T(8,128)(2,1)S(1)} %pad_maximum_fusion.3.own_ref, bf16[1152,128]{1,0:T(8,128)(2,1)S(1)} %collective-permute-done.17.sib_ref, ...), custom_call_target="tpu_custom_call" | custom-call | flops 1245708288 | bytes 4866048 | tf_op jit(solution)/shard_map/pallas_call | solution.py:62
  59.3 2.0 %collective-permute-start.20 = (bf16[4,384,256]{2,1,0:T(8,128)(2,1)S(1)}, bf16[4,384,256]{2,1,0:T(8,128)(2,1)S(1)}, u32[]{:S(2)}, u32[]{:S(2)}) collective-permute-start(bf16[4,384,256]{2,1,0:T(8,128)(2,1)S(1)} %pad_maximum_fusion.1.refs_0_), channel_id=1, source_target_pairs={{4,0},{0,4},{12,8},{8,12},{20,16},{16,20},{28,24},{24,28},{36,32},... | collective-permute-start | bytes 2359304 | tf_op jit(solution)/shard_map/ppermute | solution.py:27
  61.9 10.0 %collective-permute-done.19.refs_3_ = bf16[4,384,256]{2,1,0:T(8,128)(2,1)S(1)} collective-permute-done((bf16[4,384,256]{2,1,0:T(8,128)(2,1)S(1)}, bf16[4,384,256]{2,1,0:T(8,128)(2,1)S(1)}, u32[]{:S(2)}, u32[]{:S(2)}) %collective-permute-start.19) | collective-permute-done | bytes 786464 | tf_op jit(solution)/shard_map/ppermute | solution.py:27
  73.0 16.8 %all_to_all.5.pieces_ref = bf16[8,128,384]{2,1,0:T(8,128)(2,1)S(1)} all-to-all(bf16[8,128,384]{2,1,0:T(8,128)(2,1)S(1)} %add_convert_fusion), channel_id=1, replica_groups={{0,8,16,24,32,40,48,56},{4,12,20,28,36,44,52,60},{64,72,80,88,96,104,11..., dimensions={0} | all-to-all | bytes 1572864 | tf_op jit(solution)/shard_map/all_to_all | solution.py:375
  90.0 4.4 %shard_map.93 = (f32[384,256]{1,0:T(8,128)S(1)}, bf16[384,6144]{1,0:T(8,128)(2,1)S(1)}) custom-call(s32[2,24]{1,0:T(2,128)S(1)} %copy-done, bf16[384,12288]{1,0:T(8,128)(2,1)S(1)} %get-tuple-element.61.p_ref, bf16[4,384,256]{2,1,0:T(8,128)(2,1)S(1)} %pad_maximum_fusion.1.refs_0_, bf16[4,384,256]{2,1,0:T(8,128)(2,1)S(1)} %collective-permute-done.11.refs_1_, ...), custom_call_target="tpu_custom_call" | custom-call | flops 2415919104 | bytes 9437184 | tf_op jit(solution)/shard_map/pallas_call | solution.py:62
  96.1 1.8 %collective-permute-start.24 = (bf16[384,128]{1,0:T(8,128)(2,1)S(1)}, bf16[384,128]{1,0:T(8,128)(2,1)S(1)}, u32[]{:S(2)}, u32[]{:S(2)}) collective-permute-start(bf16[384,128]{1,0:T(8,128)(2,1)S(1)} %shard_map.92), channel_id=1, source_target_pairs={{8,0},{36,4},{16,8},{44,12},{24,16},{52,20},{0,24},{60,28},{40,32}... | collective-permute-start | bytes 294920 | tf_op jit(solution)/shard_map/ppermute | solution.py:27
  97.9 2.5 %collective-permute-done.25 = bf16[384,128]{1,0:T(8,128)(2,1)S(1)} collective-permute-done((bf16[384,128]{1,0:T(8,128)(2,1)S(1)}, bf16[384,128]{1,0:T(8,128)(2,1)S(1)}, u32[]{:S(2)}, u32[]{:S(2)}) %collective-permute-start.25) | collective-permute-done | bytes 98336 | tf_op jit(solution)/shard_map/ppermute | solution.py:27
  103.0 3.8 %collective-permute-start.30 = (bf16[4,384,128]{2,1,0:T(8,128)(2,1)S(1)}, bf16[4,384,128]{2,1,0:T(8,128)(2,1)S(1)}, u32[]{:S(2)}, u32[]{:S(2)}) collective-permute-start(bf16[4,384,128]{2,1,0:T(8,128)(2,1)S(1)} %pad_maximum_fusion.2.refs_0_), channel_id=1, source_target_pairs={{4,0},{0,4},{12,8},{8,12},{20,16},{16,20},{28,24},{24,28},{36,32},... | collective-permute-start | bytes 1179656 | tf_op jit(solution)/shard_map/ppermute | solution.py:27
  108.1 2.8 %collective-permute-start.31 = (bf16[4,384,128]{2,1,0:T(8,128)(2,1)S(1)}, bf16[4,384,128]{2,1,0:T(8,128)(2,1)S(1)}, u32[]{:S(2)}, u32[]{:S(2)}) collective-permute-start(bf16[4,384,128]{2,1,0:T(8,128)(2,1)S(1)} %collective-permute-done.27.refs_1_), channel_id=1, source_target_pairs={{4,0},{0,4},{12,8},{8,12},{20,16},{16,20},{28,24},{24,28},{36,32},... | collective-permute-start | bytes 1179656 | tf_op jit(solution)/shard_map/ppermute | solution.py:27
  110.9 2.7 %collective-permute-done.28.refs_2_ = bf16[4,384,128]{2,1,0:T(8,128)(2,1)S(1)} collective-permute-done((bf16[4,384,128]{2,1,0:T(8,128)(2,1)S(1)}, bf16[4,384,128]{2,1,0:T(8,128)(2,1)S(1)}, u32[]{:S(2)}, u32[]{:S(2)}) %collective-permute-start.28) | collective-permute-done | bytes 393248 | tf_op jit(solution)/shard_map/ppermute | solution.py:27
  113.6 3.4 %collective-permute-start.32 = (bf16[4,384,128]{2,1,0:T(8,128)(2,1)S(1)}, bf16[4,384,128]{2,1,0:T(8,128)(2,1)S(1)}, u32[]{:S(2)}, u32[]{:S(2)}) collective-permute-start(bf16[4,384,128]{2,1,0:T(8,128)(2,1)S(1)} %collective-permute-done.28.refs_2_), channel_id=1, source_target_pairs={{4,0},{0,4},{12,8},{8,12},{20,16},{16,20},{28,24},{24,28},{36,32},... | collective-permute-start | bytes 1179656 | tf_op jit(solution)/shard_map/ppermute | solution.py:27
  119.0 2.7 %shard_map.94 = f32[256,384]{1,0:T(8,128)} custom-call(f32[384,256]{1,0:T(8,128)S(1)} %get-tuple-element.67.base_ref, bf16[384,6144]{1,0:T(8,128)(2,1)S(1)} %get-tuple-element.68.p_ref, bf16[4,384,128]{2,1,0:T(8,128)(2,1)S(1)} %pad_maximum_fusion.2.refs_0_, bf16[4,384,128]{2,1,0:T(8,128)(2,1)S(1)} %collective-permute-done.27.refs_1_, ...), custom_call_target="tpu_custom_call" | custom-call | flops 1207959552 | bytes 4718592 | tf_op jit(solution)/shard_map/pallas_call | solution.py:62
  (67 shorter events, 24.1 us)
Async XLA Ops:
  1.8 6.5 %collective-permute-start = (bf16[576,128]{1,0:T(8,128)(2,1)S(1)}, bf16[576,128]{1,0:T(8,128)(2,1)S(1)}, u32[]{:S(2)}, u32[]{:S(2)}) collective-permute-start(bf16[576,128]{1,0:T(8,128)(2,1)S(1)} %get-tuple-element.71), channel_id=1, source_target_pairs={{4,0},{0,4},{12,8},{8,12},{20,16},{16,20},{28,24},{24,28},{36,32},... | collective-permute-start | bytes 442376 | tf_op jit(solution)/shard_map/ppermute | solution.py:27
  4.4 8.0 %collective-permute-start.4 = (bf16[384,256]{1,0:T(8,128)(2,1)S(1)}, bf16[384,256]{1,0:T(8,128)(2,1)S(1)}, u32[]{:S(2)}, u32[]{:S(2)}) collective-permute-start(bf16[384,256]{1,0:T(8,128)(2,1)S(1)} %bitcast.17), channel_id=1, source_target_pairs={{8,0},{36,4},{16,8},{44,12},{24,16},{52,20},{0,24},{60,28},{40,32}... | collective-permute-start | bytes 589832 | tf_op jit(solution)/shard_map/ppermute | solution.py:27
  8.4 15.3 %collective-permute-start.1 = (bf16[1152,128]{1,0:T(8,128)(2,1)S(1)}, bf16[1152,128]{1,0:T(8,128)(2,1)S(1)}, u32[]{:S(2)}, u32[]{:S(2)}) collective-permute-start(bf16[1152,128]{1,0:T(8,128)(2,1)S(1)} %maximum_select_fusion), channel_id=1, source_target_pairs={{8,0},{12,4},{16,8},{20,12},{24,16},{28,20},{0,24},{4,28},{40,32},... | collective-permute-start | bytes 884744 | tf_op jit(solution)/shard_map/ppermute | solution.py:27
  11.0 12.8 %collective-permute-start.2 = (bf16[1152,128]{1,0:T(8,128)(2,1)S(1)}, bf16[1152,128]{1,0:T(8,128)(2,1)S(1)}, u32[]{:S(2)}, u32[]{:S(2)}) collective-permute-start(bf16[1152,128]{1,0:T(8,128)(2,1)S(1)} %maximum_select_fusion), channel_id=1, source_target_pairs={{24,0},{28,4},{0,8},{4,12},{8,16},{12,20},{16,24},{20,28},{56,32},... | collective-permute-start | bytes 884744 | tf_op jit(solution)/shard_map/ppermute | solution.py:27
  11.0 12.8 %collective-permute-start.3 = (bf16[1152,128]{1,0:T(8,128)(2,1)S(1)}, bf16[1152,128]{1,0:T(8,128)(2,1)S(1)}, u32[]{:S(2)}, u32[]{:S(2)}) collective-permute-start(bf16[1152,128]{1,0:T(8,128)(2,1)S(1)} %maximum_select_fusion), channel_id=1, source_target_pairs={{32,0},{36,4},{40,8},{44,12},{48,16},{52,20},{56,24},{60,28},{0,32... | collective-permute-start | bytes 884744 | tf_op jit(solution)/shard_map/ppermute | solution.py:27
  11.0 8.9 %collective-permute-start.5 = (bf16[384,256]{1,0:T(8,128)(2,1)S(1)}, bf16[384,256]{1,0:T(8,128)(2,1)S(1)}, u32[]{:S(2)}, u32[]{:S(2)}) collective-permute-start(bf16[384,256]{1,0:T(8,128)(2,1)S(1)} %bitcast.18), channel_id=1, source_target_pairs={{24,0},{100,4},{0,8},{108,12},{8,16},{116,20},{16,24},{124,28},{56... | collective-permute-start | bytes 589832 | tf_op jit(solution)/shard_map/ppermute | solution.py:27
  12.5 11.3 %collective-permute-start.6 = (bf16[384,256]{1,0:T(8,128)(2,1)S(1)}, bf16[384,256]{1,0:T(8,128)(2,1)S(1)}, u32[]{:S(2)}, u32[]{:S(2)}) collective-permute-start(bf16[384,256]{1,0:T(8,128)(2,1)S(1)} %bitcast.19), channel_id=1, source_target_pairs={{16,0},{68,4},{24,8},{76,12},{0,16},{84,20},{8,24},{92,28},{48,32}... | collective-permute-start | bytes 589832 | tf_op jit(solution)/shard_map/ppermute | solution.py:27
  24.1 21.1 %collective-permute-start.11 = (bf16[4,384,256]{2,1,0:T(8,128)(2,1)S(1)}, bf16[4,384,256]{2,1,0:T(8,128)(2,1)S(1)}, u32[]{:S(2)}, u32[]{:S(2)}) collective-permute-start(bf16[4,384,256]{2,1,0:T(8,128)(2,1)S(1)} %pad_maximum_fusion.1.refs_0_), channel_id=1, source_target_pairs={{32,0},{12,4},{40,8},{20,12},{48,16},{28,20},{56,24},{4,28},{64,32... | collective-permute-start | bytes 2359304 | tf_op jit(solution)/shard_map/ppermute | solution.py:27
  26.8 18.4 %collective-permute-start.12 = (bf16[4,384,256]{2,1,0:T(8,128)(2,1)S(1)}, bf16[4,384,256]{2,1,0:T(8,128)(2,1)S(1)}, u32[]{:S(2)}, u32[]{:S(2)}) collective-permute-start(bf16[4,384,256]{2,1,0:T(8,128)(2,1)S(1)} %pad_maximum_fusion.1.refs_0_), channel_id=1, source_target_pairs={{96,0},{28,4},{104,8},{4,12},{112,16},{12,20},{120,24},{20,28},{0,... | collective-permute-start | bytes 2359304 | tf_op jit(solution)/shard_map/ppermute | solution.py:27
  26.8 15.3 %collective-permute-start.7 = (bf16[1152,128]{1,0:T(8,128)(2,1)S(1)}, bf16[1152,128]{1,0:T(8,128)(2,1)S(1)}, u32[]{:S(2)}, u32[]{:S(2)}) collective-permute-start(bf16[1152,128]{1,0:T(8,128)(2,1)S(1)} %collective-permute-done.1), channel_id=1, source_target_pairs={{8,0},{12,4},{16,8},{20,12},{24,16},{28,20},{0,24},{4,28},{40,32},... | collective-permute-start | bytes 884744 | tf_op jit(solution)/shard_map/ppermute | solution.py:27
  29.5 15.7 %collective-permute-start.8 = (bf16[1152,128]{1,0:T(8,128)(2,1)S(1)}, bf16[1152,128]{1,0:T(8,128)(2,1)S(1)}, u32[]{:S(2)}, u32[]{:S(2)}) collective-permute-start(bf16[1152,128]{1,0:T(8,128)(2,1)S(1)} %collective-permute-done.3), channel_id=1, source_target_pairs={{24,0},{28,4},{0,8},{4,12},{8,16},{12,20},{16,24},{20,28},{56,32},... | collective-permute-start | bytes 884744 | tf_op jit(solution)/shard_map/ppermute | solution.py:27
  29.5 15.7 %collective-permute-start.9 = (bf16[1152,128]{1,0:T(8,128)(2,1)S(1)}, bf16[1152,128]{1,0:T(8,128)(2,1)S(1)}, u32[]{:S(2)}, u32[]{:S(2)}) collective-permute-start(bf16[1152,128]{1,0:T(8,128)(2,1)S(1)} %collective-permute-done.1), channel_id=1, source_target_pairs={{32,0},{36,4},{40,8},{44,12},{48,16},{52,20},{56,24},{60,28},{0,32... | collective-permute-start | bytes 884744 | tf_op jit(solution)/shard_map/ppermute | solution.py:27
  45.3 5.8 %collective-permute-start.16 = (bf16[3456,128]{1,0:T(8,128)(2,1)S(1)}, bf16[3456,128]{1,0:T(8,128)(2,1)S(1)}, u32[]{:S(2)}, u32[]{:S(2)}) collective-permute-start(bf16[3456,128]{1,0:T(8,128)(2,1)S(1)} %get-tuple-element.52.own_ref), channel_id=1, source_target_pairs={{4,0},{0,4},{12,8},{8,12},{20,16},{16,20},{28,24},{24,28},{36,32},... | collective-permute-start | bytes 2654216 | tf_op jit(solution)/shard_map/ppermute | solution.py:27
  59.3 12.6 %collective-permute-start.19 = (bf16[4,384,256]{2,1,0:T(8,128)(2,1)S(1)}, bf16[4,384,256]{2,1,0:T(8,128)(2,1)S(1)}, u32[]{:S(2)}, u32[]{:S(2)}) collective-permute-start(bf16[4,384,256]{2,1,0:T(8,128)(2,1)S(1)} %pad_maximum_fusion.1.refs_0_), channel_id=1, source_target_pairs={{64,0},{20,4},{72,8},{28,12},{80,16},{4,20},{88,24},{12,28},{96,32... | collective-permute-start | bytes 2359304 | tf_op jit(solution)/shard_map/ppermute | solution.py:27
  59.3 30.7 %collective-permute-start.20 = (bf16[4,384,256]{2,1,0:T(8,128)(2,1)S(1)}, bf16[4,384,256]{2,1,0:T(8,128)(2,1)S(1)}, u32[]{:S(2)}, u32[]{:S(2)}) collective-permute-start(bf16[4,384,256]{2,1,0:T(8,128)(2,1)S(1)} %pad_maximum_fusion.1.refs_0_), channel_id=1, source_target_pairs={{4,0},{0,4},{12,8},{8,12},{20,16},{16,20},{28,24},{24,28},{36,32},... | collective-permute-start | bytes 2359304 | tf_op jit(solution)/shard_map/ppermute | solution.py:27
  61.2 28.8 %collective-permute-start.21 = (bf16[4,384,256]{2,1,0:T(8,128)(2,1)S(1)}, bf16[4,384,256]{2,1,0:T(8,128)(2,1)S(1)}, u32[]{:S(2)}, u32[]{:S(2)}) collective-permute-start(bf16[4,384,256]{2,1,0:T(8,128)(2,1)S(1)} %collective-permute-done.11.refs_1_), channel_id=1, source_target_pairs={{4,0},{0,4},{12,8},{8,12},{20,16},{16,20},{28,24},{24,28},{36,32},... | collective-permute-start | bytes 2359304 | tf_op jit(solution)/shard_map/ppermute | solution.py:27
  61.2 28.8 %collective-permute-start.22 = (bf16[4,384,256]{2,1,0:T(8,128)(2,1)S(1)}, bf16[4,384,256]{2,1,0:T(8,128)(2,1)S(1)}, u32[]{:S(2)}, u32[]{:S(2)}) collective-permute-start(bf16[4,384,256]{2,1,0:T(8,128)(2,1)S(1)} %collective-permute-done.12.refs_2_), channel_id=1, source_target_pairs={{4,0},{0,4},{12,8},{8,12},{20,16},{16,20},{28,24},{24,28},{36,32},... | collective-permute-start | bytes 2359304 | tf_op jit(solution)/shard_map/ppermute | solution.py:27
  71.9 18.1 %collective-permute-start.23 = (bf16[4,384,256]{2,1,0:T(8,128)(2,1)S(1)}, bf16[4,384,256]{2,1,0:T(8,128)(2,1)S(1)}, u32[]{:S(2)}, u32[]{:S(2)}) collective-permute-start(bf16[4,384,256]{2,1,0:T(8,128)(2,1)S(1)} %collective-permute-done.19.refs_3_), channel_id=1, source_target_pairs={{4,0},{0,4},{12,8},{8,12},{20,16},{16,20},{28,24},{24,28},{36,32},... | collective-permute-start | bytes 2359304 | tf_op jit(solution)/shard_map/ppermute | solution.py:27
  94.4 6.1 %collective-permute-start.25 = (bf16[384,128]{1,0:T(8,128)(2,1)S(1)}, bf16[384,128]{1,0:T(8,128)(2,1)S(1)}, u32[]{:S(2)}, u32[]{:S(2)}) collective-permute-start(bf16[384,128]{1,0:T(8,128)(2,1)S(1)} %shard_map.92), channel_id=1, source_target_pairs={{24,0},{100,4},{0,8},{108,12},{8,16},{116,20},{16,24},{124,28},{56... | collective-permute-start | bytes 294920 | tf_op jit(solution)/shard_map/ppermute | solution.py:27
  101.1 7.0 %collective-permute-start.27 = (bf16[4,384,128]{2,1,0:T(8,128)(2,1)S(1)}, bf16[4,384,128]{2,1,0:T(8,128)(2,1)S(1)}, u32[]{:S(2)}, u32[]{:S(2)}) collective-permute-start(bf16[4,384,128]{2,1,0:T(8,128)(2,1)S(1)} %pad_maximum_fusion.2.refs_0_), channel_id=1, source_target_pairs={{32,0},{12,4},{40,8},{20,12},{48,16},{28,20},{56,24},{4,28},{64,32... | collective-permute-start | bytes 1179656 | tf_op jit(solution)/shard_map/ppermute | solution.py:27
  101.2 12.4 %collective-permute-start.28 = (bf16[4,384,128]{2,1,0:T(8,128)(2,1)S(1)}, bf16[4,384,128]{2,1,0:T(8,128)(2,1)S(1)}, u32[]{:S(2)}, u32[]{:S(2)}) collective-permute-start(bf16[4,384,128]{2,1,0:T(8,128)(2,1)S(1)} %pad_maximum_fusion.2.refs_0_), channel_id=1, source_target_pairs={{96,0},{28,4},{104,8},{4,12},{112,16},{12,20},{120,24},{20,28},{0,... | collective-permute-start | bytes 1179656 | tf_op jit(solution)/shard_map/ppermute | solution.py:27
  102.6 14.4 %collective-permute-start.29 = (bf16[4,384,128]{2,1,0:T(8,128)(2,1)S(1)}, bf16[4,384,128]{2,1,0:T(8,128)(2,1)S(1)}, u32[]{:S(2)}, u32[]{:S(2)}) collective-permute-start(bf16[4,384,128]{2,1,0:T(8,128)(2,1)S(1)} %pad_maximum_fusion.2.refs_0_), channel_id=1, source_target_pairs={{64,0},{20,4},{72,8},{28,12},{80,16},{4,20},{88,24},{12,28},{96,32... | collective-permute-start | bytes 1179656 | tf_op jit(solution)/shard_map/ppermute | solution.py:27
  103.0 14.1 %collective-permute-start.30 = (bf16[4,384,128]{2,1,0:T(8,128)(2,1)S(1)}, bf16[4,384,128]{2,1,0:T(8,128)(2,1)S(1)}, u32[]{:S(2)}, u32[]{:S(2)}) collective-permute-start(bf16[4,384,128]{2,1,0:T(8,128)(2,1)S(1)} %pad_maximum_fusion.2.refs_0_), channel_id=1, source_target_pairs={{4,0},{0,4},{12,8},{8,12},{20,16},{16,20},{28,24},{24,28},{36,32},... | collective-permute-start | bytes 1179656 | tf_op jit(solution)/shard_map/ppermute | solution.py:27
  108.1 9.0 %collective-permute-start.31 = (bf16[4,384,128]{2,1,0:T(8,128)(2,1)S(1)}, bf16[4,384,128]{2,1,0:T(8,128)(2,1)S(1)}, u32[]{:S(2)}, u32[]{:S(2)}) collective-permute-start(bf16[4,384,128]{2,1,0:T(8,128)(2,1)S(1)} %collective-permute-done.27.refs_1_), channel_id=1, source_target_pairs={{4,0},{0,4},{12,8},{8,12},{20,16},{16,20},{28,24},{24,28},{36,32},... | collective-permute-start | bytes 1179656 | tf_op jit(solution)/shard_map/ppermute | solution.py:27
  (12 other events, 74.5 us)

commit v3 on v2

v3 whole, which is shorter than its diff:
```python
import functools

import jax
import jax.numpy as jnp
from jax import lax
from jax.experimental import pallas as pl
from jax.experimental.pallas import tpu as pltpu
from jax.sharding import PartitionSpec as P

BLK = 128
BF = jnp.bfloat16
F32 = jnp.float32
BANDS = 8
VMEM_LIMIT = 8 * 1024 * 1024


def flat(z, x, c):
    return (z % 4) * 8 + (x % 4) * 2 + c


def receive(value, source):
    pairs = []
    for z in range(4):
        for x in range(4):
            for c in range(2):
                pairs.append((flat(*source(z, x, c)), flat(z, x, c)))
    return lax.ppermute(value, "wide", pairs)


def from_sibling(value):
    return receive(value, lambda z, x, c: (z, x, 1 - c))


def tie(*values):
    return lax.optimization_barrier(values)


STEPS = (1, -1, 2)
REL = (0, 1, -1, 2)


def along(step, first):
    def source(z, x, c):
        return (z, x + step, c) if (c == 0) == first else (z + step, x, c)

    return source


VMEM = pl.BlockSpec(memory_space=pltpu.VMEM)
SMEM = pl.BlockSpec(memory_space=pltpu.SMEM)


HBM = pl.BlockSpec(memory_space=pltpu.HBM)


def call(kernel, out_shape, *operands, smem=0, hbm=(), scratch=()):
    specs = [SMEM if i < smem else HBM if i in hbm else VMEM for i in range(len(operands))]
    operands = [
        pltpu.with_memory_space_constraint(operand, pltpu.HBM) if i in hbm else operand
        for i, operand in enumerate(operands)
    ]
    return pl.pallas_call(
        kernel,
        in_specs=specs,
        out_specs=jax.tree.map(lambda _: VMEM, out_shape),
        out_shape=out_shape,
        scratch_shapes=scratch,
        compiler_params=pltpu.CompilerParams(vmem_limit_bytes=VMEM_LIMIT),
        cost_estimate=pl.CostEstimate(flops=0, bytes_accessed=0, transcendentals=0),
    )(*operands)


def shape(dims, dtype):
    return jax.ShapeDtypeStruct(dims, dtype)


def load_kernel(count, sources, *refs):
    targets, sems = refs[:count], refs[count]
    copies = []
    for k in range(count):
        band = sources[k].shape[0] // BANDS
        for i in range(BANDS):
            rows = pl.ds(i * band, band)
            copies.append(
                pltpu.make_async_copy(sources[k].at[rows], targets[k].at[rows], sems.at[k, i])
            )
    for copy in copies:
        copy.start()
    for copy in copies:
        copy.wait()


def load(*arrays):
    count = len(arrays)

    def kernel(*refs):
        load_kernel(count, refs[:count], *refs[count:])

    return call(
        kernel,
        [shape(a.shape, a.dtype) for a in arrays],
        *arrays,
        hbm=range(count),
        scratch=[pltpu.SemaphoreType.DMA((count, BANDS))],
    )


def place():
    rank = lax.axis_index("wide")
    return rank // 8, rank // 2 % 4, rank % 2


def part_sum(chips, inv_ref, block_refs, held_ref, total):
    rows = inv_ref.shape[0]
    z, x, core = place()
    mine = pl.ds(pl.multiple_of(core * rows, 16), rows)
    others = pl.ds(pl.multiple_of((1 - core) * rows, 16), rows)
    for i, (dz, dx) in enumerate(chips):
        held_ref[i, mine] = block_refs[i][...]
        held_ref[i, others] = block_refs[len(chips) + i][...]
        at = ((z + dz) % 2 * 4 + (x + dx) % 4) * 2 * rows
        columns = pl.ds(pl.multiple_of(at, BLK), 2 * rows)
        part = jnp.dot(inv_ref[:, columns], held_ref[i], preferred_element_type=F32)
        total = part if total is None else total + part
    return total


def held_scratch(chips, inverse, columns):
    return pltpu.VMEM((len(chips), 2 * inverse.shape[0], columns), BF)


def child_part(chips, inverse, blocks, *acc):
    rows, columns = blocks[0].shape
    count = len(blocks)

    def kernel(inv_ref, *refs):
        block_refs, refs = refs[:count], refs[count:]
        start = refs[0][...] if acc else None
        out_ref, held_ref = refs[-2:]
        out_ref[...] = part_sum(chips, inv_ref, block_refs, held_ref, start)

    return call(
        kernel,
        shape((rows, columns), F32),
        inverse,
        *blocks,
        *acc,
        scratch=[held_scratch(chips, inverse, columns)],
    )


def child_last(chips, blocks, acc, inverse, coupling, child_blocks, pieces):
    rows, columns = acc.shape
    half, width = columns // 2, coupling.shape[1] // pieces
    count = len(blocks)

    def kernel(sizes_ref, inv_ref, coupling_ref, acc_ref, *refs):
        block_refs, refs = refs[:count], refs[count:]
        out_ref, keep_ref, *give_refs, held_ref, solved_ref = refs
        total = part_sum(chips, inv_ref, block_refs, held_ref, acc_ref[...])
        z, x, core = place()
        row = lax.broadcasted_iota(jnp.int32, total.shape, 0)
        first = (z % 2 * 8 + x * 2 + core) * rows
        limit = BLK * sizes_ref[z // 2] - first
        total = jnp.where(row < limit, total, 0.0)
        out_ref[...] = total
        solved_ref[...] = total.T.astype(BF)
        mine = pl.ds(pl.multiple_of(core * half, half), half)
        others = pl.ds(pl.multiple_of((1 - core) * half, half), half)
        solved = jnp.concatenate([solved_ref[mine], solved_ref[others]], axis=0)
        for i in range(pieces):
            update = jnp.dot(
                solved, coupling_ref[:, i * width : (i + 1) * width], preferred_element_type=F32
            )
            keep_ref[i] = update[:half]
            give_refs[2 * i // pieces][i % (pieces // 2)] = update[half:].astype(BF)

    return call(
        kernel,
        [
            shape((rows, columns), F32),
            shape((pieces, half, width), F32),
        ]
        + [shape((pieces // 2, half, width), BF)] * 2,
        child_blocks,
        inverse,
        coupling,
        acc,
        *blocks,
        smem=1,
        scratch=[held_scratch(chips, inverse, columns), pltpu.VMEM((columns, rows), BF)],
    )


def thirds(zp, zm, x2):
    rows, columns = x2.shape
    third = rows // 3

    def kernel(zp_ref, zm_ref, x2_ref, *out_refs):
        for i, ref in enumerate((zp_ref, zm_ref, x2_ref)):
            out_refs[i][...] = ref[i * third : (i + 1) * third]

    return call(kernel, [shape((third, columns), BF)] * 3, zp, zm, x2)


def reduce_kernel(pieces_ref, out_ref):
    total = pieces_ref[0].astype(F32)
    for i in range(1, pieces_ref.shape[0]):
        total += pieces_ref[i].astype(F32)
    out_ref[...] = total.T.astype(BF)


def reduce_pieces(pieces):
    count, half, width = pieces.shape
    return call(reduce_kernel, shape((width, half), BF), pieces)


def chip_at(i, j, core):
    z, x, _ = place()
    dx = jnp.where(core == 0, REL[i], REL[j])
    dz = jnp.where(core == 0, REL[j], REL[i])
    return (z + dz + 4) % 4, (x + dx + 4) % 4


def base_kernel(blocks_ref, p_ref, *refs):
    r_refs, (out_ref, picked_ref) = refs[:-2], refs[-2:]
    rows = p_ref.shape[0]
    core = place()[2]
    total = None
    for k, r_ref in enumerate(r_refs):
        owner = core if k < len(ENTRIES) else 1 - core
        for n, (i, j) in enumerate(ENTRIES[k % len(ENTRIES)]):
            z, x = chip_at(i, j, owner)
            at = pl.multiple_of((z * 8 + x * 2 + owner) * rows, BLK)
            part = jnp.dot(p_ref[:, pl.ds(at, rows)], r_ref[n], preferred_element_type=F32)
            total = part if total is None else total + part
    out_ref[...] = total
    for n in range(picked_ref.shape[1] // BLK):
        z, x = chip_at(n // 3 % 4, n // 12, core)
        block = blocks_ref[z // 2, (z % 2 * 4 + x) * 3 + n % 3]
        at = pl.multiple_of(block * BLK, BLK)
        picked_ref[:, n * BLK : (n + 1) * BLK] = p_ref[:, pl.ds(at, BLK)]


def base_product(blocks, inverse, parts):
    rows, order = inverse.shape
    columns = parts[0].shape[2]
    return call(
        base_kernel,
        [shape((rows, columns), F32), shape((rows, blocks.size * BLK), inverse.dtype)],
        blocks,
        inverse,
        *parts,
        smem=1,
    )


def final_kernel(base_ref, p_ref, *refs):
    own_refs, sib_refs, out_ref = refs[:4], refs[4:8], refs[8]
    width, half = own_refs[0].shape[1:]
    total = base_ref[...]
    change = None
    for j in range(4):
        for i in range(4):
            block = jnp.concatenate([own_refs[j][i], sib_refs[i][j]], axis=1)
            at = (j * 4 + i) * width
            part = jnp.dot(p_ref[:, at : at + width], block, preferred_element_type=F32)
            change = part if change is None else change + part
    core = place()[2]

    @pl.when(core == 0)
    def _():
        out_ref[...] = (total - change).T

    @pl.when(core == 1)
    def _():
        out_ref[:half] = (total[:, :half] - change[:, half:]).T
        out_ref[half:] = (total[:, half:] - change[:, :half]).T


def final_product(base, picked, own, sib):
    rows, columns = base.shape
    return call(
        final_kernel,
        shape((columns, rows), F32),
        base,
        picked,
        *own,
        *sib,
    )


def gather_first(block):
    return [block] + [receive(block, along(s, True)) for s in STEPS]


def gather_second(first, far=True):
    part = jnp.stack(first)
    return [part] + [receive(part, along(s, False)) for s in STEPS[: 3 if far else 2]]


def halves(up, down):
    count = up.shape[0] // 2
    cut = shape((count,) + up.shape[1:], up.dtype)

    def kernel(up_ref, down_ref, a_ref, b_ref):
        a_ref[...] = up_ref[:count]
        b_ref[...] = down_ref[count:]

    return call(kernel, [cut, cut], up, down)


def gather_far(near):
    a, b = halves(near[1], near[2])
    return [receive(a, along(1, False)), receive(b, along(-1, False))]


ENTRIES = [[(i, j) for i in range(4)] for j in range(3)] + [[(0, 3), (1, 3)], [(2, 3), (3, 3)]]


def on_device(
    child_rhs, parent_rhs, child_inverse, coupling, parent_inverse, child_blocks, parent_block
):
    b0 = child_rhs.T.astype(BF)
    b0_sib = from_sibling(b0)
    xp = receive(b0, lambda z, x, c: (z, x + 1, c))
    xm = receive(b0, lambda z, x, c: (z, x - 1, c))
    zb = receive(b0, lambda z, x, c: (z ^ 1, x, c))
    child_inverse, coupling = load(child_inverse, coupling)
    root = parent_rhs.T.astype(BF)
    xp, xm, zb, b0_sib, child_inverse, coupling, root = tie(
        xp, xm, zb, b0_sib, child_inverse, coupling, root
    )
    near = [b0, xp, xm, zb, b0_sib] + [from_sibling(v) for v in (xp, xm, zb)]
    acc = child_part([(0, 0), (0, 1), (0, 3), (1, 0)], child_inverse, near)
    x2 = receive(xp, lambda z, x, c: (z, x + 1, c))
    zm = receive(zb, lambda z, x, c: (z, x - 1, c))
    zp = receive(xp, lambda z, x, c: (z ^ 1, x, c))
    x2, zm, zp, acc = tie(x2, zm, zp, acc)
    last_a, last_b, last_c = thirds(zp, zm, x2)
    mid = [x2, zm, zp] + [from_sibling(v) for v in (x2, zm, zp)]
    root, mid[3] = tie(root, mid[3])
    acc = child_part([(0, 2), (1, 3), (1, 1)], child_inverse, mid, acc)
    r_near = gather_second(gather_first(root), far=False)
    z2 = jnp.concatenate(
        [
            receive(last_a, lambda z, x, c: (z, x + 1, c)),
            receive(last_b, lambda z, x, c: (z, x - 1, c)),
            receive(last_c, lambda z, x, c: (z ^ 1, x, c)),
        ],
        axis=0,
    )
    z2, acc = tie(z2, acc)
    solution_t, keep, *give = child_last(
        [(1, 2)], [z2, from_sibling(z2)], acc, child_inverse, coupling, child_blocks, 8
    )

    got = jnp.concatenate([from_sibling(part) for part in give], axis=0)
    chip_sum = (keep + got.astype(F32)).astype(BF)
    groups = [
        [flat(2 * h + dz, xx, c) for dz in range(2) for xx in range(4)]
        for h in range(2)
        for c in range(2)
    ]
    chip_sum, *r_near = tie(chip_sum, *r_near)
    pieces = lax.all_to_all(
        chip_sum, "wide", split_axis=0, concat_axis=0, axis_index_groups=groups, tiled=True
    )
    r_far = gather_far(r_near)
    r_near_sib = [from_sibling(part) for part in r_near]
    pieces, *r_near_sib = tie(pieces, *r_near_sib)
    u_first = gather_first(reduce_pieces(pieces))
    *u_first, r_far[0], r_far[1] = tie(*u_first, *r_far)
    u_own = gather_second(u_first)
    r_far_sib = [from_sibling(part) for part in r_far]
    base, picked = base_product(
        parent_block, parent_inverse, [*r_near, *r_far, *r_near_sib, *r_far_sib]
    )
    base, picked, *u_own = tie(base, picked, *u_own)
    u_sib = [from_sibling(part) for part in u_own]
    parent_solution = final_product(base, picked, u_own, u_sib)
    return (solution_t.T, parent_solution)


def solution(mesh):
    placed = (
        P("rhs", "wide"),
        P("rhs", "wide"),
        P("wide", None),
        P("wide", None),
        P("wide", None),
        P(),
        P(),
    )
    return jax.shard_map(
        on_device,
        mesh=mesh,
        in_specs=placed,
        out_specs=(P("rhs", "wide"), P("rhs", "wide")),
        check_vma=False,
    )
```

time: 122 us -> 108 us (0.89)
  blocking collectives: 16.8 us -> 0 us
  waiting for transfers between devices: 39.4 us -> 29.9 us
  starting transfers between devices: 38.8 us -> 47.9 us
  local copies, waits for them, and re-layouts: 1.16 us -> 4.81 us
    ppermute x34 -> x41, waiting for transfers between devices: 39.4 us -> 20.4 us  [receive(): return lax.ppermute(value, 'wide', pairs)]
    all_to_all x1 -> x0, blocking collectives: 16.8 us -> none  [on_device(): lax.all_to_all(chip_sum, 'wide', split_axis=0, concat_axis=0, axis_index_...]
    all_to_all x0 -> x1, waiting for transfers between devices: none -> 9.56 us  [on_device(): lax.all_to_all(chip_sum, 'wide', split_axis=0, concat_axis=0, axis_index_...]
    ppermute x34 -> x41, starting transfers between devices: 38.8 us -> 44.4 us  [receive(): return lax.ppermute(value, 'wide', pairs)]
    unnamed x5 -> x7, local copies, waits for them, and re-layouts: 1.13 us -> 4.81 us
    all_to_all x0 -> x1, starting transfers between devices: none -> 3.55 us  [on_device(): lax.all_to_all(chip_sum, 'wide', split_axis=0, concat_axis=0, axis_index_...]
  transfers between devices with their start and end apart: 34 -> 42, of which waited for: 14 -> 18; matrix products, arithmetic and copies ran while one was open for 1% -> 2% of each run, Pallas kernels for 9% -> 18%
where the time goes in v3:
time: 108 us
  starting transfers between devices  47.9 us (44%)
  waiting for transfers between devices  29.9 us (28%)
  Pallas kernels  21.9 us (20%)
  local copies, waits for them, and re-layouts  4.81 us (4%)
  other arithmetic  2.36 us (2%)
    ppermute x41, starting transfers between devices, receive(): return lax.ppermute(value, 'wide', pairs)  44.4 us
    pallas_call x9, Pallas kernels, call(): pl.pallas_call(kernel, in_specs=specs, out_specs=jax.tree.map(lambda _: V...  21.9 us
    ppermute x41, waiting for transfers between devices, receive(): return lax.ppermute(value, 'wide', pairs)  20.4 us
    all_to_all x1, waiting for transfers between devices, on_device(): lax.all_to_all(chip_sum, 'wide', split_axis=0, concat_axis=0, axis_index_...  9.56 us
    unnamed x7, local copies, waits for them, and re-layouts  4.81 us
    all_to_all x1, starting transfers between devices, on_device(): lax.all_to_all(chip_sum, 'wide', split_axis=0, concat_axis=0, axis_index_...  3.55 us
  transfers between devices with their start and end apart: 42, of which 18 were waited for; matrix products, arithmetic and copies ran while one was open for 2% of the time, Pallas kernels for 18%

profile of v3, /device:TPU:1, one launch (start us, length us, event | category | flops | bytes accessed | tf_op | source)
XLA Modules:
  0.0 107.8 jit_solution(12040240086206643444)
XLA Ops:
  1.7 3.4 %collective-permute-start = (bf16[576,256]{1,0:T(8,128)(2,1)S(1)}, bf16[576,256]{1,0:T(8,128)(2,1)S(1)}, u32[]{:S(2)}, u32[]{:S(2)}) collective-permute-start(bf16[576,256]{1,0:T(8,128)(2,1)S(1)} %convert_bitcast_fusion.refs_0_), channel_id=1, source_target_pairs={{8,0},{12,4},{16,8},{20,12},{24,16},{28,20},{0,24},{4,28},{40,32},... | collective-permute-start | bytes 884744 | tf_op jit(solution)/shard_map/ppermute | solution.py:27
  5.1 1.6 %collective-permute-start.2 = (bf16[576,256]{1,0:T(8,128)(2,1)S(1)}, bf16[576,256]{1,0:T(8,128)(2,1)S(1)}, u32[]{:S(2)}, u32[]{:S(2)}) collective-permute-start(bf16[576,256]{1,0:T(8,128)(2,1)S(1)} %convert_bitcast_fusion.refs_0_), channel_id=1, source_target_pairs={{32,0},{36,4},{40,8},{44,12},{48,16},{52,20},{56,24},{60,28},{0,32... | collective-permute-start | bytes 884744 | tf_op jit(solution)/shard_map/ppermute | solution.py:27
  9.1 5.1 %shard_map.86 = (bf16[576,9216]{1,0:T(8,128)(2,1)S(1)}, bf16[576,3072]{1,0:T(8,128)(2,1)S(1)}) custom-call(bf16[576,9216]{1,0:T(8,128)(2,1)} %refs_0_.1, bf16[576,3072]{1,0:T(8,128)(2,1)} %refs_1_.1), custom_call_target="tpu_custom_call" | custom-call | tf_op jit(solution)/shard_map/pallas_call | solution.py:62
  16.3 1.7 %collective-permute-start.4 = (bf16[576,256]{1,0:T(8,128)(2,1)S(1)}, bf16[576,256]{1,0:T(8,128)(2,1)S(1)}, u32[]{:S(2)}, u32[]{:S(2)}) collective-permute-start(bf16[576,256]{1,0:T(8,128)(2,1)S(1)} %collective-permute-done.refs_1_), channel_id=1, source_target_pairs={{8,0},{12,4},{16,8},{20,12},{24,16},{28,20},{0,24},{4,28},{40,32},... | collective-permute-start | bytes 884744 | tf_op jit(solution)/shard_map/ppermute | solution.py:27
  19.4 1.9 %shard_map.87.refs_6_ = f32[576,256]{1,0:T(8,128)S(1)} custom-call(bf16[576,9216]{1,0:T(8,128)(2,1)S(1)} %get-tuple-element.52.inv_ref, bf16[576,256]{1,0:T(8,128)(2,1)S(1)} %convert_bitcast_fusion.refs_0_, bf16[576,256]{1,0:T(8,128)(2,1)S(1)} %collective-permute-done.refs_1_, bf16[576,256]{1,0:T(8,128)(2,1)S(1)} %collective-permute-done.1.refs_2_, ...), custom_call_target="tpu_custom_call" | custom-call | tf_op jit(solution)/shard_map/pallas_call | solution.py:62
  21.3 3.6 %collective-permute-done.4.x2_ref.refs_0_ = bf16[576,256]{1,0:T(8,128)(2,1)S(1)} collective-permute-done((bf16[576,256]{1,0:T(8,128)(2,1)S(1)}, bf16[576,256]{1,0:T(8,128)(2,1)S(1)}, u32[]{:S(2)}, u32[]{:S(2)}) %collective-permute-start.4) | collective-permute-done | bytes 294944 | tf_op jit(solution)/shard_map/ppermute | solution.py:27
  24.8 2.2 %collective-permute-done.5.zm_ref.refs_1_ = bf16[576,256]{1,0:T(8,128)(2,1)S(1)} collective-permute-done((bf16[576,256]{1,0:T(8,128)(2,1)S(1)}, bf16[576,256]{1,0:T(8,128)(2,1)S(1)}, u32[]{:S(2)}, u32[]{:S(2)}) %collective-permute-start.5) | collective-permute-done | bytes 294944 | tf_op jit(solution)/shard_map/ppermute | solution.py:27
  30.6 2.7 %collective-permute-start.10 = (bf16[192,256]{1,0:T(8,128)(2,1)S(1)}, bf16[192,256]{1,0:T(8,128)(2,1)S(1)}, u32[]{:S(2)}, u32[]{:S(2)}) collective-permute-start(bf16[192,256]{1,0:T(8,128)(2,1)S(1)} %get-tuple-element.61), channel_id=1, source_target_pairs={{8,0},{12,4},{16,8},{20,12},{24,16},{28,20},{0,24},{4,28},{40,32},... | collective-permute-start | bytes 294920 | tf_op jit(solution)/shard_map/ppermute | solution.py:27
  33.6 3.4 %collective-permute-start.21 = (bf16[384,256]{1,0:T(8,128)(2,1)S(1)}, bf16[384,256]{1,0:T(8,128)(2,1)S(1)}, u32[]{:S(2)}, u32[]{:S(2)}) collective-permute-start(bf16[384,256]{1,0:T(8,128)(2,1)S(1)} %bitcast.15), channel_id=1, source_target_pairs={{16,0},{68,4},{24,8},{76,12},{0,16},{84,20},{8,24},{92,28},{48,32}... | collective-permute-start | bytes 589832 | tf_op jit(solution)/shard_map/ppermute | solution.py:27
  37.7 1.9 %collective-permute-start.19 = (bf16[384,256]{1,0:T(8,128)(2,1)S(1)}, bf16[384,256]{1,0:T(8,128)(2,1)S(1)}, u32[]{:S(2)}, u32[]{:S(2)}) collective-permute-start(bf16[384,256]{1,0:T(8,128)(2,1)S(1)} %bitcast.17), channel_id=1, source_target_pairs={{8,0},{36,4},{16,8},{44,12},{24,16},{52,20},{0,24},{60,28},{40,32}... | collective-permute-start | bytes 589832 | tf_op jit(solution)/shard_map/ppermute | solution.py:27
  44.8 4.1 %shard_map.90 = (f32[576,256]{1,0:T(8,128)}, f32[8,128,384]{2,1,0:T(8,128)S(1)}, bf16[4,128,384]{2,1,0:T(8,128)(2,1)S(1)}, bf16[4,128,384]{2,1,0:T(8,128)(2,1)S(1)}) custom-call(s32[2]{0:T(128)S(1)} %copy-done.2, bf16[576,9216]{1,0:T(8,128)(2,1)S(1)} %get-tuple-element.52.inv_ref, bf16[576,3072]{1,0:T(8,128)(2,1)S(1)} %get-tuple-element.53.coupling_ref, ...), custom_call_target="tpu_custom_call" | custom-call | tf_op jit(solution)/shard_map/pallas_call | solution.py:62
  48.9 2.9 %collective-permute-start.18 = (bf16[4,128,384]{2,1,0:T(8,128)(2,1)S(1)}, bf16[4,128,384]{2,1,0:T(8,128)(2,1)S(1)}, u32[]{:S(2)}, u32[]{:S(2)}) collective-permute-start(bf16[4,128,384]{2,1,0:T(8,128)(2,1)S(1)} %get-tuple-element.72), channel_id=1, source_target_pairs={{4,0},{0,4},{12,8},{8,12},{20,16},{16,20},{28,24},{24,28},{36,32},... | collective-permute-start | bytes 1179656 | tf_op jit(solution)/shard_map/ppermute | solution.py:27
  54.8 2.4 %collective-permute-done.23.down_ref.refs_2_ = bf16[4,384,256]{2,1,0:T(8,128)(2,1)S(1)} collective-permute-done((bf16[4,384,256]{2,1,0:T(8,128)(2,1)S(1)}, bf16[4,384,256]{2,1,0:T(8,128)(2,1)S(1)}, u32[]{:S(2)}, u32[]{:S(2)}) %collective-permute-start.23) | collective-permute-done | bytes 786464 | tf_op jit(solution)/shard_map/ppermute | solution.py:27
  57.2 3.7 %collective-permute-start.24 = (bf16[4,384,256]{2,1,0:T(8,128)(2,1)S(1)}, bf16[4,384,256]{2,1,0:T(8,128)(2,1)}, u32[]{:S(2)}, u32[]{:S(2)}) collective-permute-start(bf16[4,384,256]{2,1,0:T(8,128)(2,1)S(1)} %pad_maximum_fusion.refs_0_), channel_id=1, source_target_pairs={{4,0},{0,4},{12,8},{8,12},{20,16},{16,20},{28,24},{24,28},{36,32},... | collective-permute-start | bytes 2359304 | tf_op jit(solution)/shard_map/ppermute | solution.py:27
  61.4 3.5 %all-to-all-start = ((bf16[8,128,384]{2,1,0:T(8,128)(2,1)}), bf16[8,128,384]{2,1,0:T(8,128)(2,1)S(1)}, u32[]{:S(2)}, u32[]{:S(2)}) async-start(bf16[8,128,384]{2,1,0:T(8,128)(2,1)} %add_convert_fusion), calls=%async_computation | async-start | bytes 1572864 | tf_op jit(solution)/shard_map/all_to_all | solution.py:366
  65.9 2.6 %collective-permute-start.30 = (bf16[2,384,256]{2,1,0:T(8,128)(2,1)}, bf16[2,384,256]{2,1,0:T(8,128)(2,1)S(1)}, u32[]{:S(2)}, u32[]{:S(2)}) collective-permute-start(bf16[2,384,256]{2,1,0:T(8,128)(2,1)} %get-tuple-element.79), channel_id=1, source_target_pairs={{32,0},{12,4},{40,8},{20,12},{48,16},{28,20},{56,24},{4,28},{64,32... | collective-permute-start | bytes 1179656 | tf_op jit(solution)/shard_map/ppermute | solution.py:27
  68.5 9.6 %all-to-all-done.pieces_ref = bf16[8,128,384]{2,1,0:T(8,128)(2,1)S(1)} async-done(((bf16[8,128,384]{2,1,0:T(8,128)(2,1)}), bf16[8,128,384]{2,1,0:T(8,128)(2,1)S(1)}, u32[]{:S(2)}, u32[]{:S(2)}) %all-to-all-start) | async-done | bytes 786464 | tf_op jit(solution)/shard_map/all_to_all | solution.py:366
  83.0 1.7 %collective-permute-done.29 = bf16[384,128]{1,0:T(8,128)(2,1)S(1)} collective-permute-done((bf16[384,128]{1,0:T(8,128)(2,1)S(1)}, bf16[384,128]{1,0:T(8,128)(2,1)S(1)}, u32[]{:S(2)}, u32[]{:S(2)}) %collective-permute-start.29) | collective-permute-done | bytes 98336 | tf_op jit(solution)/shard_map/ppermute | solution.py:27
  84.7 2.7 %collective-permute-start.32 = (bf16[2,384,256]{2,1,0:T(8,128)(2,1)S(1)}, bf16[2,384,256]{2,1,0:T(8,128)(2,1)S(1)}, u32[]{:S(2)}, u32[]{:S(2)}) collective-permute-start(bf16[2,384,256]{2,1,0:T(8,128)(2,1)S(1)} %collective-permute-done.30.refs_3_), channel_id=1, source_target_pairs={{4,0},{0,4},{12,8},{8,12},{20,16},{16,20},{28,24},{24,28},{36,32},... | collective-permute-start | bytes 1179656 | tf_op jit(solution)/shard_map/ppermute | solution.py:27
  87.5 1.7 %collective-permute-start.34 = (bf16[4,384,128]{2,1,0:T(8,128)(2,1)S(1)}, bf16[4,384,128]{2,1,0:T(8,128)(2,1)S(1)}, u32[]{:S(2)}, u32[]{:S(2)}) collective-permute-start(bf16[4,384,128]{2,1,0:T(8,128)(2,1)S(1)} %pad_maximum_fusion.1.refs_0_), channel_id=1, source_target_pairs={{32,0},{12,4},{40,8},{20,12},{48,16},{28,20},{56,24},{4,28},{64,32... | collective-permute-start | bytes 1179656 | tf_op jit(solution)/shard_map/ppermute | solution.py:27
  90.5 3.7 %copy-done = bf16[384,12288]{1,0:T(8,128)(2,1)S(1)} copy-done((bf16[384,12288]{1,0:T(8,128)(2,1)S(1)}, bf16[384,12288]{1,0:T(8,128)(2,1)}, u32[]{:S(2)}) %copy-start) | copy-done | bytes 9437208
  94.1 5.5 %shard_map.93 = (f32[384,256]{1,0:T(8,128)S(1)}, bf16[384,6144]{1,0:T(8,128)(2,1)S(1)}) custom-call(s32[2,24]{1,0:T(2,128)S(1)} %copy-done.1, bf16[384,12288]{1,0:T(8,128)(2,1)S(1)} %copy-done, bf16[4,384,256]{2,1,0:T(8,128)(2,1)S(1)} %pad_maximum_fusion.refs_0_, bf16[4,384,256]{2,1,0:T(8,128)(2,1)S(1)} %collective-permute-done.22.up_ref.refs_1_, ...), custom_call_target="tpu_custom_call" | custom-call | tf_op jit(solution)/shard_map/pallas_call | solution.py:62
  99.6 1.9 %collective-permute-done.35.refs_2_ = bf16[4,384,128]{2,1,0:T(8,128)(2,1)S(1)} collective-permute-done((bf16[4,384,128]{2,1,0:T(8,128)(2,1)S(1)}, bf16[4,384,128]{2,1,0:T(8,128)(2,1)S(1)}, u32[]{:S(2)}, u32[]{:S(2)}) %collective-permute-start.35) | collective-permute-done | bytes 393248 | tf_op jit(solution)/shard_map/ppermute | solution.py:27
  105.0 2.7 %shard_map.94 = f32[256,384]{1,0:T(8,128)} custom-call(f32[384,256]{1,0:T(8,128)S(1)} %get-tuple-element.92.base_ref, bf16[384,6144]{1,0:T(8,128)(2,1)S(1)} %get-tuple-element.93.p_ref, bf16[4,384,128]{2,1,0:T(8,128)(2,1)S(1)} %pad_maximum_fusion.1.refs_0_, bf16[4,384,128]{2,1,0:T(8,128)(2,1)S(1)} %collective-permute-done.34.refs_1_, ...), custom_call_target="tpu_custom_call" | custom-call | tf_op jit(solution)/shard_map/pallas_call | solution.py:62
  (81 shorter events, 31.0 us)
Async XLA Ops:
  1.7 12.5 %collective-permute-start = (bf16[576,256]{1,0:T(8,128)(2,1)S(1)}, bf16[576,256]{1,0:T(8,128)(2,1)S(1)}, u32[]{:S(2)}, u32[]{:S(2)}) collective-permute-start(bf16[576,256]{1,0:T(8,128)(2,1)S(1)} %convert_bitcast_fusion.refs_0_), channel_id=1, source_target_pairs={{8,0},{12,4},{16,8},{20,12},{24,16},{28,20},{0,24},{4,28},{40,32},... | collective-permute-start | bytes 884744 | tf_op jit(solution)/shard_map/ppermute | solution.py:27
  5.1 9.2 %collective-permute-start.1 = (bf16[576,256]{1,0:T(8,128)(2,1)S(1)}, bf16[576,256]{1,0:T(8,128)(2,1)S(1)}, u32[]{:S(2)}, u32[]{:S(2)}) collective-permute-start(bf16[576,256]{1,0:T(8,128)(2,1)S(1)} %convert_bitcast_fusion.refs_0_), channel_id=1, source_target_pairs={{24,0},{28,4},{0,8},{4,12},{8,16},{12,20},{16,24},{20,28},{56,32},... | collective-permute-start | bytes 884744 | tf_op jit(solution)/shard_map/ppermute | solution.py:27
  5.1 9.2 %collective-permute-start.2 = (bf16[576,256]{1,0:T(8,128)(2,1)S(1)}, bf16[576,256]{1,0:T(8,128)(2,1)S(1)}, u32[]{:S(2)}, u32[]{:S(2)}) collective-permute-start(bf16[576,256]{1,0:T(8,128)(2,1)S(1)} %convert_bitcast_fusion.refs_0_), channel_id=1, source_target_pairs={{32,0},{36,4},{40,8},{44,12},{48,16},{52,20},{56,24},{60,28},{0,32... | collective-permute-start | bytes 884744 | tf_op jit(solution)/shard_map/ppermute | solution.py:27
  6.7 7.6 %collective-permute-start.3 = (bf16[576,256]{1,0:T(8,128)(2,1)S(1)}, bf16[576,256]{1,0:T(8,128)(2,1)S(1)}, u32[]{:S(2)}, u32[]{:S(2)}) collective-permute-start(bf16[576,256]{1,0:T(8,128)(2,1)S(1)} %convert_bitcast_fusion.refs_0_), channel_id=1, source_target_pairs={{4,0},{0,4},{12,8},{8,12},{20,16},{16,20},{28,24},{24,28},{36,32},... | collective-permute-start | bytes 884744 | tf_op jit(solution)/shard_map/ppermute | solution.py:27
  16.3 8.6 %collective-permute-start.4 = (bf16[576,256]{1,0:T(8,128)(2,1)S(1)}, bf16[576,256]{1,0:T(8,128)(2,1)S(1)}, u32[]{:S(2)}, u32[]{:S(2)}) collective-permute-start(bf16[576,256]{1,0:T(8,128)(2,1)S(1)} %collective-permute-done.refs_1_), channel_id=1, source_target_pairs={{8,0},{12,4},{16,8},{20,12},{24,16},{28,20},{0,24},{4,28},{40,32},... | collective-permute-start | bytes 884744 | tf_op jit(solution)/shard_map/ppermute | solution.py:27
  17.9 9.1 %collective-permute-start.5 = (bf16[576,256]{1,0:T(8,128)(2,1)S(1)}, bf16[576,256]{1,0:T(8,128)(2,1)S(1)}, u32[]{:S(2)}, u32[]{:S(2)}) collective-permute-start(bf16[576,256]{1,0:T(8,128)(2,1)S(1)} %collective-permute-done.2.refs_3_), channel_id=1, source_target_pairs={{24,0},{28,4},{0,8},{4,12},{8,16},{12,20},{16,24},{20,28},{56,32},... | collective-permute-start | bytes 884744 | tf_op jit(solution)/shard_map/ppermute | solution.py:27
  17.9 9.1 %collective-permute-start.6 = (bf16[576,256]{1,0:T(8,128)(2,1)S(1)}, bf16[576,256]{1,0:T(8,128)(2,1)S(1)}, u32[]{:S(2)}, u32[]{:S(2)}) collective-permute-start(bf16[576,256]{1,0:T(8,128)(2,1)S(1)} %collective-permute-done.refs_1_), channel_id=1, source_target_pairs={{32,0},{36,4},{40,8},{44,12},{48,16},{52,20},{56,24},{60,28},{0,32... | collective-permute-start | bytes 884744 | tf_op jit(solution)/shard_map/ppermute | solution.py:27
  28.6 11.1 %collective-permute-start.14 = (bf16[576,256]{1,0:T(8,128)(2,1)S(1)}, bf16[576,256]{1,0:T(8,128)(2,1)S(1)}, u32[]{:S(2)}, u32[]{:S(2)}) collective-permute-start(bf16[576,256]{1,0:T(8,128)(2,1)S(1)} %collective-permute-done.5.zm_ref.refs_1_), channel_id=1, source_target_pairs={{4,0},{0,4},{12,8},{8,12},{20,16},{16,20},{28,24},{24,28},{36,32},... | collective-permute-start | bytes 884744 | tf_op jit(solution)/shard_map/ppermute | solution.py:27
  28.6 11.1 %collective-permute-start.15 = (bf16[576,256]{1,0:T(8,128)(2,1)S(1)}, bf16[576,256]{1,0:T(8,128)(2,1)S(1)}, u32[]{:S(2)}, u32[]{:S(2)}) collective-permute-start(bf16[576,256]{1,0:T(8,128)(2,1)S(1)} %collective-permute-done.6.zp_ref.refs_2_), channel_id=1, source_target_pairs={{4,0},{0,4},{12,8},{8,12},{20,16},{16,20},{28,24},{24,28},{36,32},... | collective-permute-start | bytes 884744 | tf_op jit(solution)/shard_map/ppermute | solution.py:27
  30.6 6.4 %collective-permute-start.11 = (bf16[192,256]{1,0:T(8,128)(2,1)S(1)}, bf16[192,256]{1,0:T(8,128)(2,1)S(1)}, u32[]{:S(2)}, u32[]{:S(2)}) collective-permute-start(bf16[192,256]{1,0:T(8,128)(2,1)S(1)} %get-tuple-element.62), channel_id=1, source_target_pairs={{24,0},{28,4},{0,8},{4,12},{8,16},{12,20},{16,24},{20,28},{56,32},... | collective-permute-start | bytes 294920 | tf_op jit(solution)/shard_map/ppermute | solution.py:27
  30.6 7.1 %collective-permute-start.10 = (bf16[192,256]{1,0:T(8,128)(2,1)S(1)}, bf16[192,256]{1,0:T(8,128)(2,1)S(1)}, u32[]{:S(2)}, u32[]{:S(2)}) collective-permute-start(bf16[192,256]{1,0:T(8,128)(2,1)S(1)} %get-tuple-element.61), channel_id=1, source_target_pairs={{8,0},{12,4},{16,8},{20,12},{24,16},{28,20},{0,24},{4,28},{40,32},... | collective-permute-start | bytes 294920 | tf_op jit(solution)/shard_map/ppermute | solution.py:27
  33.6 8.3 %collective-permute-start.21 = (bf16[384,256]{1,0:T(8,128)(2,1)S(1)}, bf16[384,256]{1,0:T(8,128)(2,1)S(1)}, u32[]{:S(2)}, u32[]{:S(2)}) collective-permute-start(bf16[384,256]{1,0:T(8,128)(2,1)S(1)} %bitcast.15), channel_id=1, source_target_pairs={{16,0},{68,4},{24,8},{76,12},{0,16},{84,20},{8,24},{92,28},{48,32}... | collective-permute-start | bytes 589832 | tf_op jit(solution)/shard_map/ppermute | solution.py:27
  37.0 6.0 %collective-permute-start.20 = (bf16[384,256]{1,0:T(8,128)(2,1)S(1)}, bf16[384,256]{1,0:T(8,128)(2,1)S(1)}, u32[]{:S(2)}, u32[]{:S(2)}) collective-permute-start(bf16[384,256]{1,0:T(8,128)(2,1)S(1)} %bitcast.16), channel_id=1, source_target_pairs={{24,0},{100,4},{0,8},{108,12},{8,16},{116,20},{16,24},{124,28},{56... | collective-permute-start | bytes 589832 | tf_op jit(solution)/shard_map/ppermute | solution.py:27
  43.3 11.5 %collective-permute-start.22 = (bf16[4,384,256]{2,1,0:T(8,128)(2,1)S(1)}, bf16[4,384,256]{2,1,0:T(8,128)(2,1)S(1)}, u32[]{:S(2)}, u32[]{:S(2)}) collective-permute-start(bf16[4,384,256]{2,1,0:T(8,128)(2,1)S(1)} %pad_maximum_fusion.refs_0_), channel_id=1, source_target_pairs={{32,0},{12,4},{40,8},{20,12},{48,16},{28,20},{56,24},{4,28},{64,32... | collective-permute-start | bytes 2359304 | tf_op jit(solution)/shard_map/ppermute | solution.py:27
  44.8 12.3 %collective-permute-start.23 = (bf16[4,384,256]{2,1,0:T(8,128)(2,1)S(1)}, bf16[4,384,256]{2,1,0:T(8,128)(2,1)S(1)}, u32[]{:S(2)}, u32[]{:S(2)}) collective-permute-start(bf16[4,384,256]{2,1,0:T(8,128)(2,1)S(1)} %pad_maximum_fusion.refs_0_), channel_id=1, source_target_pairs={{96,0},{28,4},{104,8},{4,12},{112,16},{12,20},{120,24},{20,28},{0,... | collective-permute-start | bytes 2359304 | tf_op jit(solution)/shard_map/ppermute | solution.py:27
  57.2 20.8 %collective-permute-start.24 = (bf16[4,384,256]{2,1,0:T(8,128)(2,1)S(1)}, bf16[4,384,256]{2,1,0:T(8,128)(2,1)}, u32[]{:S(2)}, u32[]{:S(2)}) collective-permute-start(bf16[4,384,256]{2,1,0:T(8,128)(2,1)S(1)} %pad_maximum_fusion.refs_0_), channel_id=1, source_target_pairs={{4,0},{0,4},{12,8},{8,12},{20,16},{16,20},{28,24},{24,28},{36,32},... | collective-permute-start | bytes 2359304 | tf_op jit(solution)/shard_map/ppermute | solution.py:27
  60.9 17.1 %collective-permute-start.25 = (bf16[4,384,256]{2,1,0:T(8,128)(2,1)S(1)}, bf16[4,384,256]{2,1,0:T(8,128)(2,1)}, u32[]{:S(2)}, u32[]{:S(2)}) collective-permute-start(bf16[4,384,256]{2,1,0:T(8,128)(2,1)S(1)} %collective-permute-done.22.up_ref.refs_1_), channel_id=1, source_target_pairs={{4,0},{0,4},{12,8},{8,12},{20,16},{16,20},{28,24},{24,28},{36,32},... | collective-permute-start | bytes 2359304 | tf_op jit(solution)/shard_map/ppermute | solution.py:27
  60.9 17.1 %collective-permute-start.26 = (bf16[4,384,256]{2,1,0:T(8,128)(2,1)S(1)}, bf16[4,384,256]{2,1,0:T(8,128)(2,1)}, u32[]{:S(2)}, u32[]{:S(2)}) collective-permute-start(bf16[4,384,256]{2,1,0:T(8,128)(2,1)S(1)} %collective-permute-done.23.down_ref.refs_2_), channel_id=1, source_target_pairs={{4,0},{0,4},{12,8},{8,12},{20,16},{16,20},{28,24},{24,28},{36,32},... | collective-permute-start | bytes 2359304 | tf_op jit(solution)/shard_map/ppermute | solution.py:27
  61.4 16.6 %all-to-all-start = ((bf16[8,128,384]{2,1,0:T(8,128)(2,1)}), bf16[8,128,384]{2,1,0:T(8,128)(2,1)S(1)}, u32[]{:S(2)}, u32[]{:S(2)}) async-start(bf16[8,128,384]{2,1,0:T(8,128)(2,1)} %add_convert_fusion), calls=%async_computation | async-start | bytes 1572864 | tf_op jit(solution)/shard_map/all_to_all | solution.py:366
  65.9 14.5 %collective-permute-start.30 = (bf16[2,384,256]{2,1,0:T(8,128)(2,1)}, bf16[2,384,256]{2,1,0:T(8,128)(2,1)S(1)}, u32[]{:S(2)}, u32[]{:S(2)}) collective-permute-start(bf16[2,384,256]{2,1,0:T(8,128)(2,1)} %get-tuple-element.79), channel_id=1, source_target_pairs={{32,0},{12,4},{40,8},{20,12},{48,16},{28,20},{56,24},{4,28},{64,32... | collective-permute-start | bytes 1179656 | tf_op jit(solution)/shard_map/ppermute | solution.py:27
  68.5 13.0 %collective-permute-start.31 = (bf16[2,384,256]{2,1,0:T(8,128)(2,1)}, bf16[2,384,256]{2,1,0:T(8,128)(2,1)}, u32[]{:S(2)}, u32[]{:S(2)}) collective-permute-start(bf16[2,384,256]{2,1,0:T(8,128)(2,1)} %get-tuple-element.80), channel_id=1, source_target_pairs={{96,0},{28,4},{104,8},{4,12},{112,16},{12,20},{120,24},{20,28},{0,... | collective-permute-start | bytes 1179656 | tf_op jit(solution)/shard_map/ppermute | solution.py:27
  87.5 12.1 %collective-permute-start.34 = (bf16[4,384,128]{2,1,0:T(8,128)(2,1)S(1)}, bf16[4,384,128]{2,1,0:T(8,128)(2,1)S(1)}, u32[]{:S(2)}, u32[]{:S(2)}) collective-permute-start(bf16[4,384,128]{2,1,0:T(8,128)(2,1)S(1)} %pad_maximum_fusion.1.refs_0_), channel_id=1, source_target_pairs={{32,0},{12,4},{40,8},{20,12},{48,16},{28,20},{56,24},{4,28},{64,32... | collective-permute-start | bytes 1179656 | tf_op jit(solution)/shard_map/ppermute | solution.py:27
  89.2 12.3 %collective-permute-start.35 = (bf16[4,384,128]{2,1,0:T(8,128)(2,1)S(1)}, bf16[4,384,128]{2,1,0:T(8,128)(2,1)S(1)}, u32[]{:S(2)}, u32[]{:S(2)}) collective-permute-start(bf16[4,384,128]{2,1,0:T(8,128)(2,1)S(1)} %pad_maximum_fusion.1.refs_0_), channel_id=1, source_target_pairs={{96,0},{28,4},{104,8},{4,12},{112,16},{12,20},{120,24},{20,28},{0,... | collective-permute-start | bytes 1179656 | tf_op jit(solution)/shard_map/ppermute | solution.py:27
  89.2 12.3 %collective-permute-start.36 = (bf16[4,384,128]{2,1,0:T(8,128)(2,1)S(1)}, bf16[4,384,128]{2,1,0:T(8,128)(2,1)S(1)}, u32[]{:S(2)}, u32[]{:S(2)}) collective-permute-start(bf16[4,384,128]{2,1,0:T(8,128)(2,1)S(1)} %pad_maximum_fusion.1.refs_0_), channel_id=1, source_target_pairs={{64,0},{20,4},{72,8},{28,12},{80,16},{4,20},{88,24},{12,28},{96,32... | collective-permute-start | bytes 1179656 | tf_op jit(solution)/shard_map/ppermute | solution.py:27
  (21 other events, 110.4 us)

commit v4 on v3

--- a/solution.py
+++ b/solution.py
@@ -53,7 +53,7 @@
 HBM = pl.BlockSpec(memory_space=pltpu.HBM)
 
 
-def call(kernel, out_shape, *operands, smem=0, hbm=(), scratch=()):
+def call(kernel, out_shape, *operands, smem=0, hbm=(), scratch=(), weight=0):
     specs = [SMEM if i < smem else HBM if i in hbm else VMEM for i in range(len(operands))]
     operands = [
         pltpu.with_memory_space_constraint(operand, pltpu.HBM) if i in hbm else operand
@@ -66,7 +66,7 @@
         out_shape=out_shape,
         scratch_shapes=scratch,
         compiler_params=pltpu.CompilerParams(vmem_limit_bytes=VMEM_LIMIT),
-        cost_estimate=pl.CostEstimate(flops=0, bytes_accessed=0, transcendentals=0),
+        cost_estimate=pl.CostEstimate(flops=0, bytes_accessed=weight, transcendentals=0),
     )(*operands)
 
 
@@ -116,8 +116,8 @@
     mine = pl.ds(pl.multiple_of(core * rows, 16), rows)
     others = pl.ds(pl.multiple_of((1 - core) * rows, 16), rows)
     for i, (dz, dx) in enumerate(chips):
-        held_ref[i, mine] = block_refs[i][...]
-        held_ref[i, others] = block_refs[len(chips) + i][...]
+        held_ref[i, mine] = block_refs[i]
+        held_ref[i, others] = block_refs[len(chips) + i]
         at = ((z + dz) % 2 * 4 + (x + dx) % 4) * 2 * rows
         columns = pl.ds(pl.multiple_of(at, BLK), 2 * rows)
         part = jnp.dot(inv_ref[:, columns], held_ref[i], preferred_element_type=F32)
@@ -129,15 +129,22 @@
     return pltpu.VMEM((len(chips), 2 * inverse.shape[0], columns), BF)
 
 
+def entries(refs):
+    blocks = []
+    for ref in refs:
+        blocks += [ref[...]] if len(ref.shape) == 2 else [ref[i] for i in range(ref.shape[0])]
+    return blocks
+
+
 def child_part(chips, inverse, blocks, *acc):
-    rows, columns = blocks[0].shape
+    rows, columns = blocks[0].shape[-2:]
     count = len(blocks)
 
     def kernel(inv_ref, *refs):
         block_refs, refs = refs[:count], refs[count:]
         start = refs[0][...] if acc else None
         out_ref, held_ref = refs[-2:]
-        out_ref[...] = part_sum(chips, inv_ref, block_refs, held_ref, start)
+        out_ref[...] = part_sum(chips, inv_ref, entries(block_refs), held_ref, start)
 
     return call(
         kernel,
@@ -157,7 +164,7 @@
     def kernel(sizes_ref, inv_ref, coupling_ref, acc_ref, *refs):
         block_refs, refs = refs[:count], refs[count:]
         out_ref, keep_ref, *give_refs, held_ref, solved_ref = refs
-        total = part_sum(chips, inv_ref, block_refs, held_ref, acc_ref[...])
+        total = part_sum(chips, inv_ref, entries(block_refs), held_ref, acc_ref[...])
         z, x, core = place()
         row = lax.broadcasted_iota(jnp.int32, total.shape, 0)
         first = (z % 2 * 8 + x * 2 + core) * rows
@@ -192,15 +199,48 @@
     )
 
 
-def thirds(zp, zm, x2):
+def turn(block):
+    def kernel(block_ref, out_ref):
+        out_ref[...] = block_ref[...].T.astype(BF)
+
+    return call(kernel, shape(block.shape[::-1], BF), block)
+
+
+def pile(*blocks):
+    def kernel(*refs):
+        for i, ref in enumerate(refs[:-1]):
+            refs[-1][i] = ref[...]
+
+    return call(kernel, shape((len(blocks),) + blocks[0].shape, BF), *blocks)
+
+
+def pile_and_cut(x2, zm, zp):
     rows, columns = x2.shape
-    third = rows // 3
-
-    def kernel(zp_ref, zm_ref, x2_ref, *out_refs):
-        for i, ref in enumerate((zp_ref, zm_ref, x2_ref)):
-            out_refs[i][...] = ref[i * third : (i + 1) * third]
-
-    return call(kernel, [shape((third, columns), BF)] * 3, zp, zm, x2)
+
+    def kernel(x2_ref, zm_ref, zp_ref, pile_ref, a_ref, b_ref):
+        for i, ref in enumerate((x2_ref, zm_ref, zp_ref)):
+            pile_ref[i] = ref[...]
+        a_ref[...] = zp_ref[: rows // 2]
+        b_ref[...] = zm_ref[rows // 2 :]
+
+    return call(
+        kernel,
+        [shape((3, rows, columns), BF)] + [shape((rows // 2, columns), BF)] * 2,
+        x2,
+        zm,
+        zp,
+    )
+
+
+def cut_halves(up, down, weight=0):
+    count = up.shape[0] // 2
+    cut = shape((count,) + up.shape[1:], up.dtype)
+
+    def kernel(up_ref, down_ref, a_ref, b_ref):
+        a_ref[...] = up_ref[:count]
+        b_ref[...] = down_ref[count:]
+
+    return call(kernel, [cut, cut], up, down, weight=weight)
 
 
 def reduce_kernel(pieces_ref, out_ref):
@@ -222,35 +262,40 @@
     return (z + dz + 4) % 4, (x + dx + 4) % 4
 
 
-def base_kernel(blocks_ref, p_ref, *refs):
-    r_refs, (out_ref, picked_ref) = refs[:-2], refs[-2:]
+def root_sum(entries, p_ref, r_refs, total):
     rows = p_ref.shape[0]
     core = place()[2]
-    total = None
     for k, r_ref in enumerate(r_refs):
-        owner = core if k < len(ENTRIES) else 1 - core
-        for n, (i, j) in enumerate(ENTRIES[k % len(ENTRIES)]):
+        owner = core if k < len(entries) else 1 - core
+        for n, (i, j) in enumerate(entries[k % len(entries)]):
             z, x = chip_at(i, j, owner)
             at = pl.multiple_of((z * 8 + x * 2 + owner) * rows, BLK)
             part = jnp.dot(p_ref[:, pl.ds(at, rows)], r_ref[n], preferred_element_type=F32)
             total = part if total is None else total + part
-    out_ref[...] = total
-    for n in range(picked_ref.shape[1] // BLK):
-        z, x = chip_at(n // 3 % 4, n // 12, core)
-        block = blocks_ref[z // 2, (z % 2 * 4 + x) * 3 + n % 3]
-        at = pl.multiple_of(block * BLK, BLK)
-        picked_ref[:, n * BLK : (n + 1) * BLK] = p_ref[:, pl.ds(at, BLK)]
-
-
-def base_product(blocks, inverse, parts):
-    rows, order = inverse.shape
-    columns = parts[0].shape[2]
-    return call(
-        base_kernel,
+    return total
+
+
+def base_product(blocks, inverse, near, far):
+    rows, columns = inverse.shape[0], near[0].shape[2]
+
+    def kernel(blocks_ref, p_ref, *refs):
+        r_refs, (out_ref, picked_ref) = refs[:-2], refs[-2:]
+        total = root_sum(NEAR, p_ref, r_refs[: len(near)], None)
+        out_ref[...] = root_sum(FAR, p_ref, r_refs[len(near) :], total)
+        core = place()[2]
+        for n in range(picked_ref.shape[1] // BLK):
+            z, x = chip_at(n // 3 % 4, n // 12, core)
+            block = blocks_ref[z // 2, (z % 2 * 4 + x) * 3 + n % 3]
+            at = pl.multiple_of(block * BLK, BLK)
+            picked_ref[:, n * BLK : (n + 1) * BLK] = p_ref[:, pl.ds(at, BLK)]
+
+    return call(
+        kernel,
         [shape((rows, columns), F32), shape((rows, blocks.size * BLK), inverse.dtype)],
         blocks,
         inverse,
-        *parts,
+        *near,
+        *far,
         smem=1,
     )
 
@@ -294,28 +339,22 @@
     return [block] + [receive(block, along(s, True)) for s in STEPS]
 
 
-def gather_second(first, far=True):
+def gather_second(first):
     part = jnp.stack(first)
-    return [part] + [receive(part, along(s, False)) for s in STEPS[: 3 if far else 2]]
-
-
-def halves(up, down):
-    count = up.shape[0] // 2
-    cut = shape((count,) + up.shape[1:], up.dtype)
-
-    def kernel(up_ref, down_ref, a_ref, b_ref):
-        a_ref[...] = up_ref[:count]
-        b_ref[...] = down_ref[count:]
-
-    return call(kernel, [cut, cut], up, down)
-
-
-def gather_far(near):
-    a, b = halves(near[1], near[2])
-    return [receive(a, along(1, False)), receive(b, along(-1, False))]
-
-
-ENTRIES = [[(i, j) for i in range(4)] for j in range(3)] + [[(0, 3), (1, 3)], [(2, 3), (3, 3)]]
+    return [part] + [receive(part, along(s, False)) for s in STEPS]
+
+
+def gather_near(first):
+    part = jnp.stack(first)
+    return [part] + [receive(part, along(s, False)) for s in STEPS[:2]]
+
+
+def gather_far(up, down):
+    return [receive(up, along(1, False)), receive(down, along(-1, False))]
+
+
+NEAR = [[(i, j) for i in range(4)] for j in range(3)]
+FAR = [[(0, 3), (1, 3)], [(2, 3), (3, 3)]]
 
 
 def on_device(
@@ -326,27 +365,28 @@
     xp = receive(b0, lambda z, x, c: (z, x + 1, c))
     xm = receive(b0, lambda z, x, c: (z, x - 1, c))
     zb = receive(b0, lambda z, x, c: (z ^ 1, x, c))
-    child_inverse, coupling = load(child_inverse, coupling)
-    root = parent_rhs.T.astype(BF)
-    xp, xm, zb, b0_sib, child_inverse, coupling, root = tie(
-        xp, xm, zb, b0_sib, child_inverse, coupling, root
-    )
-    near = [b0, xp, xm, zb, b0_sib] + [from_sibling(v) for v in (xp, xm, zb)]
-    acc = child_part([(0, 0), (0, 1), (0, 3), (1, 0)], child_inverse, near)
+    (child_inverse,) = load(child_inverse)
+    xp, xm, zb, b0_sib, child_inverse, coupling, parent_rhs = tie(
+        xp, xm, zb, b0_sib, child_inverse, coupling, parent_rhs
+    )
+    near = pile(xp, xm, zb)
+    near_sib = from_sibling(near)
+    parent_rhs, coupling, near_sib = tie(parent_rhs, coupling, near_sib)
+    root = turn(parent_rhs)
+    (coupling,) = load(coupling)
+    acc = child_part([(0, 0), (0, 1), (0, 3), (1, 0)], child_inverse, [b0, near, b0_sib, near_sib])
     x2 = receive(xp, lambda z, x, c: (z, x + 1, c))
     zm = receive(zb, lambda z, x, c: (z, x - 1, c))
     zp = receive(xp, lambda z, x, c: (z ^ 1, x, c))
-    x2, zm, zp, acc = tie(x2, zm, zp, acc)
-    last_a, last_b, last_c = thirds(zp, zm, x2)
-    mid = [x2, zm, zp] + [from_sibling(v) for v in (x2, zm, zp)]
-    root, mid[3] = tie(root, mid[3])
-    acc = child_part([(0, 2), (1, 3), (1, 1)], child_inverse, mid, acc)
-    r_near = gather_second(gather_first(root), far=False)
+    r_first = [root] + [receive(root, along(s, True)) for s in STEPS[:2]]
+    x2, zm, zp, acc, coupling, *r_first = tie(x2, zm, zp, acc, coupling, *r_first)
+    mid, last_a, last_b = pile_and_cut(x2, zm, zp)
+    acc = child_part([(0, 2), (1, 3), (1, 1)], child_inverse, [mid, from_sibling(mid)], acc)
+    r_near = gather_near(r_first + [receive(r_first[1], along(1, True))])
     z2 = jnp.concatenate(
         [
             receive(last_a, lambda z, x, c: (z, x + 1, c)),
             receive(last_b, lambda z, x, c: (z, x - 1, c)),
-            receive(last_c, lambda z, x, c: (z ^ 1, x, c)),
         ],
         axis=0,
     )
@@ -362,22 +402,25 @@
         for h in range(2)
         for c in range(2)
     ]
-    chip_sum, *r_near = tie(chip_sum, *r_near)
+    far_up, far_down = cut_halves(r_near[1], r_near[2], weight=2 << 20)
+    chip_sum, far_up, far_down, *r_near = tie(chip_sum, far_up, far_down, *r_near)
     pieces = lax.all_to_all(
         chip_sum, "wide", split_axis=0, concat_axis=0, axis_index_groups=groups, tiled=True
     )
-    r_far = gather_far(r_near)
-    r_near_sib = [from_sibling(part) for part in r_near]
-    pieces, *r_near_sib = tie(pieces, *r_near_sib)
-    u_first = gather_first(reduce_pieces(pieces))
-    *u_first, r_far[0], r_far[1] = tie(*u_first, *r_far)
+    r_far = gather_far(far_up, far_down)
+    update, *r_sib = tie(reduce_pieces(pieces), *[from_sibling(part) for part in r_near])
+    r_near += r_sib
+    update, parent_inverse = tie(update, parent_inverse)
+    (parent_inverse,) = load(parent_inverse)
+    *u_first, parent_inverse, r_far[0], r_far[1] = tie(
+        *gather_first(update), parent_inverse, *r_far
+    )
+    r_far += [from_sibling(part) for part in r_far]
     u_own = gather_second(u_first)
-    r_far_sib = [from_sibling(part) for part in r_far]
-    base, picked = base_product(
-        parent_block, parent_inverse, [*r_near, *r_far, *r_near_sib, *r_far_sib]
-    )
-    base, picked, *u_own = tie(base, picked, *u_own)
-    u_sib = [from_sibling(part) for part in u_own]
+    u_sib = [from_sibling(u_own[0])]
+    base, picked = base_product(parent_block, parent_inverse, r_near, r_far)
+    base, u_own[1], u_sib[0] = tie(base, u_own[1], u_sib[0])
+    u_sib += [from_sibling(part) for part in u_own[1:]]
     parent_solution = final_product(base, picked, u_own, u_sib)
     return (solution_t.T, parent_solution)
 

time: 108 us -> 105 us (0.972)
  waiting for transfers between devices: 29.9 us -> 21.5 us
  Pallas kernels: 21.9 us -> 26.2 us
  starting transfers between devices: 47.9 us -> 51.9 us
  local copies, waits for them, and re-layouts: 4.81 us -> 1.51 us
    ppermute x41 -> x36, waiting for transfers between devices: 20.4 us -> 11.1 us  [receive(): return lax.ppermute(value, 'wide', pairs)]
    pallas_call x9 -> x13, Pallas kernels: 21.9 us -> 26.2 us  [call(): pl.pallas_call(kernel, in_specs=specs, out_specs=jax.tree.map(lambda _: V...]
    ppermute x41 -> x36, starting transfers between devices: 44.4 us -> 48.3 us  [receive(): return lax.ppermute(value, 'wide', pairs)]
    unnamed x7 -> x10, local copies, waits for them, and re-layouts: 4.81 us -> 1.51 us
  transfers between devices with their start and end apart: 42 -> 37, of which waited for: 18 -> 11; matrix products, arithmetic and copies ran while one was open for 2% -> 0% of each run, Pallas kernels for 18% -> 22%
where the time goes in v4:
time: 105 us; the launch traced here: 104 us
  starting transfers between devices  51.9 us (49%)
  Pallas kernels  26.2 us (25%)
  waiting for transfers between devices  21.5 us (20%)
  other arithmetic  2.37 us (2%)
  local copies, waits for them, and re-layouts  1.51 us (1%)
    ppermute x36, starting transfers between devices, receive(): return lax.ppermute(value, 'wide', pairs)  48.3 us
    pallas_call x13, Pallas kernels, call(): pl.pallas_call(kernel, in_specs=specs, out_specs=jax.tree.map(lambda _: V...  26.2 us
    ppermute x36, waiting for transfers between devices, receive(): return lax.ppermute(value, 'wide', pairs)  11.1 us
    all_to_all x1, waiting for transfers between devices, on_device(): lax.all_to_all(chip_sum, 'wide', split_axis=0, concat_axis=0, axis_index_...  10.4 us
    all_to_all x1, starting transfers between devices, on_device(): lax.all_to_all(chip_sum, 'wide', split_axis=0, concat_axis=0, axis_index_...  3.57 us
  transfers between devices with their start and end apart: 37, of which 11 were waited for; matrix products, arithmetic and copies ran while one was open for 0% of the time, Pallas kernels for 22%

profile of v4, /device:TPU:1, one launch (start us, length us, event | category | flops | bytes accessed | tf_op | source)
XLA Modules:
  0.0 104.4 jit_solution(3970140790965022962)
XLA Ops:
  1.7 3.4 %collective-permute-start = (bf16[576,256]{1,0:T(8,128)(2,1)S(1)}, bf16[576,256]{1,0:T(8,128)(2,1)S(1)}, u32[]{:S(2)}, u32[]{:S(2)}) collective-permute-start(bf16[576,256]{1,0:T(8,128)(2,1)S(1)} %convert_bitcast_fusion.refs_0_), channel_id=1, source_target_pairs={{8,0},{12,4},{16,8},{20,12},{24,16},{28,20},{0,24},{4,28},{40,32},... | collective-permute-start | bytes 884744 | tf_op jit(solution)/shard_map/ppermute | solution.py:27
  8.0 4.1 %shard_map.86.inv_ref = bf16[576,9216]{1,0:T(8,128)(2,1)S(1)} custom-call(bf16[576,9216]{1,0:T(8,128)(2,1)} %refs_0_.1), custom_call_target="tpu_custom_call" | custom-call | tf_op jit(solution)/shard_map/pallas_call | solution.py:62
  12.1 1.8 %collective-permute-done.1.refs_1_ = bf16[576,256]{1,0:T(8,128)(2,1)S(1)} collective-permute-done((bf16[576,256]{1,0:T(8,128)(2,1)S(1)}, bf16[576,256]{1,0:T(8,128)(2,1)S(1)}, u32[]{:S(2)}, u32[]{:S(2)}) %collective-permute-start.1) | collective-permute-done | bytes 294944 | tf_op jit(solution)/shard_map/ppermute | solution.py:27
  14.0 1.9 %collective-permute-start.7 = (bf16[3,576,256]{2,1,0:T(8,128)(2,1)S(1)}, bf16[3,576,256]{2,1,0:T(8,128)(2,1)S(1)}, u32[]{:S(2)}, u32[]{:S(2)}) collective-permute-start(bf16[3,576,256]{2,1,0:T(8,128)(2,1)S(1)} %shard_map.87.refs_1_), channel_id=1, source_target_pairs={{4,0},{0,4},{12,8},{8,12},{20,16},{16,20},{28,24},{24,28},{36,32},... | collective-permute-start | bytes 2654216 | tf_op jit(solution)/shard_map/ppermute | solution.py:27
  19.2 2.8 %collective-permute-start.8 = (bf16[384,256]{1,0:T(8,128)(2,1)S(1)}, bf16[384,256]{1,0:T(8,128)(2,1)S(1)}, u32[]{:S(2)}, u32[]{:S(2)}) collective-permute-start(bf16[384,256]{1,0:T(8,128)(2,1)S(1)} %shard_map.90), channel_id=1, source_target_pairs={{8,0},{36,4},{16,8},{44,12},{24,16},{52,20},{0,24},{60,28},{40,32}... | collective-permute-start | bytes 589832 | tf_op jit(solution)/shard_map/ppermute | solution.py:27
  21.9 2.0 %shard_map.89.coupling_ref = bf16[576,3072]{1,0:T(8,128)(2,1)S(1)} custom-call(bf16[576,3072]{1,0:T(8,128)(2,1)} %refs_0_.2), custom_call_target="tpu_custom_call" | custom-call | tf_op jit(solution)/shard_map/pallas_call | solution.py:62
  23.9 1.9 %shard_map.88.refs_2_ = f32[576,256]{1,0:T(8,128)S(1)} custom-call(bf16[576,9216]{1,0:T(8,128)(2,1)S(1)} %shard_map.86.inv_ref, bf16[576,256]{1,0:T(8,128)(2,1)S(1)} %convert_bitcast_fusion.refs_0_, bf16[3,576,256]{2,1,0:T(8,128)(2,1)S(1)} %shard_map.87.refs_1_, bf16[576,256]{1,0:T(8,128)(2,1)S(1)} %collective-permute-done.3.refs_2_, ...), custom_call_target="tpu_custom_call" | custom-call | tf_op jit(solution)/shard_map/pallas_call | solution.py:62
  27.0 1.7 %collective-permute-done.8 = bf16[384,256]{1,0:T(8,128)(2,1)S(1)} collective-permute-done((bf16[384,256]{1,0:T(8,128)(2,1)S(1)}, bf16[384,256]{1,0:T(8,128)(2,1)S(1)}, u32[]{:S(2)}, u32[]{:S(2)}) %collective-permute-start.8) | collective-permute-done | bytes 196640 | tf_op jit(solution)/shard_map/ppermute | solution.py:27
  28.8 1.7 %collective-permute-start.12 = (bf16[3,576,256]{2,1,0:T(8,128)(2,1)S(1)}, bf16[3,576,256]{2,1,0:T(8,128)(2,1)S(1)}, u32[]{:S(2)}, u32[]{:S(2)}) collective-permute-start(bf16[3,576,256]{2,1,0:T(8,128)(2,1)S(1)} %get-tuple-element.71.refs_0_), channel_id=1, source_target_pairs={{4,0},{0,4},{12,8},{8,12},{20,16},{16,20},{28,24},{24,28},{36,32},... | collective-permute-start | bytes 2654216 | tf_op jit(solution)/shard_map/ppermute | solution.py:27
  30.5 3.6 %collective-permute-start.16 = (bf16[384,256]{1,0:T(8,128)(2,1)S(1)}, bf16[384,256]{1,0:T(8,128)(2,1)S(1)}, u32[]{:S(2)}, u32[]{:S(2)}) collective-permute-start(bf16[384,256]{1,0:T(8,128)(2,1)S(1)} %collective-permute-done.8), channel_id=1, source_target_pairs={{8,0},{36,4},{16,8},{44,12},{24,16},{52,20},{0,24},{60,28},{40,32}... | collective-permute-start | bytes 589832 | tf_op jit(solution)/shard_map/ppermute | solution.py:27
  34.0 2.7 %collective-permute-start.10 = (bf16[288,256]{1,0:T(8,128)(2,1)S(1)}, bf16[288,256]{1,0:T(8,128)(2,1)S(1)}, u32[]{:S(2)}, u32[]{:S(2)}) collective-permute-start(bf16[288,256]{1,0:T(8,128)(2,1)S(1)} %get-tuple-element.69), channel_id=1, source_target_pairs={{8,0},{12,4},{16,8},{20,12},{24,16},{28,20},{0,24},{4,28},{40,32},... | collective-permute-start | bytes 442376 | tf_op jit(solution)/shard_map/ppermute | solution.py:27
  40.8 2.2 %collective-permute-start.13 = (bf16[576,256]{1,0:T(8,128)(2,1)S(1)}, bf16[576,256]{1,0:T(8,128)(2,1)S(1)}, u32[]{:S(2)}, u32[]{:S(2)}) collective-permute-start(bf16[576,256]{1,0:T(8,128)(2,1)S(1)} %pad_maximum_fusion.2.refs_0_), channel_id=1, source_target_pairs={{4,0},{0,4},{12,8},{8,12},{20,16},{16,20},{28,24},{24,28},{36,32},... | collective-permute-start | bytes 884744 | tf_op jit(solution)/shard_map/ppermute | solution.py:27
  44.2 4.1 %shard_map.93 = (f32[576,256]{1,0:T(8,128)}, f32[8,128,384]{2,1,0:T(8,128)S(1)}, bf16[4,128,384]{2,1,0:T(8,128)(2,1)S(1)}, bf16[4,128,384]{2,1,0:T(8,128)(2,1)S(1)}) custom-call(s32[2]{0:T(128)S(1)} %copy-done.2, bf16[576,9216]{1,0:T(8,128)(2,1)S(1)} %shard_map.86.inv_ref, bf16[576,3072]{1,0:T(8,128)(2,1)S(1)} %shard_map.89.coupling_ref, ...), custom_call_target="tpu_custom_call" | custom-call | tf_op jit(solution)/shard_map/pallas_call | solution.py:62
  52.7 4.6 %collective-permute-start.19 = (bf16[4,384,256]{2,1,0:T(8,128)(2,1)S(1)}, bf16[4,384,256]{2,1,0:T(8,128)(2,1)}, u32[]{:S(2)}, u32[]{:S(2)}) collective-permute-start(bf16[4,384,256]{2,1,0:T(8,128)(2,1)S(1)} %pad_maximum_fusion.refs_0_), channel_id=1, source_target_pairs={{4,0},{0,4},{12,8},{8,12},{20,16},{16,20},{28,24},{24,28},{36,32},... | collective-permute-start | bytes 2359304 | tf_op jit(solution)/shard_map/ppermute | solution.py:27
  57.8 3.6 %all-to-all-start = ((bf16[8,128,384]{2,1,0:T(8,128)(2,1)}), bf16[8,128,384]{2,1,0:T(8,128)(2,1)S(1)}, u32[]{:S(2)}, u32[]{:S(2)}) async-start(bf16[8,128,384]{2,1,0:T(8,128)(2,1)} %add_convert_fusion), calls=%async_computation | async-start | bytes 1572864 | tf_op jit(solution)/shard_map/all_to_all | solution.py:407
  61.4 2.7 %collective-permute-start.25 = (bf16[2,384,256]{2,1,0:T(8,128)(2,1)}, bf16[2,384,256]{2,1,0:T(8,128)(2,1)S(1)}, u32[]{:S(2)}, u32[]{:S(2)}) collective-permute-start(bf16[2,384,256]{2,1,0:T(8,128)(2,1)} %copy-done.4), channel_id=1, source_target_pairs={{32,0},{12,4},{40,8},{20,12},{48,16},{28,20},{56,24},{4,28},{64,32... | collective-permute-start | bytes 1179656 | tf_op jit(solution)/shard_map/ppermute | solution.py:27
  64.0 10.4 %all-to-all-done.pieces_ref = bf16[8,128,384]{2,1,0:T(8,128)(2,1)S(1)} async-done(((bf16[8,128,384]{2,1,0:T(8,128)(2,1)}), bf16[8,128,384]{2,1,0:T(8,128)(2,1)S(1)}, u32[]{:S(2)}, u32[]{:S(2)}) %all-to-all-start) | async-done | bytes 786464 | tf_op jit(solution)/shard_map/all_to_all | solution.py:407
  76.8 3.8 %shard_map.96.p_ref = bf16[384,12288]{1,0:T(8,128)(2,1)S(1)} custom-call(bf16[384,12288]{1,0:T(8,128)(2,1)} %refs_0_.3), custom_call_target="tpu_custom_call" | custom-call | tf_op jit(solution)/shard_map/pallas_call | solution.py:62
  81.2 2.8 %collective-permute-start.27 = (bf16[2,384,256]{2,1,0:T(8,128)(2,1)S(1)}, bf16[2,384,256]{2,1,0:T(8,128)(2,1)S(1)}, u32[]{:S(2)}, u32[]{:S(2)}) collective-permute-start(bf16[2,384,256]{2,1,0:T(8,128)(2,1)S(1)} %collective-permute-done.25.refs_6_), channel_id=1, source_target_pairs={{4,0},{0,4},{12,8},{8,12},{20,16},{16,20},{28,24},{24,28},{36,32},... | collective-permute-start | bytes 1179656 | tf_op jit(solution)/shard_map/ppermute | solution.py:27
  84.0 2.0 %collective-permute-start.29 = (bf16[4,384,128]{2,1,0:T(8,128)(2,1)S(1)}, bf16[4,384,128]{2,1,0:T(8,128)(2,1)S(1)}, u32[]{:S(2)}, u32[]{:S(2)}) collective-permute-start(bf16[4,384,128]{2,1,0:T(8,128)(2,1)S(1)} %pad_maximum_fusion.1.refs_0_), channel_id=1, source_target_pairs={{32,0},{12,4},{40,8},{20,12},{48,16},{28,20},{56,24},{4,28},{64,32... | collective-permute-start | bytes 1179656 | tf_op jit(solution)/shard_map/ppermute | solution.py:27
  86.1 2.5 %collective-permute-start.32 = (bf16[4,384,128]{2,1,0:T(8,128)(2,1)S(1)}, bf16[4,384,128]{2,1,0:T(8,128)(2,1)S(1)}, u32[]{:S(2)}, u32[]{:S(2)}) collective-permute-start(bf16[4,384,128]{2,1,0:T(8,128)(2,1)S(1)} %pad_maximum_fusion.1.refs_0_), channel_id=1, source_target_pairs={{64,0},{20,4},{72,8},{28,12},{80,16},{4,20},{88,24},{12,28},{96,32... | collective-permute-start | bytes 1179656 | tf_op jit(solution)/shard_map/ppermute | solution.py:27
  88.6 5.6 %shard_map.97 = (f32[384,256]{1,0:T(8,128)S(1)}, bf16[384,6144]{1,0:T(8,128)(2,1)S(1)}) custom-call(s32[2,24]{1,0:T(2,128)S(1)} %copy-done.1, bf16[384,12288]{1,0:T(8,128)(2,1)S(1)} %shard_map.96.p_ref, bf16[4,384,256]{2,1,0:T(8,128)(2,1)S(1)} %pad_maximum_fusion.refs_0_, bf16[4,384,256]{2,1,0:T(8,128)(2,1)S(1)} %collective-permute-done.17.up_ref.refs_1_, ...), custom_call_target="tpu_custom_call" | custom-call | tf_op jit(solution)/shard_map/pallas_call | solution.py:62
  94.9 4.8 %collective-permute-start.34 = (bf16[4,384,128]{2,1,0:T(8,128)(2,1)S(1)}, bf16[4,384,128]{2,1,0:T(8,128)(2,1)S(1)}, u32[]{:S(2)}, u32[]{:S(2)}) collective-permute-start(bf16[4,384,128]{2,1,0:T(8,128)(2,1)S(1)} %collective-permute-done.31.refs_2_), channel_id=1, source_target_pairs={{4,0},{0,4},{12,8},{8,12},{20,16},{16,20},{28,24},{24,28},{36,32},... | collective-permute-start | bytes 1179656 | tf_op jit(solution)/shard_map/ppermute | solution.py:27
  101.6 2.7 %shard_map.98 = f32[256,384]{1,0:T(8,128)} custom-call(f32[384,256]{1,0:T(8,128)S(1)} %get-tuple-element.104.base_ref, bf16[384,6144]{1,0:T(8,128)(2,1)S(1)} %get-tuple-element.105.p_ref, bf16[4,384,128]{2,1,0:T(8,128)(2,1)S(1)} %pad_maximum_fusion.1.refs_0_, bf16[4,384,128]{2,1,0:T(8,128)(2,1)S(1)} %collective-permute-done.29.refs_1_, ...), custom_call_target="tpu_custom_call" | custom-call | tf_op jit(solution)/shard_map/pallas_call | solution.py:62
  (78 shorter events, 24.3 us)
Async XLA Ops:
  1.7 10.4 %collective-permute-start = (bf16[576,256]{1,0:T(8,128)(2,1)S(1)}, bf16[576,256]{1,0:T(8,128)(2,1)S(1)}, u32[]{:S(2)}, u32[]{:S(2)}) collective-permute-start(bf16[576,256]{1,0:T(8,128)(2,1)S(1)} %convert_bitcast_fusion.refs_0_), channel_id=1, source_target_pairs={{8,0},{12,4},{16,8},{20,12},{24,16},{28,20},{0,24},{4,28},{40,32},... | collective-permute-start | bytes 884744 | tf_op jit(solution)/shard_map/ppermute | solution.py:27
  5.1 8.8 %collective-permute-start.1 = (bf16[576,256]{1,0:T(8,128)(2,1)S(1)}, bf16[576,256]{1,0:T(8,128)(2,1)S(1)}, u32[]{:S(2)}, u32[]{:S(2)}) collective-permute-start(bf16[576,256]{1,0:T(8,128)(2,1)S(1)} %convert_bitcast_fusion.refs_0_), channel_id=1, source_target_pairs={{24,0},{28,4},{0,8},{4,12},{8,16},{12,20},{16,24},{20,28},{56,32},... | collective-permute-start | bytes 884744 | tf_op jit(solution)/shard_map/ppermute | solution.py:27
  5.1 8.8 %collective-permute-start.2 = (bf16[576,256]{1,0:T(8,128)(2,1)S(1)}, bf16[576,256]{1,0:T(8,128)(2,1)S(1)}, u32[]{:S(2)}, u32[]{:S(2)}) collective-permute-start(bf16[576,256]{1,0:T(8,128)(2,1)S(1)} %convert_bitcast_fusion.refs_0_), channel_id=1, source_target_pairs={{32,0},{36,4},{40,8},{44,12},{48,16},{52,20},{56,24},{60,28},{0,32... | collective-permute-start | bytes 884744 | tf_op jit(solution)/shard_map/ppermute | solution.py:27
  6.8 7.1 %collective-permute-start.3 = (bf16[576,256]{1,0:T(8,128)(2,1)S(1)}, bf16[576,256]{1,0:T(8,128)(2,1)S(1)}, u32[]{:S(2)}, u32[]{:S(2)}) collective-permute-start(bf16[576,256]{1,0:T(8,128)(2,1)S(1)} %convert_bitcast_fusion.refs_0_), channel_id=1, source_target_pairs={{4,0},{0,4},{12,8},{8,12},{20,16},{16,20},{28,24},{24,28},{36,32},... | collective-permute-start | bytes 884744 | tf_op jit(solution)/shard_map/ppermute | solution.py:27
  15.9 9.9 %collective-permute-start.4 = (bf16[576,256]{1,0:T(8,128)(2,1)S(1)}, bf16[576,256]{1,0:T(8,128)(2,1)S(1)}, u32[]{:S(2)}, u32[]{:S(2)}) collective-permute-start(bf16[576,256]{1,0:T(8,128)(2,1)S(1)} %collective-permute-done.refs_0_), channel_id=1, source_target_pairs={{8,0},{12,4},{16,8},{20,12},{24,16},{28,20},{0,24},{4,28},{40,32},... | collective-permute-start | bytes 884744 | tf_op jit(solution)/shard_map/ppermute | solution.py:27
  17.6 9.5 %collective-permute-start.5 = (bf16[576,256]{1,0:T(8,128)(2,1)S(1)}, bf16[576,256]{1,0:T(8,128)(2,1)S(1)}, u32[]{:S(2)}, u32[]{:S(2)}) collective-permute-start(bf16[576,256]{1,0:T(8,128)(2,1)S(1)} %collective-permute-done.2.refs_2_), channel_id=1, source_target_pairs={{24,0},{28,4},{0,8},{4,12},{8,16},{12,20},{16,24},{20,28},{56,32},... | collective-permute-start | bytes 884744 | tf_op jit(solution)/shard_map/ppermute | solution.py:27
  17.6 9.5 %collective-permute-start.6 = (bf16[576,256]{1,0:T(8,128)(2,1)S(1)}, bf16[576,256]{1,0:T(8,128)(2,1)S(1)}, u32[]{:S(2)}, u32[]{:S(2)}) collective-permute-start(bf16[576,256]{1,0:T(8,128)(2,1)S(1)} %collective-permute-done.refs_0_), channel_id=1, source_target_pairs={{32,0},{36,4},{40,8},{44,12},{48,16},{52,20},{56,24},{60,28},{0,32... | collective-permute-start | bytes 884744 | tf_op jit(solution)/shard_map/ppermute | solution.py:27
  19.2 9.5 %collective-permute-start.8 = (bf16[384,256]{1,0:T(8,128)(2,1)S(1)}, bf16[384,256]{1,0:T(8,128)(2,1)S(1)}, u32[]{:S(2)}, u32[]{:S(2)}) collective-permute-start(bf16[384,256]{1,0:T(8,128)(2,1)S(1)} %shard_map.90), channel_id=1, source_target_pairs={{8,0},{36,4},{16,8},{44,12},{24,16},{52,20},{0,24},{60,28},{40,32}... | collective-permute-start | bytes 589832 | tf_op jit(solution)/shard_map/ppermute | solution.py:27
  21.9 6.8 %collective-permute-start.9 = (bf16[384,256]{1,0:T(8,128)(2,1)S(1)}, bf16[384,256]{1,0:T(8,128)(2,1)S(1)}, u32[]{:S(2)}, u32[]{:S(2)}) collective-permute-start(bf16[384,256]{1,0:T(8,128)(2,1)S(1)} %shard_map.90), channel_id=1, source_target_pairs={{24,0},{100,4},{0,8},{108,12},{8,16},{116,20},{16,24},{124,28},{56... | collective-permute-start | bytes 589832 | tf_op jit(solution)/shard_map/ppermute | solution.py:27
  28.8 10.5 %collective-permute-start.12 = (bf16[3,576,256]{2,1,0:T(8,128)(2,1)S(1)}, bf16[3,576,256]{2,1,0:T(8,128)(2,1)S(1)}, u32[]{:S(2)}, u32[]{:S(2)}) collective-permute-start(bf16[3,576,256]{2,1,0:T(8,128)(2,1)S(1)} %get-tuple-element.71.refs_0_), channel_id=1, source_target_pairs={{4,0},{0,4},{12,8},{8,12},{20,16},{16,20},{28,24},{24,28},{36,32},... | collective-permute-start | bytes 2654216 | tf_op jit(solution)/shard_map/ppermute | solution.py:27
  30.5 6.3 %collective-permute-start.16 = (bf16[384,256]{1,0:T(8,128)(2,1)S(1)}, bf16[384,256]{1,0:T(8,128)(2,1)S(1)}, u32[]{:S(2)}, u32[]{:S(2)}) collective-permute-start(bf16[384,256]{1,0:T(8,128)(2,1)S(1)} %collective-permute-done.8), channel_id=1, source_target_pairs={{8,0},{36,4},{16,8},{44,12},{24,16},{52,20},{0,24},{60,28},{40,32}... | collective-permute-start | bytes 589832 | tf_op jit(solution)/shard_map/ppermute | solution.py:27
  36.8 12.0 %collective-permute-start.17 = (bf16[4,384,256]{2,1,0:T(8,128)(2,1)S(1)}, bf16[4,384,256]{2,1,0:T(8,128)(2,1)S(1)}, u32[]{:S(2)}, u32[]{:S(2)}) collective-permute-start(bf16[4,384,256]{2,1,0:T(8,128)(2,1)S(1)} %pad_maximum_fusion.refs_0_), channel_id=1, source_target_pairs={{32,0},{12,4},{40,8},{20,12},{48,16},{28,20},{56,24},{4,28},{64,32... | collective-permute-start | bytes 2359304 | tf_op jit(solution)/shard_map/ppermute | solution.py:27
  37.7 12.3 %collective-permute-start.18 = (bf16[4,384,256]{2,1,0:T(8,128)(2,1)S(1)}, bf16[4,384,256]{2,1,0:T(8,128)(2,1)S(1)}, u32[]{:S(2)}, u32[]{:S(2)}) collective-permute-start(bf16[4,384,256]{2,1,0:T(8,128)(2,1)S(1)} %pad_maximum_fusion.refs_0_), channel_id=1, source_target_pairs={{96,0},{28,4},{104,8},{4,12},{112,16},{12,20},{120,24},{20,28},{0,... | collective-permute-start | bytes 2359304 | tf_op jit(solution)/shard_map/ppermute | solution.py:27
  52.7 21.9 %collective-permute-start.19 = (bf16[4,384,256]{2,1,0:T(8,128)(2,1)S(1)}, bf16[4,384,256]{2,1,0:T(8,128)(2,1)}, u32[]{:S(2)}, u32[]{:S(2)}) collective-permute-start(bf16[4,384,256]{2,1,0:T(8,128)(2,1)S(1)} %pad_maximum_fusion.refs_0_), channel_id=1, source_target_pairs={{4,0},{0,4},{12,8},{8,12},{20,16},{16,20},{28,24},{24,28},{36,32},... | collective-permute-start | bytes 2359304 | tf_op jit(solution)/shard_map/ppermute | solution.py:27
  57.3 17.4 %collective-permute-start.20 = (bf16[4,384,256]{2,1,0:T(8,128)(2,1)S(1)}, bf16[4,384,256]{2,1,0:T(8,128)(2,1)}, u32[]{:S(2)}, u32[]{:S(2)}) collective-permute-start(bf16[4,384,256]{2,1,0:T(8,128)(2,1)S(1)} %collective-permute-done.17.up_ref.refs_1_), channel_id=1, source_target_pairs={{4,0},{0,4},{12,8},{8,12},{20,16},{16,20},{28,24},{24,28},{36,32},... | collective-permute-start | bytes 2359304 | tf_op jit(solution)/shard_map/ppermute | solution.py:27
  57.3 17.4 %collective-permute-start.21 = (bf16[4,384,256]{2,1,0:T(8,128)(2,1)S(1)}, bf16[4,384,256]{2,1,0:T(8,128)(2,1)}, u32[]{:S(2)}, u32[]{:S(2)}) collective-permute-start(bf16[4,384,256]{2,1,0:T(8,128)(2,1)S(1)} %collective-permute-done.18.down_ref.refs_2_), channel_id=1, source_target_pairs={{4,0},{0,4},{12,8},{8,12},{20,16},{16,20},{28,24},{24,28},{36,32},... | collective-permute-start | bytes 2359304 | tf_op jit(solution)/shard_map/ppermute | solution.py:27
  57.8 16.7 %all-to-all-start = ((bf16[8,128,384]{2,1,0:T(8,128)(2,1)}), bf16[8,128,384]{2,1,0:T(8,128)(2,1)S(1)}, u32[]{:S(2)}, u32[]{:S(2)}) async-start(bf16[8,128,384]{2,1,0:T(8,128)(2,1)} %add_convert_fusion), calls=%async_computation | async-start | bytes 1572864 | tf_op jit(solution)/shard_map/all_to_all | solution.py:407
  61.4 19.3 %collective-permute-start.25 = (bf16[2,384,256]{2,1,0:T(8,128)(2,1)}, bf16[2,384,256]{2,1,0:T(8,128)(2,1)S(1)}, u32[]{:S(2)}, u32[]{:S(2)}) collective-permute-start(bf16[2,384,256]{2,1,0:T(8,128)(2,1)} %copy-done.4), channel_id=1, source_target_pairs={{32,0},{12,4},{40,8},{20,12},{48,16},{28,20},{56,24},{4,28},{64,32... | collective-permute-start | bytes 1179656 | tf_op jit(solution)/shard_map/ppermute | solution.py:27
  64.0 16.6 %collective-permute-start.26 = (bf16[2,384,256]{2,1,0:T(8,128)(2,1)}, bf16[2,384,256]{2,1,0:T(8,128)(2,1)}, u32[]{:S(2)}, u32[]{:S(2)}) collective-permute-start(bf16[2,384,256]{2,1,0:T(8,128)(2,1)} %copy-done.3), channel_id=1, source_target_pairs={{96,0},{28,4},{104,8},{4,12},{112,16},{12,20},{120,24},{20,28},{0,... | collective-permute-start | bytes 1179656 | tf_op jit(solution)/shard_map/ppermute | solution.py:27
  84.0 10.9 %collective-permute-start.29 = (bf16[4,384,128]{2,1,0:T(8,128)(2,1)S(1)}, bf16[4,384,128]{2,1,0:T(8,128)(2,1)S(1)}, u32[]{:S(2)}, u32[]{:S(2)}) collective-permute-start(bf16[4,384,128]{2,1,0:T(8,128)(2,1)S(1)} %pad_maximum_fusion.1.refs_0_), channel_id=1, source_target_pairs={{32,0},{12,4},{40,8},{20,12},{48,16},{28,20},{56,24},{4,28},{64,32... | collective-permute-start | bytes 1179656 | tf_op jit(solution)/shard_map/ppermute | solution.py:27
  86.0 8.9 %collective-permute-start.30 = (bf16[4,384,128]{2,1,0:T(8,128)(2,1)S(1)}, bf16[4,384,128]{2,1,0:T(8,128)(2,1)S(1)}, u32[]{:S(2)}, u32[]{:S(2)}) collective-permute-start(bf16[4,384,128]{2,1,0:T(8,128)(2,1)S(1)} %pad_maximum_fusion.1.refs_0_), channel_id=1, source_target_pairs={{4,0},{0,4},{12,8},{8,12},{20,16},{16,20},{28,24},{24,28},{36,32},... | collective-permute-start | bytes 1179656 | tf_op jit(solution)/shard_map/ppermute | solution.py:27
  86.0 8.9 %collective-permute-start.31 = (bf16[4,384,128]{2,1,0:T(8,128)(2,1)S(1)}, bf16[4,384,128]{2,1,0:T(8,128)(2,1)S(1)}, u32[]{:S(2)}, u32[]{:S(2)}) collective-permute-start(bf16[4,384,128]{2,1,0:T(8,128)(2,1)S(1)} %pad_maximum_fusion.1.refs_0_), channel_id=1, source_target_pairs={{96,0},{28,4},{104,8},{4,12},{112,16},{12,20},{120,24},{20,28},{0,... | collective-permute-start | bytes 1179656 | tf_op jit(solution)/shard_map/ppermute | solution.py:27
  86.1 13.6 %collective-permute-start.32 = (bf16[4,384,128]{2,1,0:T(8,128)(2,1)S(1)}, bf16[4,384,128]{2,1,0:T(8,128)(2,1)S(1)}, u32[]{:S(2)}, u32[]{:S(2)}) collective-permute-start(bf16[4,384,128]{2,1,0:T(8,128)(2,1)S(1)} %pad_maximum_fusion.1.refs_0_), channel_id=1, source_target_pairs={{64,0},{20,4},{72,8},{28,12},{80,16},{4,20},{88,24},{12,28},{96,32... | collective-permute-start | bytes 1179656 | tf_op jit(solution)/shard_map/ppermute | solution.py:27
  94.9 6.1 %collective-permute-start.34 = (bf16[4,384,128]{2,1,0:T(8,128)(2,1)S(1)}, bf16[4,384,128]{2,1,0:T(8,128)(2,1)S(1)}, u32[]{:S(2)}, u32[]{:S(2)}) collective-permute-start(bf16[4,384,128]{2,1,0:T(8,128)(2,1)S(1)} %collective-permute-done.31.refs_2_), channel_id=1, source_target_pairs={{4,0},{0,4},{12,8},{8,12},{20,16},{16,20},{28,24},{24,28},{36,32},... | collective-permute-start | bytes 1179656 | tf_op jit(solution)/shard_map/ppermute | solution.py:27
  (18 other events, 95.9 us)

commit v5 on v4

--- a/solution.py
+++ b/solution.py
@@ -297,20 +297,20 @@
         *near,
         *far,
         smem=1,
+        weight=7 << 19,
     )
 
 
 def final_kernel(base_ref, p_ref, *refs):
-    own_refs, sib_refs, out_ref = refs[:4], refs[4:8], refs[8]
+    own_refs, sib_refs, out_ref, held_ref = refs[:4], refs[4:8], refs[8], refs[9]
     width, half = own_refs[0].shape[1:]
     total = base_ref[...]
-    change = None
     for j in range(4):
         for i in range(4):
-            block = jnp.concatenate([own_refs[j][i], sib_refs[i][j]], axis=1)
-            at = (j * 4 + i) * width
-            part = jnp.dot(p_ref[:, at : at + width], block, preferred_element_type=F32)
-            change = part if change is None else change + part
+            rows = pl.ds((j * 4 + i) * width, width)
+            held_ref[rows, :half] = own_refs[j][i]
+            held_ref[rows, half:] = sib_refs[i][j]
+    change = jnp.dot(p_ref[...], held_ref[...], preferred_element_type=F32)
     core = place()[2]
 
     @pl.when(core == 0)
@@ -332,6 +332,7 @@
         picked,
         *own,
         *sib,
+        scratch=[pltpu.VMEM((picked.shape[1], columns), BF)],
     )
 
 

time: 105 us -> 104 us (level)
  no operation moved by 1% of the time
where the time goes in v5:
time: 104 us
  starting transfers between devices  51.9 us (50%)
  Pallas kernels  25.9 us (25%)
  waiting for transfers between devices  21.6 us (21%)
  other arithmetic  2.37 us (2%)
  local copies, waits for them, and re-layouts  1.51 us (1%)
    ppermute x36, starting transfers between devices, receive(): return lax.ppermute(value, 'wide', pairs)  48.3 us
    pallas_call x13, Pallas kernels, call(): pl.pallas_call(kernel, in_specs=specs, out_specs=jax.tree.map(lambda _: V...  25.9 us
    ppermute x36, waiting for transfers between devices, receive(): return lax.ppermute(value, 'wide', pairs)  11.2 us
    all_to_all x1, waiting for transfers between devices, on_device(): lax.all_to_all(chip_sum, 'wide', split_axis=0, concat_axis=0, axis_index_...  10.4 us
    all_to_all x1, starting transfers between devices, on_device(): lax.all_to_all(chip_sum, 'wide', split_axis=0, concat_axis=0, axis_index_...  3.57 us
  transfers between devices with their start and end apart: 37, of which 11 were waited for; matrix products, arithmetic and copies ran while one was open for 0% of the time, Pallas kernels for 22%

profile of v5, /device:TPU:1, one launch (start us, length us, event | category | flops | bytes accessed | tf_op | source)
XLA Modules:
  0.0 104.2 jit_solution(6794589196228492078)
XLA Ops:
  1.7 3.4 %collective-permute-start = (bf16[576,256]{1,0:T(8,128)(2,1)S(1)}, bf16[576,256]{1,0:T(8,128)(2,1)S(1)}, u32[]{:S(2)}, u32[]{:S(2)}) collective-permute-start(bf16[576,256]{1,0:T(8,128)(2,1)S(1)} %convert_bitcast_fusion.refs_0_), channel_id=1, source_target_pairs={{8,0},{12,4},{16,8},{20,12},{24,16},{28,20},{0,24},{4,28},{40,32},... | collective-permute-start | bytes 884744 | tf_op jit(solution)/shard_map/ppermute | solution.py:27
  8.0 4.1 %shard_map.86.inv_ref = bf16[576,9216]{1,0:T(8,128)(2,1)S(1)} custom-call(bf16[576,9216]{1,0:T(8,128)(2,1)} %refs_0_.1), custom_call_target="tpu_custom_call" | custom-call | tf_op jit(solution)/shard_map/pallas_call | solution.py:62
  12.1 1.8 %collective-permute-done.1.refs_1_ = bf16[576,256]{1,0:T(8,128)(2,1)S(1)} collective-permute-done((bf16[576,256]{1,0:T(8,128)(2,1)S(1)}, bf16[576,256]{1,0:T(8,128)(2,1)S(1)}, u32[]{:S(2)}, u32[]{:S(2)}) %collective-permute-start.1) | collective-permute-done | bytes 294944 | tf_op jit(solution)/shard_map/ppermute | solution.py:27
  14.0 1.9 %collective-permute-start.7 = (bf16[3,576,256]{2,1,0:T(8,128)(2,1)S(1)}, bf16[3,576,256]{2,1,0:T(8,128)(2,1)S(1)}, u32[]{:S(2)}, u32[]{:S(2)}) collective-permute-start(bf16[3,576,256]{2,1,0:T(8,128)(2,1)S(1)} %shard_map.87.refs_1_), channel_id=1, source_target_pairs={{4,0},{0,4},{12,8},{8,12},{20,16},{16,20},{28,24},{24,28},{36,32},... | collective-permute-start | bytes 2654216 | tf_op jit(solution)/shard_map/ppermute | solution.py:27
  19.2 2.8 %collective-permute-start.8 = (bf16[384,256]{1,0:T(8,128)(2,1)S(1)}, bf16[384,256]{1,0:T(8,128)(2,1)S(1)}, u32[]{:S(2)}, u32[]{:S(2)}) collective-permute-start(bf16[384,256]{1,0:T(8,128)(2,1)S(1)} %shard_map.90), channel_id=1, source_target_pairs={{8,0},{36,4},{16,8},{44,12},{24,16},{52,20},{0,24},{60,28},{40,32}... | collective-permute-start | bytes 589832 | tf_op jit(solution)/shard_map/ppermute | solution.py:27
  21.9 2.0 %shard_map.89.coupling_ref = bf16[576,3072]{1,0:T(8,128)(2,1)S(1)} custom-call(bf16[576,3072]{1,0:T(8,128)(2,1)} %refs_0_.2), custom_call_target="tpu_custom_call" | custom-call | tf_op jit(solution)/shard_map/pallas_call | solution.py:62
  23.9 1.9 %shard_map.88.refs_2_ = f32[576,256]{1,0:T(8,128)S(1)} custom-call(bf16[576,9216]{1,0:T(8,128)(2,1)S(1)} %shard_map.86.inv_ref, bf16[576,256]{1,0:T(8,128)(2,1)S(1)} %convert_bitcast_fusion.refs_0_, bf16[3,576,256]{2,1,0:T(8,128)(2,1)S(1)} %shard_map.87.refs_1_, bf16[576,256]{1,0:T(8,128)(2,1)S(1)} %collective-permute-done.3.refs_2_, ...), custom_call_target="tpu_custom_call" | custom-call | tf_op jit(solution)/shard_map/pallas_call | solution.py:62
  27.0 1.7 %collective-permute-done.8 = bf16[384,256]{1,0:T(8,128)(2,1)S(1)} collective-permute-done((bf16[384,256]{1,0:T(8,128)(2,1)S(1)}, bf16[384,256]{1,0:T(8,128)(2,1)S(1)}, u32[]{:S(2)}, u32[]{:S(2)}) %collective-permute-start.8) | collective-permute-done | bytes 196640 | tf_op jit(solution)/shard_map/ppermute | solution.py:27
  28.8 1.7 %collective-permute-start.12 = (bf16[3,576,256]{2,1,0:T(8,128)(2,1)S(1)}, bf16[3,576,256]{2,1,0:T(8,128)(2,1)S(1)}, u32[]{:S(2)}, u32[]{:S(2)}) collective-permute-start(bf16[3,576,256]{2,1,0:T(8,128)(2,1)S(1)} %get-tuple-element.71.refs_0_), channel_id=1, source_target_pairs={{4,0},{0,4},{12,8},{8,12},{20,16},{16,20},{28,24},{24,28},{36,32},... | collective-permute-start | bytes 2654216 | tf_op jit(solution)/shard_map/ppermute | solution.py:27
  30.5 3.6 %collective-permute-start.16 = (bf16[384,256]{1,0:T(8,128)(2,1)S(1)}, bf16[384,256]{1,0:T(8,128)(2,1)S(1)}, u32[]{:S(2)}, u32[]{:S(2)}) collective-permute-start(bf16[384,256]{1,0:T(8,128)(2,1)S(1)} %collective-permute-done.8), channel_id=1, source_target_pairs={{8,0},{36,4},{16,8},{44,12},{24,16},{52,20},{0,24},{60,28},{40,32}... | collective-permute-start | bytes 589832 | tf_op jit(solution)/shard_map/ppermute | solution.py:27
  34.0 2.7 %collective-permute-start.10 = (bf16[288,256]{1,0:T(8,128)(2,1)S(1)}, bf16[288,256]{1,0:T(8,128)(2,1)S(1)}, u32[]{:S(2)}, u32[]{:S(2)}) collective-permute-start(bf16[288,256]{1,0:T(8,128)(2,1)S(1)} %get-tuple-element.69), channel_id=1, source_target_pairs={{8,0},{12,4},{16,8},{20,12},{24,16},{28,20},{0,24},{4,28},{40,32},... | collective-permute-start | bytes 442376 | tf_op jit(solution)/shard_map/ppermute | solution.py:27
  40.8 2.2 %collective-permute-start.13 = (bf16[576,256]{1,0:T(8,128)(2,1)S(1)}, bf16[576,256]{1,0:T(8,128)(2,1)S(1)}, u32[]{:S(2)}, u32[]{:S(2)}) collective-permute-start(bf16[576,256]{1,0:T(8,128)(2,1)S(1)} %pad_maximum_fusion.2.refs_0_), channel_id=1, source_target_pairs={{4,0},{0,4},{12,8},{8,12},{20,16},{16,20},{28,24},{24,28},{36,32},... | collective-permute-start | bytes 884744 | tf_op jit(solution)/shard_map/ppermute | solution.py:27
  44.2 4.1 %shard_map.93 = (f32[576,256]{1,0:T(8,128)}, f32[8,128,384]{2,1,0:T(8,128)S(1)}, bf16[4,128,384]{2,1,0:T(8,128)(2,1)S(1)}, bf16[4,128,384]{2,1,0:T(8,128)(2,1)S(1)}) custom-call(s32[2]{0:T(128)S(1)} %copy-done.2, bf16[576,9216]{1,0:T(8,128)(2,1)S(1)} %shard_map.86.inv_ref, bf16[576,3072]{1,0:T(8,128)(2,1)S(1)} %shard_map.89.coupling_ref, ...), custom_call_target="tpu_custom_call" | custom-call | tf_op jit(solution)/shard_map/pallas_call | solution.py:62
  52.7 4.6 %collective-permute-start.19 = (bf16[4,384,256]{2,1,0:T(8,128)(2,1)S(1)}, bf16[4,384,256]{2,1,0:T(8,128)(2,1)}, u32[]{:S(2)}, u32[]{:S(2)}) collective-permute-start(bf16[4,384,256]{2,1,0:T(8,128)(2,1)S(1)} %pad_maximum_fusion.refs_0_), channel_id=1, source_target_pairs={{4,0},{0,4},{12,8},{8,12},{20,16},{16,20},{28,24},{24,28},{36,32},... | collective-permute-start | bytes 2359304 | tf_op jit(solution)/shard_map/ppermute | solution.py:27
  57.8 3.6 %all-to-all-start = ((bf16[8,128,384]{2,1,0:T(8,128)(2,1)}), bf16[8,128,384]{2,1,0:T(8,128)(2,1)S(1)}, u32[]{:S(2)}, u32[]{:S(2)}) async-start(bf16[8,128,384]{2,1,0:T(8,128)(2,1)} %add_convert_fusion), calls=%async_computation | async-start | bytes 1572864 | tf_op jit(solution)/shard_map/all_to_all | solution.py:408
  61.4 2.7 %collective-permute-start.25 = (bf16[2,384,256]{2,1,0:T(8,128)(2,1)}, bf16[2,384,256]{2,1,0:T(8,128)(2,1)S(1)}, u32[]{:S(2)}, u32[]{:S(2)}) collective-permute-start(bf16[2,384,256]{2,1,0:T(8,128)(2,1)} %copy-done.4), channel_id=1, source_target_pairs={{32,0},{12,4},{40,8},{20,12},{48,16},{28,20},{56,24},{4,28},{64,32... | collective-permute-start | bytes 1179656 | tf_op jit(solution)/shard_map/ppermute | solution.py:27
  64.0 10.4 %all-to-all-done.pieces_ref = bf16[8,128,384]{2,1,0:T(8,128)(2,1)S(1)} async-done(((bf16[8,128,384]{2,1,0:T(8,128)(2,1)}), bf16[8,128,384]{2,1,0:T(8,128)(2,1)S(1)}, u32[]{:S(2)}, u32[]{:S(2)}) %all-to-all-start) | async-done | bytes 786464 | tf_op jit(solution)/shard_map/all_to_all | solution.py:408
  76.8 3.8 %shard_map.96.p_ref = bf16[384,12288]{1,0:T(8,128)(2,1)S(1)} custom-call(bf16[384,12288]{1,0:T(8,128)(2,1)} %refs_0_.3), custom_call_target="tpu_custom_call" | custom-call | tf_op jit(solution)/shard_map/pallas_call | solution.py:62
  81.2 2.8 %collective-permute-start.27 = (bf16[2,384,256]{2,1,0:T(8,128)(2,1)S(1)}, bf16[2,384,256]{2,1,0:T(8,128)(2,1)S(1)}, u32[]{:S(2)}, u32[]{:S(2)}) collective-permute-start(bf16[2,384,256]{2,1,0:T(8,128)(2,1)S(1)} %collective-permute-done.25.refs_6_), channel_id=1, source_target_pairs={{4,0},{0,4},{12,8},{8,12},{20,16},{16,20},{28,24},{24,28},{36,32},... | collective-permute-start | bytes 1179656 | tf_op jit(solution)/shard_map/ppermute | solution.py:27
  84.0 2.0 %collective-permute-start.29 = (bf16[4,384,128]{2,1,0:T(8,128)(2,1)S(1)}, bf16[4,384,128]{2,1,0:T(8,128)(2,1)S(1)}, u32[]{:S(2)}, u32[]{:S(2)}) collective-permute-start(bf16[4,384,128]{2,1,0:T(8,128)(2,1)S(1)} %pad_maximum_fusion.1.refs_0_), channel_id=1, source_target_pairs={{32,0},{12,4},{40,8},{20,12},{48,16},{28,20},{56,24},{4,28},{64,32... | collective-permute-start | bytes 1179656 | tf_op jit(solution)/shard_map/ppermute | solution.py:27
  86.1 2.5 %collective-permute-start.32 = (bf16[4,384,128]{2,1,0:T(8,128)(2,1)S(1)}, bf16[4,384,128]{2,1,0:T(8,128)(2,1)S(1)}, u32[]{:S(2)}, u32[]{:S(2)}) collective-permute-start(bf16[4,384,128]{2,1,0:T(8,128)(2,1)S(1)} %pad_maximum_fusion.1.refs_0_), channel_id=1, source_target_pairs={{64,0},{20,4},{72,8},{28,12},{80,16},{4,20},{88,24},{12,28},{96,32... | collective-permute-start | bytes 1179656 | tf_op jit(solution)/shard_map/ppermute | solution.py:27
  88.6 5.5 %shard_map.97 = (f32[384,256]{1,0:T(8,128)S(1)}, bf16[384,6144]{1,0:T(8,128)(2,1)S(1)}) custom-call(s32[2,24]{1,0:T(2,128)S(1)} %copy-done.1, bf16[384,12288]{1,0:T(8,128)(2,1)S(1)} %shard_map.96.p_ref, bf16[4,384,256]{2,1,0:T(8,128)(2,1)S(1)} %pad_maximum_fusion.refs_0_, bf16[4,384,256]{2,1,0:T(8,128)(2,1)S(1)} %collective-permute-done.17.up_ref.refs_1_, ...), custom_call_target="tpu_custom_call" | custom-call | bytes 3670016 | tf_op jit(solution)/shard_map/pallas_call | solution.py:62
  94.9 4.8 %collective-permute-start.34 = (bf16[4,384,128]{2,1,0:T(8,128)(2,1)S(1)}, bf16[4,384,128]{2,1,0:T(8,128)(2,1)S(1)}, u32[]{:S(2)}, u32[]{:S(2)}) collective-permute-start(bf16[4,384,128]{2,1,0:T(8,128)(2,1)S(1)} %collective-permute-done.31.refs_2_), channel_id=1, source_target_pairs={{4,0},{0,4},{12,8},{8,12},{20,16},{16,20},{28,24},{24,28},{36,32},... | collective-permute-start | bytes 1179656 | tf_op jit(solution)/shard_map/ppermute | solution.py:27
  101.6 2.6 %shard_map.98 = f32[256,384]{1,0:T(8,128)} custom-call(f32[384,256]{1,0:T(8,128)S(1)} %get-tuple-element.104.base_ref, bf16[384,6144]{1,0:T(8,128)(2,1)S(1)} %get-tuple-element.105.p_ref, bf16[4,384,128]{2,1,0:T(8,128)(2,1)S(1)} %pad_maximum_fusion.1.refs_0_, bf16[4,384,128]{2,1,0:T(8,128)(2,1)S(1)} %collective-permute-done.29.refs_1_, ...), custom_call_target="tpu_custom_call" | custom-call | tf_op jit(solution)/shard_map/pallas_call | solution.py:62
  (78 shorter events, 24.4 us)
Async XLA Ops:
  1.7 10.4 %collective-permute-start = (bf16[576,256]{1,0:T(8,128)(2,1)S(1)}, bf16[576,256]{1,0:T(8,128)(2,1)S(1)}, u32[]{:S(2)}, u32[]{:S(2)}) collective-permute-start(bf16[576,256]{1,0:T(8,128)(2,1)S(1)} %convert_bitcast_fusion.refs_0_), channel_id=1, source_target_pairs={{8,0},{12,4},{16,8},{20,12},{24,16},{28,20},{0,24},{4,28},{40,32},... | collective-permute-start | bytes 884744 | tf_op jit(solution)/shard_map/ppermute | solution.py:27
  5.1 8.8 %collective-permute-start.1 = (bf16[576,256]{1,0:T(8,128)(2,1)S(1)}, bf16[576,256]{1,0:T(8,128)(2,1)S(1)}, u32[]{:S(2)}, u32[]{:S(2)}) collective-permute-start(bf16[576,256]{1,0:T(8,128)(2,1)S(1)} %convert_bitcast_fusion.refs_0_), channel_id=1, source_target_pairs={{24,0},{28,4},{0,8},{4,12},{8,16},{12,20},{16,24},{20,28},{56,32},... | collective-permute-start | bytes 884744 | tf_op jit(solution)/shard_map/ppermute | solution.py:27
  5.1 8.8 %collective-permute-start.2 = (bf16[576,256]{1,0:T(8,128)(2,1)S(1)}, bf16[576,256]{1,0:T(8,128)(2,1)S(1)}, u32[]{:S(2)}, u32[]{:S(2)}) collective-permute-start(bf16[576,256]{1,0:T(8,128)(2,1)S(1)} %convert_bitcast_fusion.refs_0_), channel_id=1, source_target_pairs={{32,0},{36,4},{40,8},{44,12},{48,16},{52,20},{56,24},{60,28},{0,32... | collective-permute-start | bytes 884744 | tf_op jit(solution)/shard_map/ppermute | solution.py:27
  6.8 7.1 %collective-permute-start.3 = (bf16[576,256]{1,0:T(8,128)(2,1)S(1)}, bf16[576,256]{1,0:T(8,128)(2,1)S(1)}, u32[]{:S(2)}, u32[]{:S(2)}) collective-permute-start(bf16[576,256]{1,0:T(8,128)(2,1)S(1)} %convert_bitcast_fusion.refs_0_), channel_id=1, source_target_pairs={{4,0},{0,4},{12,8},{8,12},{20,16},{16,20},{28,24},{24,28},{36,32},... | collective-permute-start | bytes 884744 | tf_op jit(solution)/shard_map/ppermute | solution.py:27
  15.9 9.9 %collective-permute-start.4 = (bf16[576,256]{1,0:T(8,128)(2,1)S(1)}, bf16[576,256]{1,0:T(8,128)(2,1)S(1)}, u32[]{:S(2)}, u32[]{:S(2)}) collective-permute-start(bf16[576,256]{1,0:T(8,128)(2,1)S(1)} %collective-permute-done.refs_0_), channel_id=1, source_target_pairs={{8,0},{12,4},{16,8},{20,12},{24,16},{28,20},{0,24},{4,28},{40,32},... | collective-permute-start | bytes 884744 | tf_op jit(solution)/shard_map/ppermute | solution.py:27
  17.6 9.5 %collective-permute-start.5 = (bf16[576,256]{1,0:T(8,128)(2,1)S(1)}, bf16[576,256]{1,0:T(8,128)(2,1)S(1)}, u32[]{:S(2)}, u32[]{:S(2)}) collective-permute-start(bf16[576,256]{1,0:T(8,128)(2,1)S(1)} %collective-permute-done.2.refs_2_), channel_id=1, source_target_pairs={{24,0},{28,4},{0,8},{4,12},{8,16},{12,20},{16,24},{20,28},{56,32},... | collective-permute-start | bytes 884744 | tf_op jit(solution)/shard_map/ppermute | solution.py:27
  17.6 9.5 %collective-permute-start.6 = (bf16[576,256]{1,0:T(8,128)(2,1)S(1)}, bf16[576,256]{1,0:T(8,128)(2,1)S(1)}, u32[]{:S(2)}, u32[]{:S(2)}) collective-permute-start(bf16[576,256]{1,0:T(8,128)(2,1)S(1)} %collective-permute-done.refs_0_), channel_id=1, source_target_pairs={{32,0},{36,4},{40,8},{44,12},{48,16},{52,20},{56,24},{60,28},{0,32... | collective-permute-start | bytes 884744 | tf_op jit(solution)/shard_map/ppermute | solution.py:27
  19.2 9.5 %collective-permute-start.8 = (bf16[384,256]{1,0:T(8,128)(2,1)S(1)}, bf16[384,256]{1,0:T(8,128)(2,1)S(1)}, u32[]{:S(2)}, u32[]{:S(2)}) collective-permute-start(bf16[384,256]{1,0:T(8,128)(2,1)S(1)} %shard_map.90), channel_id=1, source_target_pairs={{8,0},{36,4},{16,8},{44,12},{24,16},{52,20},{0,24},{60,28},{40,32}... | collective-permute-start | bytes 589832 | tf_op jit(solution)/shard_map/ppermute | solution.py:27
  21.9 6.8 %collective-permute-start.9 = (bf16[384,256]{1,0:T(8,128)(2,1)S(1)}, bf16[384,256]{1,0:T(8,128)(2,1)S(1)}, u32[]{:S(2)}, u32[]{:S(2)}) collective-permute-start(bf16[384,256]{1,0:T(8,128)(2,1)S(1)} %shard_map.90), channel_id=1, source_target_pairs={{24,0},{100,4},{0,8},{108,12},{8,16},{116,20},{16,24},{124,28},{56... | collective-permute-start | bytes 589832 | tf_op jit(solution)/shard_map/ppermute | solution.py:27
  28.8 10.5 %collective-permute-start.12 = (bf16[3,576,256]{2,1,0:T(8,128)(2,1)S(1)}, bf16[3,576,256]{2,1,0:T(8,128)(2,1)S(1)}, u32[]{:S(2)}, u32[]{:S(2)}) collective-permute-start(bf16[3,576,256]{2,1,0:T(8,128)(2,1)S(1)} %get-tuple-element.71.refs_0_), channel_id=1, source_target_pairs={{4,0},{0,4},{12,8},{8,12},{20,16},{16,20},{28,24},{24,28},{36,32},... | collective-permute-start | bytes 2654216 | tf_op jit(solution)/shard_map/ppermute | solution.py:27
  30.5 6.3 %collective-permute-start.16 = (bf16[384,256]{1,0:T(8,128)(2,1)S(1)}, bf16[384,256]{1,0:T(8,128)(2,1)S(1)}, u32[]{:S(2)}, u32[]{:S(2)}) collective-permute-start(bf16[384,256]{1,0:T(8,128)(2,1)S(1)} %collective-permute-done.8), channel_id=1, source_target_pairs={{8,0},{36,4},{16,8},{44,12},{24,16},{52,20},{0,24},{60,28},{40,32}... | collective-permute-start | bytes 589832 | tf_op jit(solution)/shard_map/ppermute | solution.py:27
  36.8 12.0 %collective-permute-start.17 = (bf16[4,384,256]{2,1,0:T(8,128)(2,1)S(1)}, bf16[4,384,256]{2,1,0:T(8,128)(2,1)S(1)}, u32[]{:S(2)}, u32[]{:S(2)}) collective-permute-start(bf16[4,384,256]{2,1,0:T(8,128)(2,1)S(1)} %pad_maximum_fusion.refs_0_), channel_id=1, source_target_pairs={{32,0},{12,4},{40,8},{20,12},{48,16},{28,20},{56,24},{4,28},{64,32... | collective-permute-start | bytes 2359304 | tf_op jit(solution)/shard_map/ppermute | solution.py:27
  37.7 12.3 %collective-permute-start.18 = (bf16[4,384,256]{2,1,0:T(8,128)(2,1)S(1)}, bf16[4,384,256]{2,1,0:T(8,128)(2,1)S(1)}, u32[]{:S(2)}, u32[]{:S(2)}) collective-permute-start(bf16[4,384,256]{2,1,0:T(8,128)(2,1)S(1)} %pad_maximum_fusion.refs_0_), channel_id=1, source_target_pairs={{96,0},{28,4},{104,8},{4,12},{112,16},{12,20},{120,24},{20,28},{0,... | collective-permute-start | bytes 2359304 | tf_op jit(solution)/shard_map/ppermute | solution.py:27
  52.7 21.9 %collective-permute-start.19 = (bf16[4,384,256]{2,1,0:T(8,128)(2,1)S(1)}, bf16[4,384,256]{2,1,0:T(8,128)(2,1)}, u32[]{:S(2)}, u32[]{:S(2)}) collective-permute-start(bf16[4,384,256]{2,1,0:T(8,128)(2,1)S(1)} %pad_maximum_fusion.refs_0_), channel_id=1, source_target_pairs={{4,0},{0,4},{12,8},{8,12},{20,16},{16,20},{28,24},{24,28},{36,32},... | collective-permute-start | bytes 2359304 | tf_op jit(solution)/shard_map/ppermute | solution.py:27
  57.3 17.4 %collective-permute-start.20 = (bf16[4,384,256]{2,1,0:T(8,128)(2,1)S(1)}, bf16[4,384,256]{2,1,0:T(8,128)(2,1)}, u32[]{:S(2)}, u32[]{:S(2)}) collective-permute-start(bf16[4,384,256]{2,1,0:T(8,128)(2,1)S(1)} %collective-permute-done.17.up_ref.refs_1_), channel_id=1, source_target_pairs={{4,0},{0,4},{12,8},{8,12},{20,16},{16,20},{28,24},{24,28},{36,32},... | collective-permute-start | bytes 2359304 | tf_op jit(solution)/shard_map/ppermute | solution.py:27
  57.3 17.4 %collective-permute-start.21 = (bf16[4,384,256]{2,1,0:T(8,128)(2,1)S(1)}, bf16[4,384,256]{2,1,0:T(8,128)(2,1)}, u32[]{:S(2)}, u32[]{:S(2)}) collective-permute-start(bf16[4,384,256]{2,1,0:T(8,128)(2,1)S(1)} %collective-permute-done.18.down_ref.refs_2_), channel_id=1, source_target_pairs={{4,0},{0,4},{12,8},{8,12},{20,16},{16,20},{28,24},{24,28},{36,32},... | collective-permute-start | bytes 2359304 | tf_op jit(solution)/shard_map/ppermute | solution.py:27
  57.8 16.7 %all-to-all-start = ((bf16[8,128,384]{2,1,0:T(8,128)(2,1)}), bf16[8,128,384]{2,1,0:T(8,128)(2,1)S(1)}, u32[]{:S(2)}, u32[]{:S(2)}) async-start(bf16[8,128,384]{2,1,0:T(8,128)(2,1)} %add_convert_fusion), calls=%async_computation | async-start | bytes 1572864 | tf_op jit(solution)/shard_map/all_to_all | solution.py:408
  61.4 19.3 %collective-permute-start.25 = (bf16[2,384,256]{2,1,0:T(8,128)(2,1)}, bf16[2,384,256]{2,1,0:T(8,128)(2,1)S(1)}, u32[]{:S(2)}, u32[]{:S(2)}) collective-permute-start(bf16[2,384,256]{2,1,0:T(8,128)(2,1)} %copy-done.4), channel_id=1, source_target_pairs={{32,0},{12,4},{40,8},{20,12},{48,16},{28,20},{56,24},{4,28},{64,32... | collective-permute-start | bytes 1179656 | tf_op jit(solution)/shard_map/ppermute | solution.py:27
  64.0 16.6 %collective-permute-start.26 = (bf16[2,384,256]{2,1,0:T(8,128)(2,1)}, bf16[2,384,256]{2,1,0:T(8,128)(2,1)}, u32[]{:S(2)}, u32[]{:S(2)}) collective-permute-start(bf16[2,384,256]{2,1,0:T(8,128)(2,1)} %copy-done.3), channel_id=1, source_target_pairs={{96,0},{28,4},{104,8},{4,12},{112,16},{12,20},{120,24},{20,28},{0,... | collective-permute-start | bytes 1179656 | tf_op jit(solution)/shard_map/ppermute | solution.py:27
  84.0 10.9 %collective-permute-start.29 = (bf16[4,384,128]{2,1,0:T(8,128)(2,1)S(1)}, bf16[4,384,128]{2,1,0:T(8,128)(2,1)S(1)}, u32[]{:S(2)}, u32[]{:S(2)}) collective-permute-start(bf16[4,384,128]{2,1,0:T(8,128)(2,1)S(1)} %pad_maximum_fusion.1.refs_0_), channel_id=1, source_target_pairs={{32,0},{12,4},{40,8},{20,12},{48,16},{28,20},{56,24},{4,28},{64,32... | collective-permute-start | bytes 1179656 | tf_op jit(solution)/shard_map/ppermute | solution.py:27
  86.0 8.9 %collective-permute-start.30 = (bf16[4,384,128]{2,1,0:T(8,128)(2,1)S(1)}, bf16[4,384,128]{2,1,0:T(8,128)(2,1)S(1)}, u32[]{:S(2)}, u32[]{:S(2)}) collective-permute-start(bf16[4,384,128]{2,1,0:T(8,128)(2,1)S(1)} %pad_maximum_fusion.1.refs_0_), channel_id=1, source_target_pairs={{4,0},{0,4},{12,8},{8,12},{20,16},{16,20},{28,24},{24,28},{36,32},... | collective-permute-start | bytes 1179656 | tf_op jit(solution)/shard_map/ppermute | solution.py:27
  86.0 8.9 %collective-permute-start.31 = (bf16[4,384,128]{2,1,0:T(8,128)(2,1)S(1)}, bf16[4,384,128]{2,1,0:T(8,128)(2,1)S(1)}, u32[]{:S(2)}, u32[]{:S(2)}) collective-permute-start(bf16[4,384,128]{2,1,0:T(8,128)(2,1)S(1)} %pad_maximum_fusion.1.refs_0_), channel_id=1, source_target_pairs={{96,0},{28,4},{104,8},{4,12},{112,16},{12,20},{120,24},{20,28},{0,... | collective-permute-start | bytes 1179656 | tf_op jit(solution)/shard_map/ppermute | solution.py:27
  86.1 13.6 %collective-permute-start.32 = (bf16[4,384,128]{2,1,0:T(8,128)(2,1)S(1)}, bf16[4,384,128]{2,1,0:T(8,128)(2,1)S(1)}, u32[]{:S(2)}, u32[]{:S(2)}) collective-permute-start(bf16[4,384,128]{2,1,0:T(8,128)(2,1)S(1)} %pad_maximum_fusion.1.refs_0_), channel_id=1, source_target_pairs={{64,0},{20,4},{72,8},{28,12},{80,16},{4,20},{88,24},{12,28},{96,32... | collective-permute-start | bytes 1179656 | tf_op jit(solution)/shard_map/ppermute | solution.py:27
  94.9 6.1 %collective-permute-start.34 = (bf16[4,384,128]{2,1,0:T(8,128)(2,1)S(1)}, bf16[4,384,128]{2,1,0:T(8,128)(2,1)S(1)}, u32[]{:S(2)}, u32[]{:S(2)}) collective-permute-start(bf16[4,384,128]{2,1,0:T(8,128)(2,1)S(1)} %collective-permute-done.31.refs_2_), channel_id=1, source_target_pairs={{4,0},{0,4},{12,8},{8,12},{20,16},{16,20},{28,24},{24,28},{36,32},... | collective-permute-start | bytes 1179656 | tf_op jit(solution)/shard_map/ppermute | solution.py:27
  (18 other events, 95.9 us)

commit v6 on v5

--- a/solution.py
+++ b/solution.py
@@ -175,12 +175,14 @@
         mine = pl.ds(pl.multiple_of(core * half, half), half)
         others = pl.ds(pl.multiple_of((1 - core) * half, half), half)
         solved = jnp.concatenate([solved_ref[mine], solved_ref[others]], axis=0)
-        for i in range(pieces):
-            update = jnp.dot(
-                solved, coupling_ref[:, i * width : (i + 1) * width], preferred_element_type=F32
-            )
-            keep_ref[i] = update[:half]
-            give_refs[2 * i // pieces][i % (pieces // 2)] = update[half:].astype(BF)
+        per_half = pieces // 2
+        for k in range(2):
+            columns_k = slice(k * per_half * width, (k + 1) * per_half * width)
+            update = jnp.dot(solved, coupling_ref[:, columns_k], preferred_element_type=F32)
+            for i in range(per_half):
+                piece = update[:, i * width : (i + 1) * width]
+                keep_ref[k * per_half + i] = piece[:half]
+                give_refs[k][i] = piece[half:].astype(BF)
 
     return call(
         kernel,

time: 104 us -> 104 us (level)
  transfers between devices with their start and end apart: 37 -> 37, of which waited for: 11 -> 11; matrix products, arithmetic and copies ran while one was open for 0% -> 0% of each run, Pallas kernels for 22% -> 21%
where the time goes in v6:
time: 104 us
  starting transfers between devices  52 us (50%)
  Pallas kernels  25 us (24%)
  waiting for transfers between devices  22.4 us (22%)
  other arithmetic  2.37 us (2%)
  local copies, waits for them, and re-layouts  1.51 us (1%)
    ppermute x36, starting transfers between devices, receive(): return lax.ppermute(value, 'wide', pairs)  48.4 us
    pallas_call x13, Pallas kernels, call(): pl.pallas_call(kernel, in_specs=specs, out_specs=jax.tree.map(lambda _: V...  25 us
    ppermute x36, waiting for transfers between devices, receive(): return lax.ppermute(value, 'wide', pairs)  12 us
    all_to_all x1, waiting for transfers between devices, on_device(): lax.all_to_all(chip_sum, 'wide', split_axis=0, concat_axis=0, axis_index_...  10.4 us
    all_to_all x1, starting transfers between devices, on_device(): lax.all_to_all(chip_sum, 'wide', split_axis=0, concat_axis=0, axis_index_...  3.57 us
  transfers between devices with their start and end apart: 37, of which 11 were waited for; matrix products, arithmetic and copies ran while one was open for 0% of the time, Pallas kernels for 21%

profile of v6, /device:TPU:1, one launch (start us, length us, event | category | flops | bytes accessed | tf_op | source)
XLA Modules:
  0.0 104.2 jit_solution(6841243002655949384)
XLA Ops:
  1.7 3.4 %collective-permute-start = (bf16[576,256]{1,0:T(8,128)(2,1)S(1)}, bf16[576,256]{1,0:T(8,128)(2,1)S(1)}, u32[]{:S(2)}, u32[]{:S(2)}) collective-permute-start(bf16[576,256]{1,0:T(8,128)(2,1)S(1)} %convert_bitcast_fusion.refs_0_), channel_id=1, source_target_pairs={{8,0},{12,4},{16,8},{20,12},{24,16},{28,20},{0,24},{4,28},{40,32},... | collective-permute-start | bytes 884744 | tf_op jit(solution)/shard_map/ppermute | solution.py:27
  8.0 4.1 %shard_map.86.inv_ref = bf16[576,9216]{1,0:T(8,128)(2,1)S(1)} custom-call(bf16[576,9216]{1,0:T(8,128)(2,1)} %refs_0_.1), custom_call_target="tpu_custom_call" | custom-call | tf_op jit(solution)/shard_map/pallas_call | solution.py:62
  12.1 1.8 %collective-permute-done.1.refs_1_ = bf16[576,256]{1,0:T(8,128)(2,1)S(1)} collective-permute-done((bf16[576,256]{1,0:T(8,128)(2,1)S(1)}, bf16[576,256]{1,0:T(8,128)(2,1)S(1)}, u32[]{:S(2)}, u32[]{:S(2)}) %collective-permute-start.1) | collective-permute-done | bytes 294944 | tf_op jit(solution)/shard_map/ppermute | solution.py:27
  14.0 1.9 %collective-permute-start.7 = (bf16[3,576,256]{2,1,0:T(8,128)(2,1)S(1)}, bf16[3,576,256]{2,1,0:T(8,128)(2,1)S(1)}, u32[]{:S(2)}, u32[]{:S(2)}) collective-permute-start(bf16[3,576,256]{2,1,0:T(8,128)(2,1)S(1)} %shard_map.87.refs_1_), channel_id=1, source_target_pairs={{4,0},{0,4},{12,8},{8,12},{20,16},{16,20},{28,24},{24,28},{36,32},... | collective-permute-start | bytes 2654216 | tf_op jit(solution)/shard_map/ppermute | solution.py:27
  19.2 2.8 %collective-permute-start.8 = (bf16[384,256]{1,0:T(8,128)(2,1)S(1)}, bf16[384,256]{1,0:T(8,128)(2,1)S(1)}, u32[]{:S(2)}, u32[]{:S(2)}) collective-permute-start(bf16[384,256]{1,0:T(8,128)(2,1)S(1)} %shard_map.90), channel_id=1, source_target_pairs={{8,0},{36,4},{16,8},{44,12},{24,16},{52,20},{0,24},{60,28},{40,32}... | collective-permute-start | bytes 589832 | tf_op jit(solution)/shard_map/ppermute | solution.py:27
  21.9 2.0 %shard_map.89.coupling_ref = bf16[576,3072]{1,0:T(8,128)(2,1)S(1)} custom-call(bf16[576,3072]{1,0:T(8,128)(2,1)} %refs_0_.2), custom_call_target="tpu_custom_call" | custom-call | tf_op jit(solution)/shard_map/pallas_call | solution.py:62
  23.9 1.9 %shard_map.88.refs_2_ = f32[576,256]{1,0:T(8,128)S(1)} custom-call(bf16[576,9216]{1,0:T(8,128)(2,1)S(1)} %shard_map.86.inv_ref, bf16[576,256]{1,0:T(8,128)(2,1)S(1)} %convert_bitcast_fusion.refs_0_, bf16[3,576,256]{2,1,0:T(8,128)(2,1)S(1)} %shard_map.87.refs_1_, bf16[576,256]{1,0:T(8,128)(2,1)S(1)} %collective-permute-done.3.refs_2_, ...), custom_call_target="tpu_custom_call" | custom-call | tf_op jit(solution)/shard_map/pallas_call | solution.py:62
  27.0 1.7 %collective-permute-done.8 = bf16[384,256]{1,0:T(8,128)(2,1)S(1)} collective-permute-done((bf16[384,256]{1,0:T(8,128)(2,1)S(1)}, bf16[384,256]{1,0:T(8,128)(2,1)S(1)}, u32[]{:S(2)}, u32[]{:S(2)}) %collective-permute-start.8) | collective-permute-done | bytes 196640 | tf_op jit(solution)/shard_map/ppermute | solution.py:27
  30.5 3.6 %collective-permute-start.16 = (bf16[384,256]{1,0:T(8,128)(2,1)S(1)}, bf16[384,256]{1,0:T(8,128)(2,1)S(1)}, u32[]{:S(2)}, u32[]{:S(2)}) collective-permute-start(bf16[384,256]{1,0:T(8,128)(2,1)S(1)} %collective-permute-done.8), channel_id=1, source_target_pairs={{8,0},{36,4},{16,8},{44,12},{24,16},{52,20},{0,24},{60,28},{40,32}... | collective-permute-start | bytes 589832 | tf_op jit(solution)/shard_map/ppermute | solution.py:27
  34.0 2.7 %collective-permute-start.10 = (bf16[288,256]{1,0:T(8,128)(2,1)S(1)}, bf16[288,256]{1,0:T(8,128)(2,1)S(1)}, u32[]{:S(2)}, u32[]{:S(2)}) collective-permute-start(bf16[288,256]{1,0:T(8,128)(2,1)S(1)} %get-tuple-element.69), channel_id=1, source_target_pairs={{8,0},{12,4},{16,8},{20,12},{24,16},{28,20},{0,24},{4,28},{40,32},... | collective-permute-start | bytes 442376 | tf_op jit(solution)/shard_map/ppermute | solution.py:27
  40.8 2.2 %collective-permute-start.13 = (bf16[576,256]{1,0:T(8,128)(2,1)S(1)}, bf16[576,256]{1,0:T(8,128)(2,1)S(1)}, u32[]{:S(2)}, u32[]{:S(2)}) collective-permute-start(bf16[576,256]{1,0:T(8,128)(2,1)S(1)} %pad_maximum_fusion.2.refs_0_), channel_id=1, source_target_pairs={{4,0},{0,4},{12,8},{8,12},{20,16},{16,20},{28,24},{24,28},{36,32},... | collective-permute-start | bytes 884744 | tf_op jit(solution)/shard_map/ppermute | solution.py:27
  44.2 3.2 %shard_map.93 = (f32[576,256]{1,0:T(8,128)}, f32[8,128,384]{2,1,0:T(8,128)S(1)}, bf16[4,128,384]{2,1,0:T(8,128)(2,1)S(1)}, bf16[4,128,384]{2,1,0:T(8,128)(2,1)S(1)}) custom-call(s32[2]{0:T(128)S(1)} %copy-done.2, bf16[576,9216]{1,0:T(8,128)(2,1)S(1)} %shard_map.86.inv_ref, bf16[576,3072]{1,0:T(8,128)(2,1)S(1)} %shard_map.89.coupling_ref, ...), custom_call_target="tpu_custom_call" | custom-call | tf_op jit(solution)/shard_map/pallas_call | solution.py:62
  48.1 2.0 %collective-permute-done.18.down_ref.refs_2_ = bf16[4,384,256]{2,1,0:T(8,128)(2,1)S(1)} collective-permute-done((bf16[4,384,256]{2,1,0:T(8,128)(2,1)S(1)}, bf16[4,384,256]{2,1,0:T(8,128)(2,1)S(1)}, u32[]{:S(2)}, u32[]{:S(2)}) %collective-permute-start.18) | collective-permute-done | bytes 786464 | tf_op jit(solution)/shard_map/ppermute | solution.py:27
  52.7 4.6 %collective-permute-start.19 = (bf16[4,384,256]{2,1,0:T(8,128)(2,1)S(1)}, bf16[4,384,256]{2,1,0:T(8,128)(2,1)}, u32[]{:S(2)}, u32[]{:S(2)}) collective-permute-start(bf16[4,384,256]{2,1,0:T(8,128)(2,1)S(1)} %pad_maximum_fusion.refs_0_), channel_id=1, source_target_pairs={{4,0},{0,4},{12,8},{8,12},{20,16},{16,20},{28,24},{24,28},{36,32},... | collective-permute-start | bytes 2359304 | tf_op jit(solution)/shard_map/ppermute | solution.py:27
  57.8 3.6 %all-to-all-start = ((bf16[8,128,384]{2,1,0:T(8,128)(2,1)}), bf16[8,128,384]{2,1,0:T(8,128)(2,1)S(1)}, u32[]{:S(2)}, u32[]{:S(2)}) async-start(bf16[8,128,384]{2,1,0:T(8,128)(2,1)} %add_convert_fusion), calls=%async_computation | async-start | bytes 1572864 | tf_op jit(solution)/shard_map/all_to_all | solution.py:410
  61.4 2.7 %collective-permute-start.25 = (bf16[2,384,256]{2,1,0:T(8,128)(2,1)}, bf16[2,384,256]{2,1,0:T(8,128)(2,1)S(1)}, u32[]{:S(2)}, u32[]{:S(2)}) collective-permute-start(bf16[2,384,256]{2,1,0:T(8,128)(2,1)} %copy-done.4), channel_id=1, source_target_pairs={{32,0},{12,4},{40,8},{20,12},{48,16},{28,20},{56,24},{4,28},{64,32... | collective-permute-start | bytes 1179656 | tf_op jit(solution)/shard_map/ppermute | solution.py:27
  64.0 10.4 %all-to-all-done.pieces_ref = bf16[8,128,384]{2,1,0:T(8,128)(2,1)S(1)} async-done(((bf16[8,128,384]{2,1,0:T(8,128)(2,1)}), bf16[8,128,384]{2,1,0:T(8,128)(2,1)S(1)}, u32[]{:S(2)}, u32[]{:S(2)}) %all-to-all-start) | async-done | bytes 786464 | tf_op jit(solution)/shard_map/all_to_all | solution.py:410
  76.8 3.8 %shard_map.96.p_ref = bf16[384,12288]{1,0:T(8,128)(2,1)S(1)} custom-call(bf16[384,12288]{1,0:T(8,128)(2,1)} %refs_0_.3), custom_call_target="tpu_custom_call" | custom-call | tf_op jit(solution)/shard_map/pallas_call | solution.py:62
  81.2 2.8 %collective-permute-start.27 = (bf16[2,384,256]{2,1,0:T(8,128)(2,1)S(1)}, bf16[2,384,256]{2,1,0:T(8,128)(2,1)S(1)}, u32[]{:S(2)}, u32[]{:S(2)}) collective-permute-start(bf16[2,384,256]{2,1,0:T(8,128)(2,1)S(1)} %collective-permute-done.25.refs_6_), channel_id=1, source_target_pairs={{4,0},{0,4},{12,8},{8,12},{20,16},{16,20},{28,24},{24,28},{36,32},... | collective-permute-start | bytes 1179656 | tf_op jit(solution)/shard_map/ppermute | solution.py:27
  84.0 2.0 %collective-permute-start.29 = (bf16[4,384,128]{2,1,0:T(8,128)(2,1)S(1)}, bf16[4,384,128]{2,1,0:T(8,128)(2,1)S(1)}, u32[]{:S(2)}, u32[]{:S(2)}) collective-permute-start(bf16[4,384,128]{2,1,0:T(8,128)(2,1)S(1)} %pad_maximum_fusion.1.refs_0_), channel_id=1, source_target_pairs={{32,0},{12,4},{40,8},{20,12},{48,16},{28,20},{56,24},{4,28},{64,32... | collective-permute-start | bytes 1179656 | tf_op jit(solution)/shard_map/ppermute | solution.py:27
  86.1 2.5 %collective-permute-start.32 = (bf16[4,384,128]{2,1,0:T(8,128)(2,1)S(1)}, bf16[4,384,128]{2,1,0:T(8,128)(2,1)S(1)}, u32[]{:S(2)}, u32[]{:S(2)}) collective-permute-start(bf16[4,384,128]{2,1,0:T(8,128)(2,1)S(1)} %pad_maximum_fusion.1.refs_0_), channel_id=1, source_target_pairs={{64,0},{20,4},{72,8},{28,12},{80,16},{4,20},{88,24},{12,28},{96,32... | collective-permute-start | bytes 1179656 | tf_op jit(solution)/shard_map/ppermute | solution.py:27
  88.6 5.5 %shard_map.97 = (f32[384,256]{1,0:T(8,128)S(1)}, bf16[384,6144]{1,0:T(8,128)(2,1)S(1)}) custom-call(s32[2,24]{1,0:T(2,128)S(1)} %copy-done.1, bf16[384,12288]{1,0:T(8,128)(2,1)S(1)} %shard_map.96.p_ref, bf16[4,384,256]{2,1,0:T(8,128)(2,1)S(1)} %pad_maximum_fusion.refs_0_, bf16[4,384,256]{2,1,0:T(8,128)(2,1)S(1)} %collective-permute-done.17.up_ref.refs_1_, ...), custom_call_target="tpu_custom_call" | custom-call | bytes 3670016 | tf_op jit(solution)/shard_map/pallas_call | solution.py:62
  94.9 4.8 %collective-permute-start.34 = (bf16[4,384,128]{2,1,0:T(8,128)(2,1)S(1)}, bf16[4,384,128]{2,1,0:T(8,128)(2,1)S(1)}, u32[]{:S(2)}, u32[]{:S(2)}) collective-permute-start(bf16[4,384,128]{2,1,0:T(8,128)(2,1)S(1)} %collective-permute-done.31.refs_2_), channel_id=1, source_target_pairs={{4,0},{0,4},{12,8},{8,12},{20,16},{16,20},{28,24},{24,28},{36,32},... | collective-permute-start | bytes 1179656 | tf_op jit(solution)/shard_map/ppermute | solution.py:27
  101.6 2.6 %shard_map.98 = f32[256,384]{1,0:T(8,128)} custom-call(f32[384,256]{1,0:T(8,128)S(1)} %get-tuple-element.104.base_ref, bf16[384,6144]{1,0:T(8,128)(2,1)S(1)} %get-tuple-element.105.p_ref, bf16[4,384,128]{2,1,0:T(8,128)(2,1)S(1)} %pad_maximum_fusion.1.refs_0_, bf16[4,384,128]{2,1,0:T(8,128)(2,1)S(1)} %collective-permute-done.29.refs_1_, ...), custom_call_target="tpu_custom_call" | custom-call | tf_op jit(solution)/shard_map/pallas_call | solution.py:62
  (78 shorter events, 25.0 us)
Async XLA Ops:
  1.7 10.4 %collective-permute-start = (bf16[576,256]{1,0:T(8,128)(2,1)S(1)}, bf16[576,256]{1,0:T(8,128)(2,1)S(1)}, u32[]{:S(2)}, u32[]{:S(2)}) collective-permute-start(bf16[576,256]{1,0:T(8,128)(2,1)S(1)} %convert_bitcast_fusion.refs_0_), channel_id=1, source_target_pairs={{8,0},{12,4},{16,8},{20,12},{24,16},{28,20},{0,24},{4,28},{40,32},... | collective-permute-start | bytes 884744 | tf_op jit(solution)/shard_map/ppermute | solution.py:27
  5.1 8.8 %collective-permute-start.1 = (bf16[576,256]{1,0:T(8,128)(2,1)S(1)}, bf16[576,256]{1,0:T(8,128)(2,1)S(1)}, u32[]{:S(2)}, u32[]{:S(2)}) collective-permute-start(bf16[576,256]{1,0:T(8,128)(2,1)S(1)} %convert_bitcast_fusion.refs_0_), channel_id=1, source_target_pairs={{24,0},{28,4},{0,8},{4,12},{8,16},{12,20},{16,24},{20,28},{56,32},... | collective-permute-start | bytes 884744 | tf_op jit(solution)/shard_map/ppermute | solution.py:27
  5.1 8.8 %collective-permute-start.2 = (bf16[576,256]{1,0:T(8,128)(2,1)S(1)}, bf16[576,256]{1,0:T(8,128)(2,1)S(1)}, u32[]{:S(2)}, u32[]{:S(2)}) collective-permute-start(bf16[576,256]{1,0:T(8,128)(2,1)S(1)} %convert_bitcast_fusion.refs_0_), channel_id=1, source_target_pairs={{32,0},{36,4},{40,8},{44,12},{48,16},{52,20},{56,24},{60,28},{0,32... | collective-permute-start | bytes 884744 | tf_op jit(solution)/shard_map/ppermute | solution.py:27
  6.8 7.1 %collective-permute-start.3 = (bf16[576,256]{1,0:T(8,128)(2,1)S(1)}, bf16[576,256]{1,0:T(8,128)(2,1)S(1)}, u32[]{:S(2)}, u32[]{:S(2)}) collective-permute-start(bf16[576,256]{1,0:T(8,128)(2,1)S(1)} %convert_bitcast_fusion.refs_0_), channel_id=1, source_target_pairs={{4,0},{0,4},{12,8},{8,12},{20,16},{16,20},{28,24},{24,28},{36,32},... | collective-permute-start | bytes 884744 | tf_op jit(solution)/shard_map/ppermute | solution.py:27
  15.9 9.9 %collective-permute-start.4 = (bf16[576,256]{1,0:T(8,128)(2,1)S(1)}, bf16[576,256]{1,0:T(8,128)(2,1)S(1)}, u32[]{:S(2)}, u32[]{:S(2)}) collective-permute-start(bf16[576,256]{1,0:T(8,128)(2,1)S(1)} %collective-permute-done.refs_0_), channel_id=1, source_target_pairs={{8,0},{12,4},{16,8},{20,12},{24,16},{28,20},{0,24},{4,28},{40,32},... | collective-permute-start | bytes 884744 | tf_op jit(solution)/shard_map/ppermute | solution.py:27
  17.6 9.5 %collective-permute-start.5 = (bf16[576,256]{1,0:T(8,128)(2,1)S(1)}, bf16[576,256]{1,0:T(8,128)(2,1)S(1)}, u32[]{:S(2)}, u32[]{:S(2)}) collective-permute-start(bf16[576,256]{1,0:T(8,128)(2,1)S(1)} %collective-permute-done.2.refs_2_), channel_id=1, source_target_pairs={{24,0},{28,4},{0,8},{4,12},{8,16},{12,20},{16,24},{20,28},{56,32},... | collective-permute-start | bytes 884744 | tf_op jit(solution)/shard_map/ppermute | solution.py:27
  17.6 9.5 %collective-permute-start.6 = (bf16[576,256]{1,0:T(8,128)(2,1)S(1)}, bf16[576,256]{1,0:T(8,128)(2,1)S(1)}, u32[]{:S(2)}, u32[]{:S(2)}) collective-permute-start(bf16[576,256]{1,0:T(8,128)(2,1)S(1)} %collective-permute-done.refs_0_), channel_id=1, source_target_pairs={{32,0},{36,4},{40,8},{44,12},{48,16},{52,20},{56,24},{60,28},{0,32... | collective-permute-start | bytes 884744 | tf_op jit(solution)/shard_map/ppermute | solution.py:27
  19.2 9.5 %collective-permute-start.8 = (bf16[384,256]{1,0:T(8,128)(2,1)S(1)}, bf16[384,256]{1,0:T(8,128)(2,1)S(1)}, u32[]{:S(2)}, u32[]{:S(2)}) collective-permute-start(bf16[384,256]{1,0:T(8,128)(2,1)S(1)} %shard_map.90), channel_id=1, source_target_pairs={{8,0},{36,4},{16,8},{44,12},{24,16},{52,20},{0,24},{60,28},{40,32}... | collective-permute-start | bytes 589832 | tf_op jit(solution)/shard_map/ppermute | solution.py:27
  21.9 6.8 %collective-permute-start.9 = (bf16[384,256]{1,0:T(8,128)(2,1)S(1)}, bf16[384,256]{1,0:T(8,128)(2,1)S(1)}, u32[]{:S(2)}, u32[]{:S(2)}) collective-permute-start(bf16[384,256]{1,0:T(8,128)(2,1)S(1)} %shard_map.90), channel_id=1, source_target_pairs={{24,0},{100,4},{0,8},{108,12},{8,16},{116,20},{16,24},{124,28},{56... | collective-permute-start | bytes 589832 | tf_op jit(solution)/shard_map/ppermute | solution.py:27
  28.8 10.5 %collective-permute-start.12 = (bf16[3,576,256]{2,1,0:T(8,128)(2,1)S(1)}, bf16[3,576,256]{2,1,0:T(8,128)(2,1)S(1)}, u32[]{:S(2)}, u32[]{:S(2)}) collective-permute-start(bf16[3,576,256]{2,1,0:T(8,128)(2,1)S(1)} %get-tuple-element.71.refs_0_), channel_id=1, source_target_pairs={{4,0},{0,4},{12,8},{8,12},{20,16},{16,20},{28,24},{24,28},{36,32},... | collective-permute-start | bytes 2654216 | tf_op jit(solution)/shard_map/ppermute | solution.py:27
  30.5 6.3 %collective-permute-start.16 = (bf16[384,256]{1,0:T(8,128)(2,1)S(1)}, bf16[384,256]{1,0:T(8,128)(2,1)S(1)}, u32[]{:S(2)}, u32[]{:S(2)}) collective-permute-start(bf16[384,256]{1,0:T(8,128)(2,1)S(1)} %collective-permute-done.8), channel_id=1, source_target_pairs={{8,0},{36,4},{16,8},{44,12},{24,16},{52,20},{0,24},{60,28},{40,32}... | collective-permute-start | bytes 589832 | tf_op jit(solution)/shard_map/ppermute | solution.py:27
  36.8 11.3 %collective-permute-start.17 = (bf16[4,384,256]{2,1,0:T(8,128)(2,1)S(1)}, bf16[4,384,256]{2,1,0:T(8,128)(2,1)S(1)}, u32[]{:S(2)}, u32[]{:S(2)}) collective-permute-start(bf16[4,384,256]{2,1,0:T(8,128)(2,1)S(1)} %pad_maximum_fusion.refs_0_), channel_id=1, source_target_pairs={{32,0},{12,4},{40,8},{20,12},{48,16},{28,20},{56,24},{4,28},{64,32... | collective-permute-start | bytes 2359304 | tf_op jit(solution)/shard_map/ppermute | solution.py:27
  37.7 12.3 %collective-permute-start.18 = (bf16[4,384,256]{2,1,0:T(8,128)(2,1)S(1)}, bf16[4,384,256]{2,1,0:T(8,128)(2,1)S(1)}, u32[]{:S(2)}, u32[]{:S(2)}) collective-permute-start(bf16[4,384,256]{2,1,0:T(8,128)(2,1)S(1)} %pad_maximum_fusion.refs_0_), channel_id=1, source_target_pairs={{96,0},{28,4},{104,8},{4,12},{112,16},{12,20},{120,24},{20,28},{0,... | collective-permute-start | bytes 2359304 | tf_op jit(solution)/shard_map/ppermute | solution.py:27
  52.7 21.9 %collective-permute-start.19 = (bf16[4,384,256]{2,1,0:T(8,128)(2,1)S(1)}, bf16[4,384,256]{2,1,0:T(8,128)(2,1)}, u32[]{:S(2)}, u32[]{:S(2)}) collective-permute-start(bf16[4,384,256]{2,1,0:T(8,128)(2,1)S(1)} %pad_maximum_fusion.refs_0_), channel_id=1, source_target_pairs={{4,0},{0,4},{12,8},{8,12},{20,16},{16,20},{28,24},{24,28},{36,32},... | collective-permute-start | bytes 2359304 | tf_op jit(solution)/shard_map/ppermute | solution.py:27
  57.3 17.4 %collective-permute-start.20 = (bf16[4,384,256]{2,1,0:T(8,128)(2,1)S(1)}, bf16[4,384,256]{2,1,0:T(8,128)(2,1)}, u32[]{:S(2)}, u32[]{:S(2)}) collective-permute-start(bf16[4,384,256]{2,1,0:T(8,128)(2,1)S(1)} %collective-permute-done.17.up_ref.refs_1_), channel_id=1, source_target_pairs={{4,0},{0,4},{12,8},{8,12},{20,16},{16,20},{28,24},{24,28},{36,32},... | collective-permute-start | bytes 2359304 | tf_op jit(solution)/shard_map/ppermute | solution.py:27
  57.3 17.4 %collective-permute-start.21 = (bf16[4,384,256]{2,1,0:T(8,128)(2,1)S(1)}, bf16[4,384,256]{2,1,0:T(8,128)(2,1)}, u32[]{:S(2)}, u32[]{:S(2)}) collective-permute-start(bf16[4,384,256]{2,1,0:T(8,128)(2,1)S(1)} %collective-permute-done.18.down_ref.refs_2_), channel_id=1, source_target_pairs={{4,0},{0,4},{12,8},{8,12},{20,16},{16,20},{28,24},{24,28},{36,32},... | collective-permute-start | bytes 2359304 | tf_op jit(solution)/shard_map/ppermute | solution.py:27
  57.8 16.7 %all-to-all-start = ((bf16[8,128,384]{2,1,0:T(8,128)(2,1)}), bf16[8,128,384]{2,1,0:T(8,128)(2,1)S(1)}, u32[]{:S(2)}, u32[]{:S(2)}) async-start(bf16[8,128,384]{2,1,0:T(8,128)(2,1)} %add_convert_fusion), calls=%async_computation | async-start | bytes 1572864 | tf_op jit(solution)/shard_map/all_to_all | solution.py:410
  61.4 19.3 %collective-permute-start.25 = (bf16[2,384,256]{2,1,0:T(8,128)(2,1)}, bf16[2,384,256]{2,1,0:T(8,128)(2,1)S(1)}, u32[]{:S(2)}, u32[]{:S(2)}) collective-permute-start(bf16[2,384,256]{2,1,0:T(8,128)(2,1)} %copy-done.4), channel_id=1, source_target_pairs={{32,0},{12,4},{40,8},{20,12},{48,16},{28,20},{56,24},{4,28},{64,32... | collective-permute-start | bytes 1179656 | tf_op jit(solution)/shard_map/ppermute | solution.py:27
  64.0 16.6 %collective-permute-start.26 = (bf16[2,384,256]{2,1,0:T(8,128)(2,1)}, bf16[2,384,256]{2,1,0:T(8,128)(2,1)}, u32[]{:S(2)}, u32[]{:S(2)}) collective-permute-start(bf16[2,384,256]{2,1,0:T(8,128)(2,1)} %copy-done.3), channel_id=1, source_target_pairs={{96,0},{28,4},{104,8},{4,12},{112,16},{12,20},{120,24},{20,28},{0,... | collective-permute-start | bytes 1179656 | tf_op jit(solution)/shard_map/ppermute | solution.py:27
  84.0 10.9 %collective-permute-start.29 = (bf16[4,384,128]{2,1,0:T(8,128)(2,1)S(1)}, bf16[4,384,128]{2,1,0:T(8,128)(2,1)S(1)}, u32[]{:S(2)}, u32[]{:S(2)}) collective-permute-start(bf16[4,384,128]{2,1,0:T(8,128)(2,1)S(1)} %pad_maximum_fusion.1.refs_0_), channel_id=1, source_target_pairs={{32,0},{12,4},{40,8},{20,12},{48,16},{28,20},{56,24},{4,28},{64,32... | collective-permute-start | bytes 1179656 | tf_op jit(solution)/shard_map/ppermute | solution.py:27
  86.0 8.9 %collective-permute-start.30 = (bf16[4,384,128]{2,1,0:T(8,128)(2,1)S(1)}, bf16[4,384,128]{2,1,0:T(8,128)(2,1)S(1)}, u32[]{:S(2)}, u32[]{:S(2)}) collective-permute-start(bf16[4,384,128]{2,1,0:T(8,128)(2,1)S(1)} %pad_maximum_fusion.1.refs_0_), channel_id=1, source_target_pairs={{4,0},{0,4},{12,8},{8,12},{20,16},{16,20},{28,24},{24,28},{36,32},... | collective-permute-start | bytes 1179656 | tf_op jit(solution)/shard_map/ppermute | solution.py:27
  86.0 8.9 %collective-permute-start.31 = (bf16[4,384,128]{2,1,0:T(8,128)(2,1)S(1)}, bf16[4,384,128]{2,1,0:T(8,128)(2,1)S(1)}, u32[]{:S(2)}, u32[]{:S(2)}) collective-permute-start(bf16[4,384,128]{2,1,0:T(8,128)(2,1)S(1)} %pad_maximum_fusion.1.refs_0_), channel_id=1, source_target_pairs={{96,0},{28,4},{104,8},{4,12},{112,16},{12,20},{120,24},{20,28},{0,... | collective-permute-start | bytes 1179656 | tf_op jit(solution)/shard_map/ppermute | solution.py:27
  86.1 13.6 %collective-permute-start.32 = (bf16[4,384,128]{2,1,0:T(8,128)(2,1)S(1)}, bf16[4,384,128]{2,1,0:T(8,128)(2,1)S(1)}, u32[]{:S(2)}, u32[]{:S(2)}) collective-permute-start(bf16[4,384,128]{2,1,0:T(8,128)(2,1)S(1)} %pad_maximum_fusion.1.refs_0_), channel_id=1, source_target_pairs={{64,0},{20,4},{72,8},{28,12},{80,16},{4,20},{88,24},{12,28},{96,32... | collective-permute-start | bytes 1179656 | tf_op jit(solution)/shard_map/ppermute | solution.py:27
  94.9 6.1 %collective-permute-start.34 = (bf16[4,384,128]{2,1,0:T(8,128)(2,1)S(1)}, bf16[4,384,128]{2,1,0:T(8,128)(2,1)S(1)}, u32[]{:S(2)}, u32[]{:S(2)}) collective-permute-start(bf16[4,384,128]{2,1,0:T(8,128)(2,1)S(1)} %collective-permute-done.31.refs_2_), channel_id=1, source_target_pairs={{4,0},{0,4},{12,8},{8,12},{20,16},{16,20},{28,24},{24,28},{36,32},... | collective-permute-start | bytes 1179656 | tf_op jit(solution)/shard_map/ppermute | solution.py:27
  (18 other events, 97.5 us)
